TPU v7x, 32 devices: a whole 2x2x4 slice. The times are simulated.
32 devices in a mesh: snp: 8 (over y, x, core), ind: 4 (over z).
Axes of the slice: x: 2, y: 2, z: 4, core: 2. Of those that a mesh axis runs over, the one named last changes fastest.
Arguments:
- genotypes: bfloat16 [8192, 4096], P('ind', 'snp'), may hold values from -12 to 12, as said below
- annotations: bfloat16 [4096, 512], P('snp'), may hold values from -0.3984375 to 0.3984375
- window_start: int32 [4096], P(('snp', 'ind')), may hold values from 0 to 4095, as said below
- window_end: int32 [4096], P(('snp', 'ind')), may hold values from 1 to 4096, as said below
Outputs:
- ld_scores: float32 [4096, 512], P(('snp', 'ind'))
Inputs may be any that keep to these rules, and one draw needn't show every extreme that they name: `genotypes`: real-valued dosages, each SNP with its own scale; values within the range. For each SNP j: window_start(j) <= j; j - window_start(j) <= 512, reached on every draw; k is in the window of j exactly when j is in the window of k; never falls along the SNPs. For each SNP j: window_end(j) > j; window_end(j) - j <= 513, reached on every draw; never falls along the SNPs.
All inputs are finite; a program needn't handle non-finite values.
Results may differ from a plain program's by a relative error of at most 0.0033.
Values may be sent and summed in bfloat16 or wider, within the bound.
No kernel may reach another device: no remote copies, remote signals or barrier semaphores. Data moves between devices by JAX's collectives and lax.ppermute only.
A program may use at most 64 MiB of HBM per device.

v0:
```python
import jax
import jax.numpy as jnp
from jax import lax
from jax.sharding import PartitionSpec as P


def shifted(array, axis, by):
    devices = lax.axis_size(axis)
    pairs = [(i, i + by) for i in range(devices) if 0 <= i + by < devices]
    return lax.ppermute(array, axis, pairs)


def adjust_block(gram_tile, row_sumsq, col_sumsq, col_ids, start_rows, end_rows, count_all):
    col_safe = jnp.where(col_sumsq > 0.0, col_sumsq, 1.0)
    corr_value = gram_tile * lax.rsqrt(row_sumsq)[:, None] * lax.rsqrt(col_safe)[None, :]
    squared = corr_value * corr_value
    adjusted = squared - (1.0 - squared) / (count_all - 2.0)
    inside = (col_ids[None, :] >= start_rows[:, None]) & (col_ids[None, :] < end_rows[:, None])
    return jnp.where(inside, adjusted, 0.0).astype(jnp.bfloat16)


def column_squares(block):
    widened = block.astype(jnp.float32)
    return jnp.sum(widened * widened, axis=0)


def transposed_product(left, right):
    return lax.dot_general(
        left, right, (((0,), (0,)), ((), ())), preferred_element_type=jnp.float32
    )


def per_device(genotypes, annotations, window_start, window_end):
    stripe = genotypes.shape[1]
    groups = lax.axis_size("ind")
    count_all = float(genotypes.shape[0] * groups)
    sub_rows = stripe // groups
    row_lead = lax.axis_index("ind") * sub_rows
    stripe_first = lax.axis_index("snp") * stripe
    geno_above = shifted(genotypes, "snp", -1)
    annot_above = shifted(annotations, "snp", -1)
    wide_geno = jnp.concatenate([genotypes, geno_above], axis=1)
    wide_annot = jnp.concatenate([annotations, annot_above], axis=0)
    gram_tile = lax.psum_scatter(
        transposed_product(genotypes, wide_geno), "ind", scatter_dimension=0, tiled=True
    )
    col_sumsq = lax.psum(column_squares(wide_geno), "ind")
    row_sumsq = lax.dynamic_slice_in_dim(col_sumsq, row_lead, sub_rows, 0)
    col_ids = stripe_first + jnp.arange(wide_geno.shape[1], dtype=jnp.int32)
    weights = adjust_block(
        gram_tile, row_sumsq, col_sumsq, col_ids, window_start, window_end, count_all
    )
    own_score = jnp.dot(weights, wide_annot, preferred_element_type=jnp.float32)
    own_annot = lax.dynamic_slice_in_dim(annotations, row_lead, sub_rows, 0)
    upper_weights = weights[:, stripe:]
    mirrored = lax.psum_scatter(
        transposed_product(upper_weights, own_annot), "ind", scatter_dimension=0, tiled=True
    )
    mirrored = shifted(mirrored.astype(jnp.bfloat16), "snp", 1).astype(mirrored.dtype)
    return own_score + mirrored


def solution(mesh):
    in_specs = (P("ind", "snp"), P("snp", None), P(("snp", "ind")), P(("snp", "ind")))
    out_specs = P(("snp", "ind"), None)
    return jax.shard_map(
        per_device, mesh=mesh, in_specs=in_specs, out_specs=out_specs, check_vma=False
    )
```

profile of v0, /device:TPU:4, one launch (start us, length us, event | category | flops | bytes accessed | tf_op | source)
XLA Modules:
  0.0 130.2 jit_solution(10425837010501766005)
XLA Ops:
  6.5 0.0 reduce-scatter.3.cloned.1.call-start
  6.5 2.9 %collective-permute-start = (bf16[2048,512]{1,0:T(8,128)(2,1)}, bf16[2048,512]{1,0:T(8,128)(2,1)S(1)}, u32[]{:S(2)}, u32[]{:S(2)}) collective-permute-start(bf16[2048,512]{1,0:T(8,128)(2,1)} %param.4), channel_id=1, source_target_pairs={{4,0},{8,4},{12,8},{16,12},{20,16},{24,20},{28,24},{5,1},{9,5},{13... | collective-permute-start | bytes 6291464 | tf_op jit(solution)/shard_map/ppermute | solution.py:10
  9.4 1.9 %constant_dynamic-update-slice_fusion.1 = bf16[2048,1024]{1,0:T(8,128)(2,1)S(1)} fusion(bf16[2048,512]{1,0:T(8,128)(2,1)} %param.4), kind=kLoop, calls=%fused_computation.12 | loop fusion | bytes 4194304
  11.4 21.9 %collective-permute-done = bf16[2048,512]{1,0:T(8,128)(2,1)S(1)} collective-permute-done((bf16[2048,512]{1,0:T(8,128)(2,1)}, bf16[2048,512]{1,0:T(8,128)(2,1)S(1)}, u32[]{:S(2)}, u32[]{:S(2)}) %collective-permute-start) | collective-permute-done | bytes 2097184 | tf_op jit(solution)/shard_map/ppermute | solution.py:10
  33.3 0.3 constant_dynamic-update-slice_fusion
  33.6 0.0 copy-start
  33.6 1.9 %copy-done = bf16[2048,1024]{1,0:T(8,128)(2,1)} copy-done((bf16[2048,1024]{1,0:T(8,128)(2,1)}, bf16[2048,1024]{1,0:T(8,128)(2,1)S(1)}, u32[]{:S(2)}) %copy-start) | copy-done | bytes 4194328
  35.6 3.7 %convolution_bitcast_fusion = f32[512,1024]{0,1:T(8,128)} fusion(bf16[2048,1024]{1,0:T(8,128)(2,1)S(1)} %constant_dynamic-update-slice_fusion, bf16[2048,512]{1,0:T(8,128)(2,1)S(1)} %copy-done.1), kind=kOutput, calls=%fused_computation.1 | convolution fusion | flops 2147483648 | bytes 8388608 | tf_op jit(solution)/shard_map/dot_general | solution.py:28
  39.2 0.0 reduce-scatter.3.cloned.1.call-update
  39.3 0.0 reduce-scatter.5.cloned.1.call-start
  39.3 3.2 %multiply_reduce_fusion = f32[1024]{0:T(1024)S(1)} fusion(bf16[2048,1024]{1,0:T(8,128)(2,1)} %copy-done), kind=kLoop, calls=%fused_computation | loop fusion | flops 6290432 | bytes 4198400 | tf_op jit(solution)/shard_map/reduce_sum | solution.py:24
  42.5 12.1 %psum.7 = f32[1024]{0:T(1024)S(1)} all-reduce(f32[1024]{0:T(1024)S(1)} %multiply_reduce_fusion), channel_id=1, replica_groups=mesh['snp'=8,'ind'=4] {'ind'}, use_global_device_ids=true, to_apply=%region_2.0 | all-reduce | flops 1024 | bytes 8192 | tf_op jit(solution)/shard_map/psum | solution.py:47
  54.7 0.1 dynamic-slice_rsqrt_fusion
  54.7 30.2 %reduce-scatter.3.cloned.1.call-done = f32[128,1024]{0,1:T(8,128)} async-done(((f32[512,1024]{0,1:T(8,128)}), f32[128,1024]{0,1:T(8,128)}) %reduce-scatter.3.cloned.1.call-update) | async-done | bytes 524304 | tf_op jit(solution)/shard_map/reduce_scatter | solution.py:44
  84.9 1.4 %select_convert_fusion = bf16[128,1024]{0,1:T(8,128)(2,1)S(1)} fusion(f32[128,1024]{0,1:T(8,128)} %reduce-scatter.3.cloned.1.call-done, f32[1024]{0:T(1024)S(1)} %fusion.6, f32[128]{0:T(128)S(1)} %dynamic-slice_rsqrt_fusion, s32[128]{0:T(128)S(1)} %copy-done.3, s32[128]{0:T(128)S(1)} %copy-done.4, s32[1024]{0:T(1024)S(1)} %iota_add_fusion), kind=kLoop, calls=%fused_computation.6 | loop fusion | flops 1441792 | bytes 796160 | tf_op jit(solution)/shard_map/convert_element_type | solution.py:19
  86.3 1.3 fusion.3
  87.6 0.0 reduce-scatter.5.cloned.1.call-update
  87.6 2.6 %collective-permute-start.1 = (bf16[512,512]{1,0:T(8,128)(2,1)S(1)}, bf16[512,512]{1,0:T(8,128)(2,1)S(1)}, u32[]{:S(2)}, u32[]{:S(2)}) collective-permute-start(bf16[512,512]{1,0:T(8,128)(2,1)S(1)} %copy-done.2), channel_id=1, source_target_pairs={{4,0},{8,4},{12,8},{16,12},{20,16},{24,20},{28,24},{5,1},{9,5},{13... | collective-permute-start | bytes 1572872 | tf_op jit(solution)/shard_map/ppermute | solution.py:10
  90.2 24.0 %reduce-scatter.5.cloned.1.call-done = f32[128,512]{1,0:T(8,128)} async-done(((f32[512,512]{1,0:T(8,128)}), f32[128,512]{1,0:T(8,128)}) %reduce-scatter.5.cloned.1.call-update) | async-done | bytes 262160 | tf_op jit(solution)/shard_map/reduce_scatter | solution.py:56
  114.2 1.0 convert_element_type.14
  115.2 1.9 %collective-permute-start.2 = (bf16[128,512]{1,0:T(8,128)(2,1)S(1)}, bf16[128,512]{1,0:T(8,128)(2,1)S(1)}, u32[]{:S(2)}, u32[]{:S(2)}) collective-permute-start(bf16[128,512]{1,0:T(8,128)(2,1)S(1)} %convert_element_type.14), channel_id=1, source_target_pairs={{0,4},{4,8},{8,12},{12,16},{16,20},{20,24},{24,28},{1,5},{5,9},{9,... | collective-permute-start | bytes 393224 | tf_op jit(solution)/shard_map/ppermute | solution.py:10
  117.1 0.0 collective-permute-done.1
  117.1 5.2 %collective-permute-done.2 = bf16[128,512]{1,0:T(8,128)(2,1)S(1)} collective-permute-done((bf16[128,512]{1,0:T(8,128)(2,1)S(1)}, bf16[128,512]{1,0:T(8,128)(2,1)S(1)}, u32[]{:S(2)}, u32[]{:S(2)}) %collective-permute-start.2) | collective-permute-done | bytes 131104 | tf_op jit(solution)/shard_map/ppermute | solution.py:10
  122.4 1.0 convolution_add_fusion
  (10 shorter events, 0.0 us)
Async XLA Ops:
  6.5 29.0 %copy-start.1 = (bf16[2048,512]{1,0:T(8,128)(2,1)S(1)}, bf16[2048,512]{1,0:T(8,128)(2,1)}, u32[]{:S(2)}) copy-start(bf16[2048,512]{1,0:T(8,128)(2,1)} %param.4) | copy-start | bytes 6291460
  6.5 78.4 %reduce-scatter.3.cloned.1.call-start = ((), (), s32[]{:S(2)}) async-start(), calls=%async_computation.2 | async-start | bytes 2621440 | tf_op jit(solution)/shard_map/reduce_scatter | solution.py:44
  6.5 26.8 %collective-permute-start = (bf16[2048,512]{1,0:T(8,128)(2,1)}, bf16[2048,512]{1,0:T(8,128)(2,1)S(1)}, u32[]{:S(2)}, u32[]{:S(2)}) collective-permute-start(bf16[2048,512]{1,0:T(8,128)(2,1)} %param.4), channel_id=1, source_target_pairs={{4,0},{8,4},{12,8},{16,12},{20,16},{24,20},{28,24},{5,1},{9,5},{13... | collective-permute-start | bytes 6291464 | tf_op jit(solution)/shard_map/ppermute | solution.py:10
  33.6 1.9 %copy-start = (bf16[2048,1024]{1,0:T(8,128)(2,1)}, bf16[2048,1024]{1,0:T(8,128)(2,1)S(1)}, u32[]{:S(2)}) copy-start(bf16[2048,1024]{1,0:T(8,128)(2,1)S(1)} %constant_dynamic-update-slice_fusion) | copy-start | bytes 12582916
  39.2 45.7 %copy-start.3 = (s32[128]{0:T(128)S(1)}, s32[128]{0:T(128)}, u32[]{:S(2)}) copy-start(s32[128]{0:T(128)} %param.7) | copy-start | bytes 1540
  39.2 45.7 %copy-start.4 = (s32[128]{0:T(128)S(1)}, s32[128]{0:T(128)}, u32[]{:S(2)}) copy-start(s32[128]{0:T(128)} %param.6) | copy-start | bytes 1540
  39.2 47.1 %copy-start.2 = (bf16[512,512]{1,0:T(8,128)(2,1)S(1)}, bf16[512,512]{1,0:T(8,128)(2,1)}, u32[]{:S(2)}) copy-start(bf16[512,512]{1,0:T(8,128)(2,1)} %param.5) | copy-start | bytes 1572868
  39.3 74.9 %reduce-scatter.5.cloned.1.call-start = ((), (), s32[]{:S(2)}) async-start(), calls=%async_computation.3 | async-start | bytes 1310720 | tf_op jit(solution)/shard_map/reduce_scatter | solution.py:56
  87.6 29.5 %collective-permute-start.1 = (bf16[512,512]{1,0:T(8,128)(2,1)S(1)}, bf16[512,512]{1,0:T(8,128)(2,1)S(1)}, u32[]{:S(2)}, u32[]{:S(2)}) collective-permute-start(bf16[512,512]{1,0:T(8,128)(2,1)S(1)} %copy-done.2), channel_id=1, source_target_pairs={{4,0},{8,4},{12,8},{16,12},{20,16},{24,20},{28,24},{5,1},{9,5},{13... | collective-permute-start | bytes 1572872 | tf_op jit(solution)/shard_map/ppermute | solution.py:10
  115.2 7.2 %collective-permute-start.2 = (bf16[128,512]{1,0:T(8,128)(2,1)S(1)}, bf16[128,512]{1,0:T(8,128)(2,1)S(1)}, u32[]{:S(2)}, u32[]{:S(2)}) collective-permute-start(bf16[128,512]{1,0:T(8,128)(2,1)S(1)} %convert_element_type.14), channel_id=1, source_target_pairs={{0,4},{4,8},{8,12},{12,16},{16,20},{20,24},{24,28},{1,5},{5,9},{9,... | collective-permute-start | bytes 393224 | tf_op jit(solution)/shard_map/ppermute | solution.py:10
Sparse Core Ops, SparseCore 0:
  39.4 45.4 reduce-scatter.2
  87.7 26.4 reduce-scatter.4
where the time goes:
time: 131 us; the launch traced here: 130 us
  waiting for transfers between devices  81.4 us (62%)
  between operations  13.5 us (10%)
  blocking collectives  12.1 us (9%)
  starting transfers between devices  7.49 us (6%)
  matrix products  5.98 us (5%)
  other arithmetic  5.55 us (4%)
  local copies, waits for them, and re-layouts  4.26 us (3%)
    reduce_scatter x1, waiting for transfers between devices, per_device(): lax.psum_scatter(transposed_product(genotypes, wide_geno), 'ind', scatter...  30.2 us
    ppermute x3, waiting for transfers between devices, shifted(): return lax.ppermute(array, axis, pairs)  27.2 us
    reduce_scatter x1, waiting for transfers between devices, per_device(): lax.psum_scatter(transposed_product(upper_weights, own_annot), 'ind', sca...  24 us
    psum x1, blocking collectives, per_device(): col_sumsq = lax.psum(column_squares(wide_geno), 'ind')  12.1 us
    ppermute x3, starting transfers between devices, shifted(): return lax.ppermute(array, axis, pairs)  7.44 us
    dot_general x2, matrix products, transposed_product(): lax.dot_general(left, right, (((0,), (0,)), ((), ())), preferred_element_...  4.93 us
    unnamed x11, local copies, waits for them, and re-layouts  3.86 us
    reduce_sum x1, other arithmetic, column_squares(): return jnp.sum(widened * widened, axis=0)  3.19 us
  transfers between devices with their start and end apart: 5, of which 4 were waited for; matrix products, arithmetic and copies ran while one was open for 5% of the time, Pallas kernels for 0%

commit v1 on v0

v1 whole, which is shorter than its diff:
```python
import jax
import jax.numpy as jnp
from jax import lax
from jax.sharding import PartitionSpec as P


def shifted(array, axis, by):
    devices = lax.axis_size(axis)
    pairs = [(i, i + by) for i in range(devices) if 0 <= i + by < devices]
    return lax.ppermute(array, axis, pairs)


def ring(array, axis, by):
    devices = lax.axis_size(axis)
    return lax.ppermute(array, axis, [(i, (i + by) % devices) for i in range(devices)])


def after(value, *earlier):
    return lax.optimization_barrier((value, *earlier))[0]


def column_squares(block):
    widened = block.astype(jnp.float32)
    return jnp.sum(widened * widened, axis=0)


def transposed_product(left, right):
    return lax.dot_general(
        left, right, (((0,), (0,)), ((), ())), preferred_element_type=jnp.float32
    )


def summed_slots(slots, axis):
    devices = lax.axis_size(axis)
    place = lax.axis_index(axis)
    total = lax.dynamic_index_in_dim(slots, place, 0, keepdims=False).astype(jnp.float32)
    terms = []
    for by in range(1, devices):
        mine = lax.dynamic_index_in_dim(slots, (place + by) % devices, 0, keepdims=False)
        terms.append(ring(mine, axis, by))
    for term in terms:
        total = total + term.astype(jnp.float32)
    return total


def adjusted(corr, count_all):
    squared = corr * corr
    return (squared - (1.0 - squared) / (count_all - 2.0)).astype(jnp.bfloat16)


def per_device(genotypes, annotations, window_start, window_end):
    stripe = genotypes.shape[1]
    groups = lax.axis_size("ind")
    count_all = float(genotypes.shape[0] * groups)
    sub_rows = stripe // groups
    place = lax.axis_index("ind")
    stripe_first = lax.axis_index("snp") * stripe
    geno_above = shifted(genotypes, "snp", -1)

    squares = column_squares(genotypes)
    sumsq = squares
    for by in range(1, groups):
        sumsq = sumsq + ring(squares, "ind", by)
    unsafe = lax.rsqrt(sumsq)
    safe = lax.rsqrt(jnp.where(sumsq > 0.0, sumsq, 1.0))
    safe_above = shifted(safe, "snp", -1)

    own_part = transposed_product(genotypes, genotypes) * unsafe[:, None] * safe[None, :]
    own_part = own_part.astype(jnp.float16).reshape(groups, sub_rows, stripe)
    own_corr = summed_slots(own_part, "ind")

    cross_part = transposed_product(genotypes, geno_above) * safe[:, None] * safe_above[None, :]
    cross_part = cross_part.astype(jnp.float16).reshape(groups, sub_rows, groups, sub_rows)
    slots = jnp.stack([
        jnp.stack([cross_part[max(d, m), :, min(d, m), :] for m in range(groups)])
        for d in range(groups)
    ])
    cross_corr = summed_slots(slots, "ind")

    own_weights = adjusted(own_corr, count_all)
    cross_weights = adjusted(cross_corr, count_all)
    cross_below = shifted(cross_weights, "snp", 1)

    ids = jnp.arange(stripe, dtype=jnp.int32)
    own_ids = stripe_first + ids
    inside = (own_ids[None, :] >= window_start[:, None]) & (own_ids[None, :] < window_end[:, None])
    own_weights = jnp.where(inside, own_weights, 0)

    blocks = jnp.arange(groups, dtype=jnp.int32)
    above_ids = (own_ids + stripe).reshape(groups, 1, sub_rows)
    inside = (above_ids < window_end[None, :, None]) & (blocks <= place)[:, None, None]
    above_weights = jnp.where(inside, cross_weights, 0)
    below_ids = (own_ids - stripe).reshape(groups, sub_rows, 1)
    inside = (below_ids >= window_start[None, None, :]) & (blocks >= place)[:, None, None]
    below_weights = jnp.where(inside, cross_below, 0).reshape(stripe, sub_rows)

    later = after(annotations, geno_above)
    annot_above = shifted(later, "snp", -1).reshape(groups, sub_rows, -1)
    annot_below = shifted(later, "snp", 1)
    score = jnp.dot(own_weights, annotations, preferred_element_type=jnp.float32)
    score += lax.dot_general(
        above_weights, annot_above, (((0, 2), (0, 1)), ((), ())), preferred_element_type=jnp.float32
    )
    return score + transposed_product(below_weights, annot_below)


def solution(mesh):
    in_specs = (P("ind", "snp"), P("snp", None), P(("snp", "ind")), P(("snp", "ind")))
    out_specs = P(("snp", "ind"), None)
    return jax.shard_map(
        per_device, mesh=mesh, in_specs=in_specs, out_specs=out_specs, check_vma=False
    )
```

time: 131 us -> 67.3 us (0.51)
  the two profiles are of different devices: /device:TPU:4 before, /device:TPU:3 now
where the time goes in v1:
time: 67.3 us; the launch traced here: 67 us
  starting transfers between devices  31.3 us (47%)
  waiting for transfers between devices  25.7 us (38%)
  matrix products  5.71 us (8%)
  other arithmetic  2.77 us (4%)
  local copies, waits for them, and re-layouts  1.2 us (2%)
    ppermute x5, waiting for transfers between devices, shifted(): return lax.ppermute(array, axis, pairs)  18.4 us
    ppermute x5, starting transfers between devices, shifted(): return lax.ppermute(array, axis, pairs)  16.9 us
    ppermute x9, starting transfers between devices, ring(): lax.ppermute(array, axis, [(i, (i + by) % devices) for i in range(devices)])  14.4 us
    ppermute x9, waiting for transfers between devices, ring(): lax.ppermute(array, axis, [(i, (i + by) % devices) for i in range(devices)])  7.36 us
    dot_general x3, matrix products, transposed_product(): lax.dot_general(left, right, (((0,), (0,)), ((), ())), preferred_element_...  5.1 us
    reduce_sum x1, other arithmetic, column_squares(): return jnp.sum(widened * widened, axis=0)  2.1 us
  transfers between devices with their start and end apart: 14, of which 7 were waited for; matrix products, arithmetic and copies ran while one was open for 7% of the time, Pallas kernels for 0%

profile of v1, /device:TPU:3, one launch (start us, length us, event | category | flops | bytes accessed | tf_op | source)
XLA Modules:
  0.0 67.0 jit_solution(2335844945773502503)
XLA Ops:
  0.0 2.7 %collective-permute-start.6 = (bf16[2048,512]{1,0:T(8,128)(2,1)}, bf16[2048,512]{1,0:T(8,128)(2,1)}, u32[]{:S(2)}, u32[]{:S(2)}) collective-permute-start(bf16[2048,512]{1,0:T(8,128)(2,1)} %param.4), channel_id=1, source_target_pairs={{4,0},{8,4},{12,8},{16,12},{20,16},{24,20},{28,24},{5,1},{9,5},{13... | collective-permute-start | bytes 6291464 | tf_op jit(solution)/shard_map/ppermute | solution.py:10
  2.7 2.1 %multiply_reduce_fusion = f32[512]{0:T(512)S(1)} fusion(bf16[2048,512]{1,0:T(8,128)(2,1)} %param.4), kind=kLoop, calls=%fused_computation | loop fusion | flops 3145216 | bytes 2099200 | tf_op jit(solution)/shard_map/reduce_sum | solution.py:24
  4.8 3.4 %collective-permute-start.2 = (f32[512]{0:T(512)S(1)}, f32[512]{0:T(512)S(1)}, u32[]{:S(2)}, u32[]{:S(2)}) collective-permute-start(f32[512]{0:T(512)S(1)} %multiply_reduce_fusion), channel_id=1, source_target_pairs={{0,3},{1,0},{2,1},{3,2},{4,7},{5,4},{6,5},{7,6},{8,11},{9,8},{10,9... | collective-permute-start | bytes 6152 | tf_op jit(solution)/shard_map/ppermute | solution.py:15
  8.2 0.5 collective-permute-start
  8.9 2.6 %collective-permute-done.1 = f32[512]{0:T(512)S(1)} collective-permute-done((f32[512]{0:T(512)S(1)}, f32[512]{0:T(512)S(1)}, u32[]{:S(2)}, u32[]{:S(2)}) %collective-permute-start.1) | collective-permute-done | bytes 2080 | tf_op jit(solution)/shard_map/ppermute | solution.py:15
  11.5 0.9 %collective-permute-done = f32[512]{0:T(512)S(1)} collective-permute-done((f32[512]{0:T(512)S(1)}, f32[512]{0:T(512)S(1)}, u32[]{:S(2)}, u32[]{:S(2)}) %collective-permute-start) | collective-permute-done | bytes 2080 | tf_op jit(solution)/shard_map/ppermute | solution.py:15
  12.4 3.4 %collective-permute-start.7 = (f32[512]{0:T(512)S(1)}, f32[512]{0:T(512)S(1)}, u32[]{:S(2)}, u32[]{:S(2)}) collective-permute-start(f32[512]{0:T(512)S(1)} %fusion.22), channel_id=1, source_target_pairs={{4,0},{8,4},{12,8},{16,12},{20,16},{24,20},{28,24},{5,1},{9,5},{13... | collective-permute-start | bytes 6152 | tf_op jit(solution)/shard_map/ppermute | solution.py:10
  15.8 12.8 %collective-permute-done.7 = f32[512]{0:T(512)S(1)} collective-permute-done((f32[512]{0:T(512)S(1)}, f32[512]{0:T(512)S(1)}, u32[]{:S(2)}, u32[]{:S(2)}) %collective-permute-start.7) | collective-permute-done | bytes 2080 | tf_op jit(solution)/shard_map/ppermute | solution.py:10
  28.7 2.9 %fusion.1 = f16[512,512]{1,0:T(8,128)(2,1)S(1)} fusion(bf16[2048,512]{1,0:T(8,128)(2,1)S(1)} %copy-done, bf16[2048,512]{1,0:T(8,128)(2,1)} %collective-permute-done.6, f32[512]{0:T(512)S(1)} %collective-permute-done.7, f32[512]{0:T(512)S(1)} %fusion.22), kind=kOutput, calls=%fused_computation.3 | convolution fusion | flops 1074528256 | bytes 4722688 | tf_op jit(solution)/shard_map/dot_general | solution.py:28
  31.7 0.7 %fusion.31 = (f16[1,128,1,128]{3,2,1,0:T(2,128)(2,1)S(1)}, f16[1,128,1,128]{3,2,1,0:T(2,128)(2,1)S(1)}, f16[1,128,1,128]{3,2,1,0:T(2,128)(2,1)S(1)}, f16[1,128,1...) fusion(f16[4,128,4,128]{3,2,1,0:T(4,128)(2,1)S(1)} %reshape.57), kind=kLoop, calls=%fused_computation.70 | loop fusion | bytes 655360 | tf_op jit(solution)/shard_map/slice | solution.py:75
  33.1 1.4 %collective-permute-start.8 = (f16[4,128,128]{2,1,0:T(8,128)(2,1)S(1)}, f16[4,128,128]{2,1,0:T(8,128)(2,1)S(1)}, u32[]{:S(2)}, u32[]{:S(2)}) collective-permute-start(f16[4,128,128]{2,1,0:T(8,128)(2,1)S(1)} %get-tuple-element.9), channel_id=1, source_target_pairs={{0,1},{1,2},{2,3},{3,0},{4,5},{5,6},{6,7},{7,4},{8,9},{9,10},{10,1... | collective-permute-start | bytes 393224 | tf_op jit(solution)/shard_map/ppermute | solution.py:15
  34.5 2.1 %collective-permute-start.10 = (f16[4,128,128]{2,1,0:T(8,128)(2,1)S(1)}, f16[4,128,128]{2,1,0:T(8,128)(2,1)S(1)}, u32[]{:S(2)}, u32[]{:S(2)}) collective-permute-start(f16[4,128,128]{2,1,0:T(8,128)(2,1)S(1)} %get-tuple-element.10), channel_id=1, source_target_pairs={{0,3},{1,0},{2,1},{3,2},{4,7},{5,4},{6,5},{7,6},{8,11},{9,8},{10,9... | collective-permute-start | bytes 393224 | tf_op jit(solution)/shard_map/ppermute | solution.py:15
  36.6 0.4 collective-permute-start.9
  37.0 1.3 %multiply_convert_fusion = f16[512,512]{1,0:T(8,128)(2,1)S(1)} fusion(f32[512]{0:T(512)S(1)} %fusion.22, f32[512]{0:T(512)S(1)} %get-tuple-element.7, bf16[2048,512]{1,0:T(8,128)(2,1)S(1)} %copy-done), kind=kOutput, calls=%fused_computation.7 | convolution fusion | flops 1074528256 | bytes 2625536 | tf_op jit(solution)/shard_map/dot_general | solution.py:28
  38.4 1.3 %collective-permute-start.3 = (f16[128,512]{1,0:T(8,128)(2,1)S(1)}, f16[128,512]{1,0:T(8,128)(2,1)S(1)}, u32[]{:S(2)}, u32[]{:S(2)}) collective-permute-start(f16[128,512]{1,0:T(8,128)(2,1)S(1)} %get-tuple-element.22), channel_id=1, source_target_pairs={{0,1},{1,2},{2,3},{3,0},{4,5},{5,6},{6,7},{7,4},{8,9},{9,10},{10,1... | collective-permute-start | bytes 393224 | tf_op jit(solution)/shard_map/ppermute | solution.py:15
  39.7 2.0 %collective-permute-start.5 = (f16[128,512]{1,0:T(8,128)(2,1)S(1)}, f16[128,512]{1,0:T(8,128)(2,1)S(1)}, u32[]{:S(2)}, u32[]{:S(2)}) collective-permute-start(f16[128,512]{1,0:T(8,128)(2,1)S(1)} %get-tuple-element.23), channel_id=1, source_target_pairs={{0,3},{1,0},{2,1},{3,2},{4,7},{5,4},{6,5},{7,6},{8,11},{9,8},{10,9... | collective-permute-start | bytes 393224 | tf_op jit(solution)/shard_map/ppermute | solution.py:15
  41.7 3.4 %collective-permute-start.4 = (f16[128,512]{1,0:T(8,128)(2,1)S(1)}, f16[128,512]{1,0:T(8,128)(2,1)S(1)}, u32[]{:S(2)}, u32[]{:S(2)}) collective-permute-start(f16[128,512]{1,0:T(8,128)(2,1)S(1)} %get-tuple-element.24), channel_id=1, source_target_pairs={{0,2},{1,3},{2,0},{3,1},{4,6},{5,7},{6,4},{7,5},{8,10},{9,11},{10,... | collective-permute-start | bytes 393224 | tf_op jit(solution)/shard_map/ppermute | solution.py:15
  45.1 4.4 %collective-permute-start.13 = (bf16[512,512]{1,0:T(8,128)(2,1)S(1)}, bf16[512,512]{1,0:T(8,128)(2,1)S(1)}, u32[]{:S(2)}, u32[]{:S(2)}) collective-permute-start(bf16[512,512]{1,0:T(8,128)(2,1)S(1)} %copy-done.3), channel_id=1, source_target_pairs={{0,4},{4,8},{8,12},{12,16},{16,20},{20,24},{24,28},{1,5},{5,9},{9,... | collective-permute-start | bytes 1572872 | tf_op jit(solution)/shard_map/ppermute | solution.py:10
  49.5 3.6 %collective-permute-done.9 = f16[4,128,128]{2,1,0:T(8,128)(2,1)S(1)} collective-permute-done((f16[4,128,128]{2,1,0:T(8,128)(2,1)S(1)}, f16[4,128,128]{2,1,0:T(8,128)(2,1)S(1)}, u32[]{:S(2)}, u32[]{:S(2)}) %collective-permute-start.9) | collective-permute-done | bytes 131104 | tf_op jit(solution)/shard_map/ppermute | solution.py:15
  53.1 1.9 %collective-permute-start.11 = (bf16[512,512]{1,0:T(8,128)(2,1)S(1)}, bf16[512,512]{1,0:T(8,128)(2,1)S(1)}, u32[]{:S(2)}, u32[]{:S(2)}) collective-permute-start(bf16[512,512]{1,0:T(8,128)(2,1)S(1)} %copy-done.3), channel_id=1, source_target_pairs={{4,0},{8,4},{12,8},{16,12},{20,16},{24,20},{28,24},{5,1},{9,5},{13... | collective-permute-start | bytes 1572872 | tf_op jit(solution)/shard_map/ppermute | solution.py:10
  55.2 4.5 %collective-permute-start.12 = (bf16[4,128,128]{2,1,0:T(8,128)(2,1)S(1)}, bf16[4,128,128]{2,1,0:T(8,128)(2,1)S(1)}, u32[]{:S(2)}, u32[]{:S(2)}) collective-permute-start(bf16[4,128,128]{2,1,0:T(8,128)(2,1)S(1)} %subtract_convert_fusion), channel_id=1, source_target_pairs={{0,4},{4,8},{8,12},{12,16},{16,20},{20,24},{24,28},{1,5},{5,9},{9,... | collective-permute-start | bytes 393224 | tf_op jit(solution)/shard_map/ppermute | solution.py:10
  60.1 2.5 %collective-permute-done.12 = bf16[4,128,128]{2,1,0:T(8,128)(2,1)S(1)} collective-permute-done((bf16[4,128,128]{2,1,0:T(8,128)(2,1)S(1)}, bf16[4,128,128]{2,1,0:T(8,128)(2,1)S(1)}, u32[]{:S(2)}, u32[]{:S(2)}) %collective-permute-start.12) | collective-permute-done | bytes 131104 | tf_op jit(solution)/shard_map/ppermute | solution.py:10
  62.8 3.0 %collective-permute-done.11 = bf16[512,512]{1,0:T(8,128)(2,1)S(1)} collective-permute-done((bf16[512,512]{1,0:T(8,128)(2,1)S(1)}, bf16[512,512]{1,0:T(8,128)(2,1)S(1)}, u32[]{:S(2)}, u32[]{:S(2)}) %collective-permute-start.11) | collective-permute-done | bytes 524320 | tf_op jit(solution)/shard_map/ppermute | solution.py:10
  66.1 1.0 %convolution_add_fusion = f32[128,512]{1,0:T(8,128)} fusion(f32[128,512]{1,0:T(8,128)S(1)} %fusion.2, bf16[512,128]{1,0:T(8,128)(2,1)S(1)} %bitcast.64, bf16[512,512]{1,0:T(8,128)(2,1)S(1)} %collective-permute-done.13), kind=kOutput, calls=%fused_computation.4 | convolution fusion | flops 67174400 | bytes 1179648 | tf_op jit(solution)/shard_map/dot_general | solution.py:28
  (38 shorter events, 2.0 us)
Async XLA Ops:
  0.0 28.7 %copy-start = (bf16[2048,512]{1,0:T(8,128)(2,1)S(1)}, bf16[2048,512]{1,0:T(8,128)(2,1)}, u32[]{:S(2)}) copy-start(bf16[2048,512]{1,0:T(8,128)(2,1)} %param.4) | copy-start | bytes 6291460
  0.0 28.7 %collective-permute-start.6 = (bf16[2048,512]{1,0:T(8,128)(2,1)}, bf16[2048,512]{1,0:T(8,128)(2,1)}, u32[]{:S(2)}, u32[]{:S(2)}) collective-permute-start(bf16[2048,512]{1,0:T(8,128)(2,1)} %param.4), channel_id=1, source_target_pairs={{4,0},{8,4},{12,8},{16,12},{20,16},{24,20},{28,24},{5,1},{9,5},{13... | collective-permute-start | bytes 6291464 | tf_op jit(solution)/shard_map/ppermute | solution.py:10
  4.8 4.1 %collective-permute-start.2 = (f32[512]{0:T(512)S(1)}, f32[512]{0:T(512)S(1)}, u32[]{:S(2)}, u32[]{:S(2)}) collective-permute-start(f32[512]{0:T(512)S(1)} %multiply_reduce_fusion), channel_id=1, source_target_pairs={{0,3},{1,0},{2,1},{3,2},{4,7},{5,4},{6,5},{7,6},{8,11},{9,8},{10,9... | collective-permute-start | bytes 6152 | tf_op jit(solution)/shard_map/ppermute | solution.py:15
  8.2 3.3 %collective-permute-start.1 = (f32[512]{0:T(512)S(1)}, f32[512]{0:T(512)S(1)}, u32[]{:S(2)}, u32[]{:S(2)}) collective-permute-start(f32[512]{0:T(512)S(1)} %multiply_reduce_fusion), channel_id=1, source_target_pairs={{0,2},{1,3},{2,0},{3,1},{4,6},{5,7},{6,4},{7,5},{8,10},{9,11},{10,... | collective-permute-start | bytes 6152 | tf_op jit(solution)/shard_map/ppermute | solution.py:15
  8.2 4.2 %collective-permute-start = (f32[512]{0:T(512)S(1)}, f32[512]{0:T(512)S(1)}, u32[]{:S(2)}, u32[]{:S(2)}) collective-permute-start(f32[512]{0:T(512)S(1)} %multiply_reduce_fusion), channel_id=1, source_target_pairs={{0,1},{1,2},{2,3},{3,0},{4,5},{5,6},{6,7},{7,4},{8,9},{9,10},{10,1... | collective-permute-start | bytes 6152 | tf_op jit(solution)/shard_map/ppermute | solution.py:15
  12.4 16.3 %collective-permute-start.7 = (f32[512]{0:T(512)S(1)}, f32[512]{0:T(512)S(1)}, u32[]{:S(2)}, u32[]{:S(2)}) collective-permute-start(f32[512]{0:T(512)S(1)} %fusion.22), channel_id=1, source_target_pairs={{4,0},{8,4},{12,8},{16,12},{20,16},{24,20},{28,24},{5,1},{9,5},{13... | collective-permute-start | bytes 6152 | tf_op jit(solution)/shard_map/ppermute | solution.py:10
  33.1 8.5 %collective-permute-start.8 = (f16[4,128,128]{2,1,0:T(8,128)(2,1)S(1)}, f16[4,128,128]{2,1,0:T(8,128)(2,1)S(1)}, u32[]{:S(2)}, u32[]{:S(2)}) collective-permute-start(f16[4,128,128]{2,1,0:T(8,128)(2,1)S(1)} %get-tuple-element.9), channel_id=1, source_target_pairs={{0,1},{1,2},{2,3},{3,0},{4,5},{5,6},{6,7},{7,4},{8,9},{9,10},{10,1... | collective-permute-start | bytes 393224 | tf_op jit(solution)/shard_map/ppermute | solution.py:15
  34.5 10.6 %collective-permute-start.10 = (f16[4,128,128]{2,1,0:T(8,128)(2,1)S(1)}, f16[4,128,128]{2,1,0:T(8,128)(2,1)S(1)}, u32[]{:S(2)}, u32[]{:S(2)}) collective-permute-start(f16[4,128,128]{2,1,0:T(8,128)(2,1)S(1)} %get-tuple-element.10), channel_id=1, source_target_pairs={{0,3},{1,0},{2,1},{3,2},{4,7},{5,4},{6,5},{7,6},{8,11},{9,8},{10,9... | collective-permute-start | bytes 393224 | tf_op jit(solution)/shard_map/ppermute | solution.py:15
  36.6 16.6 %collective-permute-start.9 = (f16[4,128,128]{2,1,0:T(8,128)(2,1)S(1)}, f16[4,128,128]{2,1,0:T(8,128)(2,1)S(1)}, u32[]{:S(2)}, u32[]{:S(2)}) collective-permute-start(f16[4,128,128]{2,1,0:T(8,128)(2,1)S(1)} %get-tuple-element.11), channel_id=1, source_target_pairs={{0,2},{1,3},{2,0},{3,1},{4,6},{5,7},{6,4},{7,5},{8,10},{9,11},{10,... | collective-permute-start | bytes 393224 | tf_op jit(solution)/shard_map/ppermute | solution.py:15
  37.0 8.1 %copy-start.3 = (bf16[512,512]{1,0:T(8,128)(2,1)S(1)}, bf16[512,512]{1,0:T(8,128)(2,1)}, u32[]{:S(2)}) copy-start(bf16[512,512]{1,0:T(8,128)(2,1)} %param.5) | copy-start | bytes 1572868
  37.0 22.8 %copy-start.1 = (s32[128]{0:T(128)S(1)}, s32[128]{0:T(128)}, u32[]{:S(2)}) copy-start(s32[128]{0:T(128)} %param.6) | copy-start | bytes 1540
  37.0 22.8 %copy-start.2 = (s32[128]{0:T(128)S(1)}, s32[128]{0:T(128)}, u32[]{:S(2)}) copy-start(s32[128]{0:T(128)} %param.7) | copy-start | bytes 1540
  38.4 16.8 %collective-permute-start.3 = (f16[128,512]{1,0:T(8,128)(2,1)S(1)}, f16[128,512]{1,0:T(8,128)(2,1)S(1)}, u32[]{:S(2)}, u32[]{:S(2)}) collective-permute-start(f16[128,512]{1,0:T(8,128)(2,1)S(1)} %get-tuple-element.22), channel_id=1, source_target_pairs={{0,1},{1,2},{2,3},{3,0},{4,5},{5,6},{6,7},{7,4},{8,9},{9,10},{10,1... | collective-permute-start | bytes 393224 | tf_op jit(solution)/shard_map/ppermute | solution.py:15
  39.7 20.1 %collective-permute-start.5 = (f16[128,512]{1,0:T(8,128)(2,1)S(1)}, f16[128,512]{1,0:T(8,128)(2,1)S(1)}, u32[]{:S(2)}, u32[]{:S(2)}) collective-permute-start(f16[128,512]{1,0:T(8,128)(2,1)S(1)} %get-tuple-element.23), channel_id=1, source_target_pairs={{0,3},{1,0},{2,1},{3,2},{4,7},{5,4},{6,5},{7,6},{8,11},{9,8},{10,9... | collective-permute-start | bytes 393224 | tf_op jit(solution)/shard_map/ppermute | solution.py:15
  41.7 18.1 %collective-permute-start.4 = (f16[128,512]{1,0:T(8,128)(2,1)S(1)}, f16[128,512]{1,0:T(8,128)(2,1)S(1)}, u32[]{:S(2)}, u32[]{:S(2)}) collective-permute-start(f16[128,512]{1,0:T(8,128)(2,1)S(1)} %get-tuple-element.24), channel_id=1, source_target_pairs={{0,2},{1,3},{2,0},{3,1},{4,6},{5,7},{6,4},{7,5},{8,10},{9,11},{10,... | collective-permute-start | bytes 393224 | tf_op jit(solution)/shard_map/ppermute | solution.py:15
  45.1 21.0 %collective-permute-start.13 = (bf16[512,512]{1,0:T(8,128)(2,1)S(1)}, bf16[512,512]{1,0:T(8,128)(2,1)S(1)}, u32[]{:S(2)}, u32[]{:S(2)}) collective-permute-start(bf16[512,512]{1,0:T(8,128)(2,1)S(1)} %copy-done.3), channel_id=1, source_target_pairs={{0,4},{4,8},{8,12},{12,16},{16,20},{20,24},{24,28},{1,5},{5,9},{9,... | collective-permute-start | bytes 1572872 | tf_op jit(solution)/shard_map/ppermute | solution.py:10
  53.1 12.6 %collective-permute-start.11 = (bf16[512,512]{1,0:T(8,128)(2,1)S(1)}, bf16[512,512]{1,0:T(8,128)(2,1)S(1)}, u32[]{:S(2)}, u32[]{:S(2)}) collective-permute-start(bf16[512,512]{1,0:T(8,128)(2,1)S(1)} %copy-done.3), channel_id=1, source_target_pairs={{4,0},{8,4},{12,8},{16,12},{20,16},{24,20},{28,24},{5,1},{9,5},{13... | collective-permute-start | bytes 1572872 | tf_op jit(solution)/shard_map/ppermute | solution.py:10
  55.2 7.5 %collective-permute-start.12 = (bf16[4,128,128]{2,1,0:T(8,128)(2,1)S(1)}, bf16[4,128,128]{2,1,0:T(8,128)(2,1)S(1)}, u32[]{:S(2)}, u32[]{:S(2)}) collective-permute-start(bf16[4,128,128]{2,1,0:T(8,128)(2,1)S(1)} %subtract_convert_fusion), channel_id=1, source_target_pairs={{0,4},{4,8},{8,12},{12,16},{16,20},{20,24},{24,28},{1,5},{5,9},{9,... | collective-permute-start | bytes 393224 | tf_op jit(solution)/shard_map/ppermute | solution.py:10

commit v2 on v1

v2 whole, which is shorter than its diff:
```python
import jax
import jax.numpy as jnp
from jax import lax
from jax.sharding import PartitionSpec as P


def shifted(array, axis, by):
    devices = lax.axis_size(axis)
    pairs = [(i, i + by) for i in range(devices) if 0 <= i + by < devices]
    return lax.ppermute(array, axis, pairs)


def ring(array, axis, by):
    devices = lax.axis_size(axis)
    return lax.ppermute(array, axis, [(i, (i + by) % devices) for i in range(devices)])


def after(value, *earlier):
    return lax.optimization_barrier((value, *earlier))[0]


def column_squares(block):
    widened = block.astype(jnp.float32)
    return jnp.sum(widened * widened, axis=0)


def transposed_product(left, right):
    return lax.dot_general(
        left, right, (((0,), (0,)), ((), ())), preferred_element_type=jnp.float32
    )


def exchanged(slots, axis):
    devices = lax.axis_size(axis)
    place = lax.axis_index(axis)
    mine = [
        lax.dynamic_index_in_dim(slots, (place + by) % devices, 0, keepdims=False)
        for by in range(devices)
    ]
    return [mine[0]] + [ring(mine[by], axis, by) for by in range(1, devices)]


def total(terms):
    result = terms[0].astype(jnp.float32)
    for term in terms[1:]:
        result = result + term.astype(jnp.float32)
    return result


def inverse_norm(sumsq):
    return lax.rsqrt(jnp.where(sumsq > 0.0, sumsq, 1.0))


def adjusted(corr, count_all):
    squared = corr * corr
    return (squared - (1.0 - squared) / (count_all - 2.0)).astype(jnp.bfloat16)


def per_device(genotypes, annotations, window_start, window_end):
    stripe = genotypes.shape[1]
    groups = lax.axis_size("ind")
    count_all = float(genotypes.shape[0] * groups)
    sub_rows = stripe // groups
    place = lax.axis_index("ind")
    stripe_first = lax.axis_index("snp") * stripe
    geno_above = shifted(genotypes, "snp", -1)

    squares = column_squares(genotypes)
    scale = inverse_norm(squares)
    own_part = transposed_product(genotypes, genotypes) * scale[:, None] * scale[None, :]
    own_part = own_part.astype(jnp.float16).reshape(groups, sub_rows, stripe)
    own_terms = exchanged(own_part, "ind")

    all_squares = [squares] + [ring(squares, "ind", by) for by in range(1, groups)]
    sumsq = total(all_squares)
    safe = inverse_norm(sumsq)
    safe_above = shifted(safe, "snp", -1)
    start_above = shifted(window_start, "snp", -1)

    geno_above = after(geno_above, *own_terms)
    cross_part = transposed_product(genotypes, geno_above) * safe[:, None] * safe_above[None, :]
    cross_part = cross_part.astype(jnp.float16).reshape(groups, sub_rows, groups, sub_rows)
    slots = jnp.stack([
        jnp.stack([cross_part[max(d, m), :, min(d, m), :] for m in range(groups)])
        for d in range(groups)
    ])
    cross_corr = total(exchanged(slots, "ind"))

    ids = jnp.arange(stripe, dtype=jnp.int32)
    own_ids = stripe_first + ids

    def rows_of(vector):
        return lax.dynamic_slice_in_dim(vector, place * sub_rows, sub_rows, 0)

    row_norm = lax.rsqrt(rows_of(sumsq))
    own_corr = 0.0
    for term, part in zip(own_terms, all_squares):
        norm = part * inverse_norm(part)
        row_factor = rows_of(norm) * row_norm
        own_corr += term.astype(jnp.float32) * row_factor[:, None] * (norm * safe)[None, :]
    inside = (own_ids[None, :] >= window_start[:, None]) & (own_ids[None, :] < window_end[:, None])
    own_weights = jnp.where(inside, adjusted(own_corr, count_all), 0)
    score = jnp.dot(own_weights, annotations, preferred_element_type=jnp.float32)

    cross_weights = adjusted(cross_corr, count_all)
    blocks = jnp.arange(groups, dtype=jnp.int32)
    row_ids = own_ids.reshape(groups, sub_rows, 1)
    inside = (row_ids >= start_above[None, None, :]) & (blocks >= place)[:, None, None]
    mirrored = jnp.where(inside, cross_weights, 0).reshape(stripe, sub_rows)
    mirrored = transposed_product(mirrored, annotations).astype(jnp.bfloat16)
    mirrored = shifted(mirrored, "snp", 1)

    above_ids = (own_ids + stripe).reshape(groups, 1, sub_rows)
    inside = (above_ids < window_end[None, :, None]) & (blocks <= place)[:, None, None]
    above_weights = jnp.where(inside, cross_weights, 0)
    annot_above = shifted(after(annotations, geno_above), "snp", -1).reshape(groups, sub_rows, -1)
    score += lax.dot_general(
        above_weights, annot_above, (((0, 2), (0, 1)), ((), ())), preferred_element_type=jnp.float32
    )
    return score + mirrored.astype(jnp.float32)


def solution(mesh):
    in_specs = (P("ind", "snp"), P("snp", None), P(("snp", "ind")), P(("snp", "ind")))
    out_specs = P(("snp", "ind"), None)
    return jax.shard_map(
        per_device, mesh=mesh, in_specs=in_specs, out_specs=out_specs, check_vma=False
    )
```

time: 67.3 us -> 58.1 us (0.86)
  the two profiles are of different devices: /device:TPU:3 before, /device:TPU:4 now
where the time goes in v2:
time: 58.1 us; the launch traced here: 57.8 us
  starting transfers between devices  26 us (45%)
  waiting for transfers between devices  20.4 us (35%)
  matrix products  5.8 us (10%)
  other arithmetic  2.8 us (5%)
  local copies, waits for them, and re-layouts  2.52 us (4%)
    ppermute x9, waiting for transfers between devices, ring(): lax.ppermute(array, axis, [(i, (i + by) % devices) for i in range(devices)])  15.6 us
    ppermute x9, starting transfers between devices, ring(): lax.ppermute(array, axis, [(i, (i + by) % devices) for i in range(devices)])  13.4 us
    ppermute x5, starting transfers between devices, shifted(): return lax.ppermute(array, axis, pairs)  12.6 us
    ppermute x5, waiting for transfers between devices, shifted(): return lax.ppermute(array, axis, pairs)  4.77 us
    dot_general x3, matrix products, transposed_product(): lax.dot_general(left, right, (((0,), (0,)), ((), ())), preferred_element_...  4.41 us
    reduce_sum x1, other arithmetic, column_squares(): return jnp.sum(widened * widened, axis=0)  2.11 us
    unnamed x18, local copies, waits for them, and re-layouts  1.33 us
  transfers between devices with their start and end apart: 14, of which 8 were waited for; matrix products, arithmetic and copies ran while one was open for 17% of the time, Pallas kernels for 0%

profile of v2, /device:TPU:4, one launch (start us, length us, event | category | flops | bytes accessed | tf_op | source)
XLA Modules:
  0.0 57.8 jit_solution(3288248182380725789)
XLA Ops:
  0.0 2.9 %collective-permute-start.6 = (bf16[2048,512]{1,0:T(8,128)(2,1)}, bf16[2048,512]{1,0:T(8,128)(2,1)}, u32[]{:S(2)}, u32[]{:S(2)}) collective-permute-start(bf16[2048,512]{1,0:T(8,128)(2,1)} %param.4), channel_id=1, source_target_pairs={{4,0},{8,4},{12,8},{16,12},{20,16},{24,20},{28,24},{5,1},{9,5},{13... | collective-permute-start | bytes 6291464 | tf_op jit(solution)/shard_map/ppermute | solution.py:10
  2.9 2.1 %multiply_reduce_fusion = f32[512]{0:T(512)S(1)} fusion(bf16[2048,512]{1,0:T(8,128)(2,1)} %param.4), kind=kLoop, calls=%fused_computation | loop fusion | flops 3145216 | bytes 2099200 | tf_op jit(solution)/shard_map/reduce_sum | solution.py:24
  5.0 1.6 %collective-permute-start = (f32[512]{0:T(512)S(1)}, f32[512]{0:T(512)S(1)}, u32[]{:S(2)}, u32[]{:S(2)}) collective-permute-start(f32[512]{0:T(512)S(1)} %multiply_reduce_fusion), channel_id=1, source_target_pairs={{0,1},{1,2},{2,3},{3,0},{4,5},{5,6},{6,7},{7,4},{8,9},{9,10},{10,1... | collective-permute-start | bytes 6152 | tf_op jit(solution)/shard_map/ppermute | solution.py:15
  6.6 2.6 %collective-permute-start.1 = (f32[512]{0:T(512)S(1)}, f32[512]{0:T(512)S(1)}, u32[]{:S(2)}, u32[]{:S(2)}) collective-permute-start(f32[512]{0:T(512)S(1)} %multiply_reduce_fusion), channel_id=1, source_target_pairs={{0,2},{1,3},{2,0},{3,1},{4,6},{5,7},{6,4},{7,5},{8,10},{9,11},{10,... | collective-permute-start | bytes 6152 | tf_op jit(solution)/shard_map/ppermute | solution.py:15
  9.2 1.3 %collective-permute-start.2 = (f32[512]{0:T(512)S(1)}, f32[512]{0:T(512)S(1)}, u32[]{:S(2)}, u32[]{:S(2)}) collective-permute-start(f32[512]{0:T(512)S(1)} %multiply_reduce_fusion), channel_id=1, source_target_pairs={{0,3},{1,0},{2,1},{3,2},{4,7},{5,4},{6,5},{7,6},{8,11},{9,8},{10,9... | collective-permute-start | bytes 6152 | tf_op jit(solution)/shard_map/ppermute | solution.py:15
  10.7 0.5 collective-permute-done.1
  11.1 1.7 %collective-permute-done.2 = f32[512]{0:T(512)S(1)} collective-permute-done((f32[512]{0:T(512)S(1)}, f32[512]{0:T(512)S(1)}, u32[]{:S(2)}, u32[]{:S(2)}) %collective-permute-start.2) | collective-permute-done | bytes 2080 | tf_op jit(solution)/shard_map/ppermute | solution.py:15
  12.9 1.3 %fusion.2 = f16[512,512]{1,0:T(8,128)(2,1)S(1)} fusion(bf16[2048,512]{1,0:T(8,128)(2,1)S(1)} %copy-done, f32[512]{0:T(512)S(1)} %get-tuple-element.46), kind=kOutput, calls=%fused_computation.5 | convolution fusion | flops 1074528256 | bytes 2623488 | tf_op jit(solution)/shard_map/dot_general | solution.py:28
  14.3 3.2 %collective-permute-start.5 = (f16[128,512]{1,0:T(8,128)(2,1)S(1)}, f16[128,512]{1,0:T(8,128)(2,1)S(1)}, u32[]{:S(2)}, u32[]{:S(2)}) collective-permute-start(f16[128,512]{1,0:T(8,128)(2,1)S(1)} %get-tuple-element.27), channel_id=1, source_target_pairs={{0,3},{1,0},{2,1},{3,2},{4,7},{5,4},{6,5},{7,6},{8,11},{9,8},{10,9... | collective-permute-start | bytes 393224 | tf_op jit(solution)/shard_map/ppermute | solution.py:15
  17.5 0.6 %collective-permute-start.3 = (f16[128,512]{1,0:T(8,128)(2,1)S(1)}, f16[128,512]{1,0:T(8,128)(2,1)S(1)}, u32[]{:S(2)}, u32[]{:S(2)}) collective-permute-start(f16[128,512]{1,0:T(8,128)(2,1)S(1)} %get-tuple-element.29), channel_id=1, source_target_pairs={{0,1},{1,2},{2,3},{3,0},{4,5},{5,6},{6,7},{7,4},{8,9},{9,10},{10,1... | collective-permute-start | bytes 393224 | tf_op jit(solution)/shard_map/ppermute | solution.py:15
  18.1 1.9 %collective-permute-start.7 = (f32[512]{0:T(512)S(1)}, f32[512]{0:T(512)S(1)}, u32[]{:S(2)}, u32[]{:S(2)}) collective-permute-start(f32[512]{0:T(512)S(1)} %get-tuple-element.11), channel_id=1, source_target_pairs={{4,0},{8,4},{12,8},{16,12},{20,16},{24,20},{28,24},{5,1},{9,5},{13... | collective-permute-start | bytes 6152 | tf_op jit(solution)/shard_map/ppermute | solution.py:10
  20.0 1.1 %collective-permute-done.5 = f16[128,512]{1,0:T(8,128)(2,1)S(1)} collective-permute-done((f16[128,512]{1,0:T(8,128)(2,1)S(1)}, f16[128,512]{1,0:T(8,128)(2,1)S(1)}, u32[]{:S(2)}, u32[]{:S(2)}) %collective-permute-start.5) | collective-permute-done | bytes 131104 | tf_op jit(solution)/shard_map/ppermute | solution.py:15
  21.2 1.9 %collective-permute-start.12 = (s32[128]{0:T(128)S(1)}, s32[128]{0:T(128)S(1)}, u32[]{:S(2)}, u32[]{:S(2)}) collective-permute-start(s32[128]{0:T(128)S(1)} %copy-done.3), channel_id=1, source_target_pairs={{4,0},{8,4},{12,8},{16,12},{20,16},{24,20},{28,24},{5,1},{9,5},{13... | collective-permute-start | bytes 1544 | tf_op jit(solution)/shard_map/ppermute | solution.py:10
  23.1 4.3 %collective-permute-done.4 = f16[128,512]{1,0:T(8,128)(2,1)S(1)} collective-permute-done((f16[128,512]{1,0:T(8,128)(2,1)S(1)}, f16[128,512]{1,0:T(8,128)(2,1)S(1)}, u32[]{:S(2)}, u32[]{:S(2)}) %collective-permute-start.4) | collective-permute-done | bytes 131104 | tf_op jit(solution)/shard_map/ppermute | solution.py:15
  27.4 2.9 %fusion.4 = f16[512,512]{0,1:T(8,128)(2,1)S(1)} fusion(bf16[2048,512]{1,0:T(8,128)(2,1)} %collective-permute-done.6, bf16[2048,512]{1,0:T(8,128)(2,1)S(1)} %copy-done, f32[512]{0:T(512)S(1)} %collective-permute-done.7, f32[512]{0:T(512)S(1)} %get-tuple-element.11), kind=kOutput, calls=%fused_computation.7 | convolution fusion | flops 1074528256 | bytes 4722688 | tf_op jit(solution)/shard_map/dot_general | solution.py:28
  30.4 0.8 %fusion.45 = (f16[1,128,1,128]{1,0,3,2:T(2,128)(2,1)S(1)}, f16[1,128,1,128]{1,0,3,2:T(2,128)(2,1)S(1)}, f16[1,128,1,128]{1,0,3,2:T(2,128)(2,1)S(1)}, f16[1,128,1...) fusion(f16[4,128,4,128]{1,0,3,2:T(4,128)(2,1)S(1)} %reshape.70), kind=kLoop, calls=%fused_computation.84 | loop fusion | bytes 655360 | tf_op jit(solution)/shard_map/slice | solution.py:84
  33.2 1.0 %collective-permute-start.8 = (f16[4,128,128]{2,1,0:T(8,128)(2,1)S(1)}, f16[4,128,128]{2,1,0:T(8,128)(2,1)S(1)}, u32[]{:S(2)}, u32[]{:S(2)}) collective-permute-start(f16[4,128,128]{2,1,0:T(8,128)(2,1)S(1)} %get-tuple-element.13), channel_id=1, source_target_pairs={{0,1},{1,2},{2,3},{3,0},{4,5},{5,6},{6,7},{7,4},{8,9},{9,10},{10,1... | collective-permute-start | bytes 393224 | tf_op jit(solution)/shard_map/ppermute | solution.py:15
  34.2 2.9 %collective-permute-start.10 = (f16[4,128,128]{2,1,0:T(8,128)(2,1)S(1)}, f16[4,128,128]{2,1,0:T(8,128)(2,1)S(1)}, u32[]{:S(2)}, u32[]{:S(2)}) collective-permute-start(f16[4,128,128]{2,1,0:T(8,128)(2,1)S(1)} %get-tuple-element.14), channel_id=1, source_target_pairs={{0,3},{1,0},{2,1},{3,2},{4,7},{5,4},{6,5},{7,6},{8,11},{9,8},{10,9... | collective-permute-start | bytes 393224 | tf_op jit(solution)/shard_map/ppermute | solution.py:15
  37.3 3.9 %collective-permute-start.11 = (bf16[512,512]{1,0:T(8,128)(2,1)S(1)}, bf16[512,512]{1,0:T(8,128)(2,1)S(1)}, u32[]{:S(2)}, u32[]{:S(2)}) collective-permute-start(bf16[512,512]{1,0:T(8,128)(2,1)S(1)} %copy-done.1), channel_id=1, source_target_pairs={{4,0},{8,4},{12,8},{16,12},{20,16},{24,20},{28,24},{5,1},{9,5},{13... | collective-permute-start | bytes 1572872 | tf_op jit(solution)/shard_map/ppermute | solution.py:10
  41.4 1.6 %collective-permute-done.10 = f16[4,128,128]{2,1,0:T(8,128)(2,1)S(1)} collective-permute-done((f16[4,128,128]{2,1,0:T(8,128)(2,1)S(1)}, f16[4,128,128]{2,1,0:T(8,128)(2,1)S(1)}, u32[]{:S(2)}, u32[]{:S(2)}) %collective-permute-start.10) | collective-permute-done | bytes 131104 | tf_op jit(solution)/shard_map/ppermute | solution.py:15
  43.0 6.2 %collective-permute-done.9 = f16[4,128,128]{2,1,0:T(8,128)(2,1)S(1)} collective-permute-done((f16[4,128,128]{2,1,0:T(8,128)(2,1)S(1)}, f16[4,128,128]{2,1,0:T(8,128)(2,1)S(1)}, u32[]{:S(2)}, u32[]{:S(2)}) %collective-permute-start.9) | collective-permute-done | bytes 131104 | tf_op jit(solution)/shard_map/ppermute | solution.py:15
  49.6 2.0 %collective-permute-start.13 = (bf16[128,512]{1,0:T(8,128)(2,1)S(1)}, bf16[128,512]{1,0:T(8,128)(2,1)S(1)}, u32[]{:S(2)}, u32[]{:S(2)}) collective-permute-start(bf16[128,512]{1,0:T(8,128)(2,1)S(1)} %convolution_convert_fusion), channel_id=1, source_target_pairs={{0,4},{4,8},{8,12},{12,16},{16,20},{20,24},{24,28},{1,5},{5,9},{9,... | collective-permute-start | bytes 393224 | tf_op jit(solution)/shard_map/ppermute | solution.py:10
  52.0 4.8 %collective-permute-done.13 = bf16[128,512]{1,0:T(8,128)(2,1)S(1)} collective-permute-done((bf16[128,512]{1,0:T(8,128)(2,1)S(1)}, bf16[128,512]{1,0:T(8,128)(2,1)S(1)}, u32[]{:S(2)}, u32[]{:S(2)}) %collective-permute-start.13) | collective-permute-done | bytes 131104 | tf_op jit(solution)/shard_map/ppermute | solution.py:10
  56.8 1.0 %fusion.6 = f32[128,512]{1,0:T(8,128)} fusion(f32[128,512]{1,0:T(8,128)S(1)} %fusion.10, bf16[4,128,512]{2,1,0:T(8,128)(2,1)S(1)} %bitcast.57, bf16[128,512]{1,0:T(8,128)(2,1)S(1)} %collective-permute-done.13, bf16[4,128,128]{2,1,0:T(8,128)(2,1)S(1)} %get-tuple-element.10, s32[4,128]{1,0:T(4,128)S(1)} %broadcast_add_fusion, s32[128]{0:T(128)S(1)} %copy-done.2, ...), kind=kOutput, calls=%fused_computation.10 | convolution fusion | flops 67502080 | bytes 1313284 | tf_op jit(solution)/shard_map/dot_general | solution.py:117
  (43 shorter events, 3.4 us)
Async XLA Ops:
  0.0 12.8 %copy-start = (bf16[2048,512]{1,0:T(8,128)(2,1)S(1)}, bf16[2048,512]{1,0:T(8,128)(2,1)}, u32[]{:S(2)}) copy-start(bf16[2048,512]{1,0:T(8,128)(2,1)} %param.4) | copy-start | bytes 6291460
  0.0 27.4 %collective-permute-start.6 = (bf16[2048,512]{1,0:T(8,128)(2,1)}, bf16[2048,512]{1,0:T(8,128)(2,1)}, u32[]{:S(2)}, u32[]{:S(2)}) collective-permute-start(bf16[2048,512]{1,0:T(8,128)(2,1)} %param.4), channel_id=1, source_target_pairs={{4,0},{8,4},{12,8},{16,12},{20,16},{24,20},{28,24},{5,1},{9,5},{13... | collective-permute-start | bytes 6291464 | tf_op jit(solution)/shard_map/ppermute | solution.py:10
  5.0 5.6 %collective-permute-start = (f32[512]{0:T(512)S(1)}, f32[512]{0:T(512)S(1)}, u32[]{:S(2)}, u32[]{:S(2)}) collective-permute-start(f32[512]{0:T(512)S(1)} %multiply_reduce_fusion), channel_id=1, source_target_pairs={{0,1},{1,2},{2,3},{3,0},{4,5},{5,6},{6,7},{7,4},{8,9},{9,10},{10,1... | collective-permute-start | bytes 6152 | tf_op jit(solution)/shard_map/ppermute | solution.py:15
  6.6 4.5 %collective-permute-start.1 = (f32[512]{0:T(512)S(1)}, f32[512]{0:T(512)S(1)}, u32[]{:S(2)}, u32[]{:S(2)}) collective-permute-start(f32[512]{0:T(512)S(1)} %multiply_reduce_fusion), channel_id=1, source_target_pairs={{0,2},{1,3},{2,0},{3,1},{4,6},{5,7},{6,4},{7,5},{8,10},{9,11},{10,... | collective-permute-start | bytes 6152 | tf_op jit(solution)/shard_map/ppermute | solution.py:15
  9.2 3.6 %collective-permute-start.2 = (f32[512]{0:T(512)S(1)}, f32[512]{0:T(512)S(1)}, u32[]{:S(2)}, u32[]{:S(2)}) collective-permute-start(f32[512]{0:T(512)S(1)} %multiply_reduce_fusion), channel_id=1, source_target_pairs={{0,3},{1,0},{2,1},{3,2},{4,7},{5,4},{6,5},{7,6},{8,11},{9,8},{10,9... | collective-permute-start | bytes 6152 | tf_op jit(solution)/shard_map/ppermute | solution.py:15
  12.9 8.3 %copy-start.3 = (s32[128]{0:T(128)S(1)}, s32[128]{0:T(128)}, u32[]{:S(2)}) copy-start(s32[128]{0:T(128)} %param.6) | copy-start | bytes 1540
  14.3 6.9 %collective-permute-start.5 = (f16[128,512]{1,0:T(8,128)(2,1)S(1)}, f16[128,512]{1,0:T(8,128)(2,1)S(1)}, u32[]{:S(2)}, u32[]{:S(2)}) collective-permute-start(f16[128,512]{1,0:T(8,128)(2,1)S(1)} %get-tuple-element.27), channel_id=1, source_target_pairs={{0,3},{1,0},{2,1},{3,2},{4,7},{5,4},{6,5},{7,6},{8,11},{9,8},{10,9... | collective-permute-start | bytes 393224 | tf_op jit(solution)/shard_map/ppermute | solution.py:15
  17.5 9.9 %collective-permute-start.4 = (f16[128,512]{1,0:T(8,128)(2,1)S(1)}, f16[128,512]{1,0:T(8,128)(2,1)S(1)}, u32[]{:S(2)}, u32[]{:S(2)}) collective-permute-start(f16[128,512]{1,0:T(8,128)(2,1)S(1)} %get-tuple-element.28), channel_id=1, source_target_pairs={{0,2},{1,3},{2,0},{3,1},{4,6},{5,7},{6,4},{7,5},{8,10},{9,11},{10,... | collective-permute-start | bytes 393224 | tf_op jit(solution)/shard_map/ppermute | solution.py:15
  17.5 9.9 %collective-permute-start.3 = (f16[128,512]{1,0:T(8,128)(2,1)S(1)}, f16[128,512]{1,0:T(8,128)(2,1)S(1)}, u32[]{:S(2)}, u32[]{:S(2)}) collective-permute-start(f16[128,512]{1,0:T(8,128)(2,1)S(1)} %get-tuple-element.29), channel_id=1, source_target_pairs={{0,1},{1,2},{2,3},{3,0},{4,5},{5,6},{6,7},{7,4},{8,9},{9,10},{10,1... | collective-permute-start | bytes 393224 | tf_op jit(solution)/shard_map/ppermute | solution.py:15
  18.1 9.3 %collective-permute-start.7 = (f32[512]{0:T(512)S(1)}, f32[512]{0:T(512)S(1)}, u32[]{:S(2)}, u32[]{:S(2)}) collective-permute-start(f32[512]{0:T(512)S(1)} %get-tuple-element.11), channel_id=1, source_target_pairs={{4,0},{8,4},{12,8},{16,12},{20,16},{24,20},{28,24},{5,1},{9,5},{13... | collective-permute-start | bytes 6152 | tf_op jit(solution)/shard_map/ppermute | solution.py:10
  21.2 20.0 %collective-permute-start.12 = (s32[128]{0:T(128)S(1)}, s32[128]{0:T(128)S(1)}, u32[]{:S(2)}, u32[]{:S(2)}) collective-permute-start(s32[128]{0:T(128)S(1)} %copy-done.3), channel_id=1, source_target_pairs={{4,0},{8,4},{12,8},{16,12},{20,16},{24,20},{28,24},{5,1},{9,5},{13... | collective-permute-start | bytes 1544 | tf_op jit(solution)/shard_map/ppermute | solution.py:10
  31.3 6.0 %copy-start.1 = (bf16[512,512]{1,0:T(8,128)(2,1)S(1)}, bf16[512,512]{1,0:T(8,128)(2,1)}, u32[]{:S(2)}) copy-start(bf16[512,512]{1,0:T(8,128)(2,1)} %param.5) | copy-start | bytes 1572868
  32.6 19.0 %copy-start.2 = (s32[128]{0:T(128)S(1)}, s32[128]{0:T(128)}, u32[]{:S(2)}) copy-start(s32[128]{0:T(128)} %param.7) | copy-start | bytes 1540
  33.2 8.2 %collective-permute-start.8 = (f16[4,128,128]{2,1,0:T(8,128)(2,1)S(1)}, f16[4,128,128]{2,1,0:T(8,128)(2,1)S(1)}, u32[]{:S(2)}, u32[]{:S(2)}) collective-permute-start(f16[4,128,128]{2,1,0:T(8,128)(2,1)S(1)} %get-tuple-element.13), channel_id=1, source_target_pairs={{0,1},{1,2},{2,3},{3,0},{4,5},{5,6},{6,7},{7,4},{8,9},{9,10},{10,1... | collective-permute-start | bytes 393224 | tf_op jit(solution)/shard_map/ppermute | solution.py:15
  34.2 8.8 %collective-permute-start.10 = (f16[4,128,128]{2,1,0:T(8,128)(2,1)S(1)}, f16[4,128,128]{2,1,0:T(8,128)(2,1)S(1)}, u32[]{:S(2)}, u32[]{:S(2)}) collective-permute-start(f16[4,128,128]{2,1,0:T(8,128)(2,1)S(1)} %get-tuple-element.14), channel_id=1, source_target_pairs={{0,3},{1,0},{2,1},{3,2},{4,7},{5,4},{6,5},{7,6},{8,11},{9,8},{10,9... | collective-permute-start | bytes 393224 | tf_op jit(solution)/shard_map/ppermute | solution.py:15
  37.0 12.1 %collective-permute-start.9 = (f16[4,128,128]{2,1,0:T(8,128)(2,1)S(1)}, f16[4,128,128]{2,1,0:T(8,128)(2,1)S(1)}, u32[]{:S(2)}, u32[]{:S(2)}) collective-permute-start(f16[4,128,128]{2,1,0:T(8,128)(2,1)S(1)} %get-tuple-element.15), channel_id=1, source_target_pairs={{0,2},{1,3},{2,0},{3,1},{4,6},{5,7},{6,4},{7,5},{8,10},{9,11},{10,... | collective-permute-start | bytes 393224 | tf_op jit(solution)/shard_map/ppermute | solution.py:15
  37.3 19.5 %collective-permute-start.11 = (bf16[512,512]{1,0:T(8,128)(2,1)S(1)}, bf16[512,512]{1,0:T(8,128)(2,1)S(1)}, u32[]{:S(2)}, u32[]{:S(2)}) collective-permute-start(bf16[512,512]{1,0:T(8,128)(2,1)S(1)} %copy-done.1), channel_id=1, source_target_pairs={{4,0},{8,4},{12,8},{16,12},{20,16},{24,20},{28,24},{5,1},{9,5},{13... | collective-permute-start | bytes 1572872 | tf_op jit(solution)/shard_map/ppermute | solution.py:10
  49.6 7.2 %collective-permute-start.13 = (bf16[128,512]{1,0:T(8,128)(2,1)S(1)}, bf16[128,512]{1,0:T(8,128)(2,1)S(1)}, u32[]{:S(2)}, u32[]{:S(2)}) collective-permute-start(bf16[128,512]{1,0:T(8,128)(2,1)S(1)} %convolution_convert_fusion), channel_id=1, source_target_pairs={{0,4},{4,8},{8,12},{12,16},{16,20},{20,24},{24,28},{1,5},{5,9},{9,... | collective-permute-start | bytes 393224 | tf_op jit(solution)/shard_map/ppermute | solution.py:10

commit v3 on v2

v3 whole, which is shorter than its diff:
```python
import jax
import jax.numpy as jnp
from jax import lax
from jax.experimental import pallas as pl
from jax.experimental.pallas import tpu as pltpu
from jax.sharding import PartitionSpec as P


def shifted(array, axis, by):
    devices = lax.axis_size(axis)
    pairs = [(i, i + by) for i in range(devices) if 0 <= i + by < devices]
    return lax.ppermute(array, axis, pairs)


def ring(array, axis, by):
    devices = lax.axis_size(axis)
    return lax.ppermute(array, axis, [(i, (i + by) % devices) for i in range(devices)])


def after(value, *earlier):
    return lax.optimization_barrier((value, *earlier))[0]


def column_squares(block):
    widened = block.astype(jnp.float32)
    return jnp.sum(widened * widened, axis=0)


def transposed_product(left, right):
    return lax.dot_general(
        left, right, (((0,), (0,)), ((), ())), preferred_element_type=jnp.float32
    )


def exchanged(slots, axis, extra=None):
    devices = lax.axis_size(axis)
    place = lax.axis_index(axis)
    terms = []
    for by in range(devices):
        mine = lax.dynamic_index_in_dim(slots, (place + by) % devices, 0, keepdims=False)
        if extra is not None:
            mine = jnp.concatenate([mine, extra], axis=0)
        terms.append(mine if by == 0 else ring(mine, axis, by))
    return terms


def coded(norm):
    exponent = jnp.floor(jnp.log2(jnp.where(norm > 0.0, norm, 1.0)))
    mantissa = norm * jnp.exp2(-exponent)
    high = lax.optimization_barrier(mantissa.astype(jnp.float16))
    low = (mantissa - high.astype(jnp.float32)).astype(jnp.float16)
    rows = jnp.stack([high, low, exponent.astype(jnp.float16)])
    return jnp.pad(rows, ((0, 13), (0, 0)))


def decoded(rows):
    high, low, exponent = (rows[i].astype(jnp.float32) for i in range(3))
    return (high + low) * jnp.exp2(exponent)


def inverse_norm(sumsq):
    return lax.rsqrt(jnp.where(sumsq > 0.0, sumsq, 1.0))


def adjusted(corr, count_all):
    squared = corr * corr
    return (squared - (1.0 - squared) / (count_all - 2.0)).astype(jnp.bfloat16)


def completed_kernel(left, right, left_scale, right_scale, out):
    product = transposed_product(left[...], right[...])
    product = product * left_scale[...] * right_scale[...]
    rows = lax.broadcasted_iota(jnp.int32, product.shape, 0)
    columns = lax.broadcasted_iota(jnp.int32, product.shape, 1)
    out[...] = jnp.where(rows >= columns, product, product.T)


def completed_product(left, right, left_scale, right_scale):
    depth, width = left.shape
    return pl.pallas_call(
        completed_kernel,
        out_shape=jax.ShapeDtypeStruct((width, width), jnp.float32),
        compiler_params=pltpu.CompilerParams(vmem_limit_bytes=32 * 1024 * 1024),
        cost_estimate=pl.CostEstimate(
            flops=2 * depth * width * width, bytes_accessed=4 * depth * width, transcendentals=0
        ),
    )(left, right, left_scale[:, None], right_scale[None, :])


def per_device(genotypes, annotations, window_start, window_end):
    stripe = genotypes.shape[1]
    groups = lax.axis_size("ind")
    count_all = float(genotypes.shape[0] * groups)
    sub_rows = stripe // groups
    place = lax.axis_index("ind")
    stripe_first = lax.axis_index("snp") * stripe
    geno_above = shifted(genotypes, "snp", -1)

    squares = column_squares(genotypes)
    scale = inverse_norm(squares)
    own_part = transposed_product(genotypes, genotypes) * scale[:, None] * scale[None, :]
    own_part = own_part.astype(jnp.float16).reshape(groups, sub_rows, stripe)
    own_terms = exchanged(own_part, "ind", coded(squares * scale))

    first, second = own_terms[-1], own_terms[-2]
    scale_above = inverse_norm(shifted(after(squares, first), "snp", -1))
    annot_above = shifted(after(annotations, first, second), "snp", -1)

    geno_above = after(geno_above, first, second)
    cross_part = completed_product(genotypes, geno_above, scale, scale_above)
    cross_part = cross_part.astype(jnp.float16).reshape(groups, sub_rows, stripe)
    cross_terms = exchanged(cross_part, "ind")

    norms = jnp.stack([decoded(after(term[sub_rows:], cross_part)) for term in own_terms])
    sumsq = jnp.sum(norms * norms, axis=0)
    shares = norms * inverse_norm(sumsq)
    starts = jnp.pad(window_start.astype(jnp.float32), (0, stripe - sub_rows))
    above = shifted(jnp.concatenate([shares, starts[None]]), "snp", -1)
    shares_above = above[:groups]
    start_above = above[groups, :sub_rows].astype(jnp.int32)

    def rows_of(array):
        return lax.dynamic_slice_in_dim(array, place * sub_rows, sub_rows, array.ndim - 1)

    ids = jnp.arange(stripe, dtype=jnp.int32)
    own_ids = stripe_first + ids
    row_ids = place * sub_rows + jnp.arange(sub_rows, dtype=jnp.int32)
    lower = row_ids[:, None] >= ids[None, :]
    row_shares = rows_of(norms) * lax.rsqrt(rows_of(sumsq))
    row_safe = rows_of(shares)
    row_above = rows_of(shares_above)
    own_corr = 0.0
    cross_corr = 0.0
    for by in range(groups):
        own = own_terms[by][:sub_rows].astype(jnp.float32)
        own_corr += own * row_shares[by][:, None] * shares[by][None, :]
        cross = cross_terms[by].astype(jnp.float32)
        below = row_safe[by][:, None] * shares_above[by][None, :]
        cross_corr += cross * jnp.where(lower, below, row_above[by][:, None] * shares[by][None, :])

    inside = (own_ids[None, :] >= window_start[:, None]) & (own_ids[None, :] < window_end[:, None])
    own_weights = jnp.where(inside, adjusted(own_corr, count_all), 0)
    score = jnp.dot(own_weights, annotations, preferred_element_type=jnp.float32)

    cross_weights = adjusted(cross_corr, count_all)
    inside = (own_ids[None, :] >= start_above[:, None]) & (ids[None, :] >= row_ids[:, None])
    mirrored = jnp.where(inside, cross_weights, 0)
    mirrored = jnp.dot(mirrored, annotations, preferred_element_type=jnp.float32)
    mirrored = shifted(mirrored.astype(jnp.bfloat16), "snp", 1)

    inside = (own_ids[None, :] + stripe < window_end[:, None]) & lower
    above_weights = jnp.where(inside, cross_weights, 0)
    score += jnp.dot(above_weights, annot_above, preferred_element_type=jnp.float32)
    return score + mirrored.astype(jnp.float32)


def solution(mesh):
    in_specs = (P("ind", "snp"), P("snp", None), P(("snp", "ind")), P(("snp", "ind")))
    out_specs = P(("snp", "ind"), None)
    return jax.shard_map(
        per_device, mesh=mesh, in_specs=in_specs, out_specs=out_specs, check_vma=False
    )
```

time: 58.1 us -> 55.5 us (0.955)
  the two profiles are of different devices: /device:TPU:4 before, /device:TPU:12 now
where the time goes in v3:
time: 55.5 us; the launch traced here: 55 us
  starting transfers between devices  22.7 us (41%)
  waiting for transfers between devices  18.7 us (34%)
  matrix products  3.97 us (7%)
  other arithmetic  3.57 us (6%)
  Pallas kernels  3.02 us (5%)
  local copies, waits for them, and re-layouts  2.64 us (5%)
    ppermute x5, starting transfers between devices, shifted(): return lax.ppermute(array, axis, pairs)  12.5 us
    ppermute x6, waiting for transfers between devices, ring(): lax.ppermute(array, axis, [(i, (i + by) % devices) for i in range(devices)])  11.3 us
    ppermute x6, starting transfers between devices, ring(): lax.ppermute(array, axis, [(i, (i + by) % devices) for i in range(devices)])  10.1 us
    ppermute x5, waiting for transfers between devices, shifted(): return lax.ppermute(array, axis, pairs)  7.37 us
    pallas_call x1, Pallas kernels, completed_product(): pl.pallas_call(completed_kernel, out_shape=jax.ShapeDtypeStruct((width, w...  3.02 us
    slice x3, local copies, waits for them, and re-layouts, per_device(): term[sub_rows:]  2.17 us
    reduce_sum x1, other arithmetic, column_squares(): return jnp.sum(widened * widened, axis=0)  2.11 us
    dot_general x1, matrix products, per_device(): jnp.dot(own_weights, annotations, preferred_element_type=jnp.float32)  1.43 us
  transfers between devices with their start and end apart: 11, of which 7 were waited for; matrix products, arithmetic and copies ran while one was open for 17% of the time, Pallas kernels for 5%

profile of v3, /device:TPU:12, one launch (start us, length us, event | category | flops | bytes accessed | tf_op | source)
XLA Modules:
  0.0 55.0 jit_solution(17077801451262188771)
XLA Ops:
  0.0 2.9 %collective-permute-start = (bf16[2048,512]{1,0:T(8,128)(2,1)}, bf16[2048,512]{1,0:T(8,128)(2,1)}, u32[]{:S(2)}, u32[]{:S(2)}) collective-permute-start(bf16[2048,512]{1,0:T(8,128)(2,1)} %left.1), channel_id=1, source_target_pairs={{4,0},{8,4},{12,8},{16,12},{20,16},{24,20},{28,24},{5,1},{9,5},{13... | collective-permute-start | bytes 6291464 | tf_op jit(solution)/shard_map/ppermute | solution.py:12
  2.9 2.1 %multiply_reduce_fusion = f32[512]{0:T(512)S(1)} fusion(bf16[2048,512]{1,0:T(8,128)(2,1)} %left.1), kind=kLoop, calls=%fused_computation | loop fusion | flops 3145216 | bytes 2099200 | tf_op jit(solution)/shard_map/reduce_sum | solution.py:26
  5.2 1.3 %fusion.1 = f16[512,512]{1,0:T(8,128)(2,1)S(1)} fusion(bf16[2048,512]{1,0:T(8,128)(2,1)S(1)} %copy-done, f32[512]{0:T(512)S(1)} %get-tuple-element.50), kind=kOutput, calls=%fused_computation.3 | convolution fusion | flops 1074528256 | bytes 2623488 | tf_op jit(solution)/shard_map/dot_general | solution.py:30
  6.6 0.8 %pad_maximum_fusion = (f16[144,512]{1,0:T(8,128)(2,1)S(1)}, f16[144,512]{1,0:T(8,128)(2,1)S(1)}, f16[144,512]{1,0:T(8,128)(2,1)}) fusion(f16[16,512]{1,0:T(8,128)(2,1)S(1)} %fusion.50, f16[128,512]{1,0:T(8,128)(2,1)S(1)} %get-tuple-element.24, f16[128,512]{1,0:T(8,128)(2,1)S(1)} %get-tuple-element.25, f16[128,512]{1,0:T(8,128)(2,1)S(1)} %get-tuple-element.26), kind=kLoop, calls=%fused_computation.29 | loop fusion | flops 221184 | bytes 851968 | tf_op jit(solution)/shard_map/concatenate | solution.py:42
  7.8 2.6 %collective-permute-start.2 = (f16[144,512]{1,0:T(8,128)(2,1)S(1)}, f16[144,512]{1,0:T(8,128)(2,1)}, u32[]{:S(2)}, u32[]{:S(2)}) collective-permute-start(f16[144,512]{1,0:T(8,128)(2,1)S(1)} %get-tuple-element.32), channel_id=1, source_target_pairs={{0,2},{1,3},{2,0},{3,1},{4,6},{5,7},{6,4},{7,5},{8,10},{9,11},{10,... | collective-permute-start | bytes 442376 | tf_op jit(solution)/shard_map/ppermute | solution.py:17
  10.4 2.5 %collective-permute-start.4 = (f16[144,512]{1,0:T(8,128)(2,1)S(1)}, f16[144,512]{1,0:T(8,128)(2,1)}, u32[]{:S(2)}, u32[]{:S(2)}) collective-permute-start(f16[144,512]{1,0:T(8,128)(2,1)S(1)} %get-tuple-element.31), channel_id=1, source_target_pairs={{0,1},{1,2},{2,3},{3,0},{4,5},{5,6},{6,7},{7,4},{8,9},{9,10},{10,1... | collective-permute-start | bytes 442376 | tf_op jit(solution)/shard_map/ppermute | solution.py:17
  13.8 1.9 %collective-permute-start.3 = (f32[512]{0:T(512)S(1)}, f32[512]{0:T(512)S(1)}, u32[]{:S(2)}, u32[]{:S(2)}) collective-permute-start(f32[512]{0:T(512)S(1)} %multiply_reduce_fusion), channel_id=1, source_target_pairs={{4,0},{8,4},{12,8},{16,12},{20,16},{24,20},{28,24},{5,1},{9,5},{13... | collective-permute-start | bytes 6152 | tf_op jit(solution)/shard_map/ppermute | solution.py:12
  15.8 4.7 %collective-permute-done.2 = f16[144,512]{1,0:T(8,128)(2,1)} collective-permute-done((f16[144,512]{1,0:T(8,128)(2,1)S(1)}, f16[144,512]{1,0:T(8,128)(2,1)}, u32[]{:S(2)}, u32[]{:S(2)}) %collective-permute-start.2) | collective-permute-done | bytes 147488 | tf_op jit(solution)/shard_map/ppermute | solution.py:17
  20.5 1.9 %collective-permute-start.9 = (bf16[512,512]{1,0:T(8,128)(2,1)}, bf16[512,512]{1,0:T(8,128)(2,1)S(1)}, u32[]{:S(2)}, u32[]{:S(2)}) collective-permute-start(bf16[512,512]{1,0:T(8,128)(2,1)} %param.5), channel_id=1, source_target_pairs={{4,0},{8,4},{12,8},{16,12},{20,16},{24,20},{28,24},{5,1},{9,5},{13... | collective-permute-start | bytes 1572872 | tf_op jit(solution)/shard_map/ppermute | solution.py:12
  22.4 0.7 %slice.169 = f16[16,512]{1,0:T(8,128)(2,1)S(1)} slice(f16[144,512]{1,0:T(8,128)(2,1)} %collective-permute-done.2), slice={[128:144], [0:512]} | slice | bytes 32768 | tf_op jit(solution)/shard_map/slice | solution.py:114
  23.1 0.7 %slice.170 = f16[16,512]{1,0:T(8,128)(2,1)S(1)} slice(f16[144,512]{1,0:T(8,128)(2,1)} %collective-permute-done.1), slice={[128:144], [0:512]} | slice | bytes 32768 | tf_op jit(solution)/shard_map/slice | solution.py:114
  23.8 0.7 %slice.168 = f16[16,512]{1,0:T(8,128)(2,1)S(1)} slice(f16[144,512]{1,0:T(8,128)(2,1)} %collective-permute-done.4), slice={[128:144], [0:512]} | slice | bytes 32768 | tf_op jit(solution)/shard_map/slice | solution.py:114
  24.6 2.2 %collective-permute-done.3 = f32[512]{0:T(512)S(1)} collective-permute-done((f32[512]{0:T(512)S(1)}, f32[512]{0:T(512)S(1)}, u32[]{:S(2)}, u32[]{:S(2)}) %collective-permute-start.3) | collective-permute-done | bytes 2080 | tf_op jit(solution)/shard_map/ppermute | solution.py:12
  26.8 3.0 %shard_map.46 = f32[512,512]{1,0:T(8,128)S(1)} custom-call(bf16[2048,512]{1,0:T(8,128)(2,1)S(1)} %copy-done, bf16[2048,512]{1,0:T(8,128)(2,1)} %collective-permute-done.right, f32[512,1]{1,0:T(8,128)S(1)} %fusion.3.left_scale, f32[1,512]{1,0:T(1,128)S(1)} %bitcast.66), custom_call_target="tpu_custom_call" | custom-call | flops 1073741824 | bytes 4194304 | tf_op jit(solution)/shard_map/pallas_call | solution.py:80
  30.2 1.6 %collective-permute-start.6 = (f16[128,512]{1,0:T(8,128)(2,1)S(1)}, f16[128,512]{1,0:T(8,128)(2,1)S(1)}, u32[]{:S(2)}, u32[]{:S(2)}) collective-permute-start(f16[128,512]{1,0:T(8,128)(2,1)S(1)} %get-tuple-element.21), channel_id=1, source_target_pairs={{0,1},{1,2},{2,3},{3,0},{4,5},{5,6},{6,7},{7,4},{8,9},{9,10},{10,1... | collective-permute-start | bytes 393224 | tf_op jit(solution)/shard_map/ppermute | solution.py:17
  31.8 2.7 %collective-permute-start.7 = (f16[128,512]{1,0:T(8,128)(2,1)S(1)}, f16[128,512]{1,0:T(8,128)(2,1)S(1)}, u32[]{:S(2)}, u32[]{:S(2)}) collective-permute-start(f16[128,512]{1,0:T(8,128)(2,1)S(1)} %get-tuple-element.23), channel_id=1, source_target_pairs={{0,2},{1,3},{2,0},{3,1},{4,6},{5,7},{6,4},{7,5},{8,10},{9,11},{10,... | collective-permute-start | bytes 393224 | tf_op jit(solution)/shard_map/ppermute | solution.py:17
  34.9 3.9 %collective-permute-start.5 = (f32[5,512]{1,0:T(8,128)S(1)}, f32[5,512]{1,0:T(8,128)S(1)}, u32[]{:S(2)}, u32[]{:S(2)}) collective-permute-start(f32[5,512]{1,0:T(8,128)S(1)} %pad_maximum_fusion.3), channel_id=1, source_target_pairs={{4,0},{8,4},{12,8},{16,12},{20,16},{24,20},{28,24},{5,1},{9,5},{13... | collective-permute-start | bytes 30728 | tf_op jit(solution)/shard_map/ppermute | solution.py:12
  38.8 1.4 %collective-permute-done.5 = f32[5,512]{1,0:T(8,128)S(1)} collective-permute-done((f32[5,512]{1,0:T(8,128)S(1)}, f32[5,512]{1,0:T(8,128)S(1)}, u32[]{:S(2)}, u32[]{:S(2)}) %collective-permute-start.5) | collective-permute-done | bytes 10272 | tf_op jit(solution)/shard_map/ppermute | solution.py:12
  40.2 3.9 %collective-permute-done.7 = f16[128,512]{1,0:T(8,128)(2,1)S(1)} collective-permute-done((f16[128,512]{1,0:T(8,128)(2,1)S(1)}, f16[128,512]{1,0:T(8,128)(2,1)S(1)}, u32[]{:S(2)}, u32[]{:S(2)}) %collective-permute-start.7) | collective-permute-done | bytes 131104 | tf_op jit(solution)/shard_map/ppermute | solution.py:17
  44.1 2.1 %collective-permute-done.8 = f16[128,512]{1,0:T(8,128)(2,1)S(1)} collective-permute-done((f16[128,512]{1,0:T(8,128)(2,1)S(1)}, f16[128,512]{1,0:T(8,128)(2,1)S(1)}, u32[]{:S(2)}, u32[]{:S(2)}) %collective-permute-start.8) | collective-permute-done | bytes 131104 | tf_op jit(solution)/shard_map/ppermute | solution.py:17
  46.8 1.9 %collective-permute-start.10 = (bf16[128,512]{1,0:T(8,128)(2,1)S(1)}, bf16[128,512]{1,0:T(8,128)(2,1)S(1)}, u32[]{:S(2)}, u32[]{:S(2)}) collective-permute-start(bf16[128,512]{1,0:T(8,128)(2,1)S(1)} %convolution_convert_fusion), channel_id=1, source_target_pairs={{0,4},{4,8},{8,12},{12,16},{16,20},{20,24},{24,28},{1,5},{5,9},{9,... | collective-permute-start | bytes 393224 | tf_op jit(solution)/shard_map/ppermute | solution.py:12
  48.7 1.4 %fusion.17 = f32[128,512]{1,0:T(8,128)S(1)} fusion(bf16[512,512]{1,0:T(8,128)(2,1)S(1)} %copy-done.2, f16[144,512]{1,0:T(8,128)(2,1)} %collective-permute-done.1, f16[144,512]{1,0:T(8,128)(2,1)} %collective-permute-done.2, f16[144,512]{1,0:T(8,128)(2,1)} %collective-permute-done.4, f32[512]{0:T(512)S(1)} %bitcast.76, f32[128]{0:T(128)S(1)} %get-tuple-element.47, ...), kind=kOutput, calls=%fused_computation.32 | convolution fusion | flops 68681728 | bytes 1324036 | tf_op jit(solution)/shard_map/dot_general | solution.py:143
  50.2 3.8 %collective-permute-done.10 = bf16[128,512]{1,0:T(8,128)(2,1)S(1)} collective-permute-done((bf16[128,512]{1,0:T(8,128)(2,1)S(1)}, bf16[128,512]{1,0:T(8,128)(2,1)S(1)}, u32[]{:S(2)}, u32[]{:S(2)}) %collective-permute-start.10) | collective-permute-done | bytes 131104 | tf_op jit(solution)/shard_map/ppermute | solution.py:12
  54.0 1.0 %fusion.2 = f32[128,512]{1,0:T(8,128)} fusion(f32[128,512]{1,0:T(8,128)S(1)} %fusion.17, bf16[512,512]{1,0:T(8,128)(2,1)S(1)} %collective-permute-done.9, bf16[128,512]{1,0:T(8,128)(2,1)S(1)} %collective-permute-done.10, bf16[128,512]{1,0:T(8,128)(2,1)S(1)} %subtract_convert_fusion, s32[128]{0:T(128)S(1)} %iota_add_fusion.1, s32[512]{0:T(512)S(1)} %broadcast_add_fusion, ...), kind=kOutput, calls=%fused_computation.5 | convolution fusion | flops 67567616 | bytes 1313792 | tf_op jit(solution)/shard_map/dot_general | solution.py:153
  (51 shorter events, 2.9 us)
Async XLA Ops:
  0.0 5.2 %copy-start = (bf16[2048,512]{1,0:T(8,128)(2,1)S(1)}, bf16[2048,512]{1,0:T(8,128)(2,1)}, u32[]{:S(2)}) copy-start(bf16[2048,512]{1,0:T(8,128)(2,1)} %left.1) | copy-start | bytes 6291460
  0.0 26.8 %collective-permute-start = (bf16[2048,512]{1,0:T(8,128)(2,1)}, bf16[2048,512]{1,0:T(8,128)(2,1)}, u32[]{:S(2)}, u32[]{:S(2)}) collective-permute-start(bf16[2048,512]{1,0:T(8,128)(2,1)} %left.1), channel_id=1, source_target_pairs={{4,0},{8,4},{12,8},{16,12},{20,16},{24,20},{28,24},{5,1},{9,5},{13... | collective-permute-start | bytes 6291464 | tf_op jit(solution)/shard_map/ppermute | solution.py:12
  6.5 9.3 %copy-start.3 = (s32[128]{0:T(128)S(1)}, s32[128]{0:T(128)}, u32[]{:S(2)}) copy-start(s32[128]{0:T(128)} %param.6) | copy-start | bytes 1540
  7.4 6.5 %collective-permute-start.1 = (f16[144,512]{1,0:T(8,128)(2,1)}, f16[144,512]{1,0:T(8,128)(2,1)}, u32[]{:S(2)}, u32[]{:S(2)}) collective-permute-start(f16[144,512]{1,0:T(8,128)(2,1)} %get-tuple-element.33), channel_id=1, source_target_pairs={{0,3},{1,0},{2,1},{3,2},{4,7},{5,4},{6,5},{7,6},{8,11},{9,8},{10,9... | collective-permute-start | bytes 442376 | tf_op jit(solution)/shard_map/ppermute | solution.py:17
  7.8 12.7 %collective-permute-start.2 = (f16[144,512]{1,0:T(8,128)(2,1)S(1)}, f16[144,512]{1,0:T(8,128)(2,1)}, u32[]{:S(2)}, u32[]{:S(2)}) collective-permute-start(f16[144,512]{1,0:T(8,128)(2,1)S(1)} %get-tuple-element.32), channel_id=1, source_target_pairs={{0,2},{1,3},{2,0},{3,1},{4,6},{5,7},{6,4},{7,5},{8,10},{9,11},{10,... | collective-permute-start | bytes 442376 | tf_op jit(solution)/shard_map/ppermute | solution.py:17
  10.4 13.4 %collective-permute-start.4 = (f16[144,512]{1,0:T(8,128)(2,1)S(1)}, f16[144,512]{1,0:T(8,128)(2,1)}, u32[]{:S(2)}, u32[]{:S(2)}) collective-permute-start(f16[144,512]{1,0:T(8,128)(2,1)S(1)} %get-tuple-element.31), channel_id=1, source_target_pairs={{0,1},{1,2},{2,3},{3,0},{4,5},{5,6},{6,7},{7,4},{8,9},{9,10},{10,1... | collective-permute-start | bytes 442376 | tf_op jit(solution)/shard_map/ppermute | solution.py:17
  13.8 12.9 %collective-permute-start.3 = (f32[512]{0:T(512)S(1)}, f32[512]{0:T(512)S(1)}, u32[]{:S(2)}, u32[]{:S(2)}) collective-permute-start(f32[512]{0:T(512)S(1)} %multiply_reduce_fusion), channel_id=1, source_target_pairs={{4,0},{8,4},{12,8},{16,12},{20,16},{24,20},{28,24},{5,1},{9,5},{13... | collective-permute-start | bytes 6152 | tf_op jit(solution)/shard_map/ppermute | solution.py:12
  20.5 29.7 %collective-permute-start.9 = (bf16[512,512]{1,0:T(8,128)(2,1)}, bf16[512,512]{1,0:T(8,128)(2,1)S(1)}, u32[]{:S(2)}, u32[]{:S(2)}) collective-permute-start(bf16[512,512]{1,0:T(8,128)(2,1)} %param.5), channel_id=1, source_target_pairs={{4,0},{8,4},{12,8},{16,12},{20,16},{24,20},{28,24},{5,1},{9,5},{13... | collective-permute-start | bytes 1572872 | tf_op jit(solution)/shard_map/ppermute | solution.py:12
  29.8 16.7 %copy-start.2 = (bf16[512,512]{1,0:T(8,128)(2,1)S(1)}, bf16[512,512]{1,0:T(8,128)(2,1)}, u32[]{:S(2)}) copy-start(bf16[512,512]{1,0:T(8,128)(2,1)} %param.5) | copy-start | bytes 1572868
  29.8 18.9 %copy-start.1 = (s32[128]{0:T(128)S(1)}, s32[128]{0:T(128)}, u32[]{:S(2)}) copy-start(s32[128]{0:T(128)} %param.7) | copy-start | bytes 1540
  30.2 10.0 %collective-permute-start.6 = (f16[128,512]{1,0:T(8,128)(2,1)S(1)}, f16[128,512]{1,0:T(8,128)(2,1)S(1)}, u32[]{:S(2)}, u32[]{:S(2)}) collective-permute-start(f16[128,512]{1,0:T(8,128)(2,1)S(1)} %get-tuple-element.21), channel_id=1, source_target_pairs={{0,1},{1,2},{2,3},{3,0},{4,5},{5,6},{6,7},{7,4},{8,9},{9,10},{10,1... | collective-permute-start | bytes 393224 | tf_op jit(solution)/shard_map/ppermute | solution.py:17
  31.8 12.3 %collective-permute-start.7 = (f16[128,512]{1,0:T(8,128)(2,1)S(1)}, f16[128,512]{1,0:T(8,128)(2,1)S(1)}, u32[]{:S(2)}, u32[]{:S(2)}) collective-permute-start(f16[128,512]{1,0:T(8,128)(2,1)S(1)} %get-tuple-element.23), channel_id=1, source_target_pairs={{0,2},{1,3},{2,0},{3,1},{4,6},{5,7},{6,4},{7,5},{8,10},{9,11},{10,... | collective-permute-start | bytes 393224 | tf_op jit(solution)/shard_map/ppermute | solution.py:17
  34.5 11.6 %collective-permute-start.8 = (f16[128,512]{1,0:T(8,128)(2,1)S(1)}, f16[128,512]{1,0:T(8,128)(2,1)S(1)}, u32[]{:S(2)}, u32[]{:S(2)}) collective-permute-start(f16[128,512]{1,0:T(8,128)(2,1)S(1)} %get-tuple-element.22), channel_id=1, source_target_pairs={{0,3},{1,0},{2,1},{3,2},{4,7},{5,4},{6,5},{7,6},{8,11},{9,8},{10,9... | collective-permute-start | bytes 393224 | tf_op jit(solution)/shard_map/ppermute | solution.py:17
  34.9 5.3 %collective-permute-start.5 = (f32[5,512]{1,0:T(8,128)S(1)}, f32[5,512]{1,0:T(8,128)S(1)}, u32[]{:S(2)}, u32[]{:S(2)}) collective-permute-start(f32[5,512]{1,0:T(8,128)S(1)} %pad_maximum_fusion.3), channel_id=1, source_target_pairs={{4,0},{8,4},{12,8},{16,12},{20,16},{24,20},{28,24},{5,1},{9,5},{13... | collective-permute-start | bytes 30728 | tf_op jit(solution)/shard_map/ppermute | solution.py:12
  46.8 7.2 %collective-permute-start.10 = (bf16[128,512]{1,0:T(8,128)(2,1)S(1)}, bf16[128,512]{1,0:T(8,128)(2,1)S(1)}, u32[]{:S(2)}, u32[]{:S(2)}) collective-permute-start(bf16[128,512]{1,0:T(8,128)(2,1)S(1)} %convolution_convert_fusion), channel_id=1, source_target_pairs={{0,4},{4,8},{8,12},{12,16},{16,20},{20,24},{24,28},{1,5},{5,9},{9,... | collective-permute-start | bytes 393224 | tf_op jit(solution)/shard_map/ppermute | solution.py:12

commit v4 on v0

v4 whole, which is shorter than its diff:
```python
import functools

import jax
import jax.numpy as jnp
from jax import lax
from jax.experimental import pallas as pl
from jax.experimental.pallas import tpu as pltpu
from jax.sharding import PartitionSpec as P

UNIT = 32000.0
COST_T, COST_O, COST_F, COST_S, COST_H = 2.0, 2.5, 2.5, 2.0, 1.0
LANES = 128
CODE_ROWS = 16


def shifted(array, axis, by):
    devices = lax.axis_size(axis)
    pairs = [(i, i + by) for i in range(devices) if 0 <= i + by < devices]
    return lax.ppermute(array, axis, pairs)


def after(value, *earlier):
    return lax.optimization_barrier((value, *earlier))[0]


def exchanged(slabs, axis):
    devices = lax.axis_size(axis)
    return [slabs[0]] + [
        lax.ppermute(slabs[by], axis, [(i, i ^ by) for i in range(devices)])
        for by in range(1, devices)
    ]


def column_squares(block):
    widened = block.astype(jnp.float32)
    return jnp.sum(widened * widened, axis=0, keepdims=True)


def transposed_product(left, right):
    return lax.dot_general(
        left, right, (((0,), (0,)), ((), ())), preferred_element_type=jnp.float32
    )


def inverse_norm(sumsq):
    return lax.rsqrt(jnp.where(sumsq > 0.0, sumsq, 1.0))


def as_columns(row, width):
    return jnp.broadcast_to(row, (width, row.shape[1])).T


def mirrored_lower(square):
    rows = lax.broadcasted_iota(jnp.int32, square.shape, 0)
    columns = lax.broadcasted_iota(jnp.int32, square.shape, 1)
    return jnp.where(rows >= columns, square, square.T)


def to_fixed(values):
    return jnp.round(values * UNIT).astype(jnp.int32).astype(jnp.int16)


def coded(norm):
    exponent = jnp.floor(jnp.log2(jnp.where(norm > 0.0, norm, 1.0)))
    mantissa = norm * jnp.exp2(-exponent) * 8192.0
    high = jnp.floor(mantissa)
    low = jnp.floor((mantissa - high) * 16384.0 + 0.5)
    rows = lax.broadcasted_iota(jnp.int32, (CODE_ROWS, norm.shape[1]), 0)
    values = jnp.where(rows == 0, high, jnp.where(rows == 1, low, exponent))
    return jnp.where(rows < 3, values, 0.0).astype(jnp.int32).astype(jnp.int16)


def decoded(rows):
    rows = rows.astype(jnp.int32).astype(jnp.float32)
    mantissa = (rows[0:1] + rows[1:2] * (1.0 / 16384.0)) * (1.0 / 8192.0)
    return mantissa * jnp.exp2(rows[2:3])


def adjusted(corr, count_all):
    squared = corr * corr
    return squared - (1.0 - squared) / (count_all - 2.0)


def kernel_call(kernel, out_shape, operands, in_specs=None, grid=None, scratch=(), cost=0.0):
    in_specs = in_specs or [None] * len(operands)
    whole = pl.BlockSpec(memory_space=pltpu.VMEM)
    extra = {} if grid is None else {"grid": grid}
    return pl.pallas_call(
        kernel,
        out_shape=out_shape,
        in_specs=[spec or whole for spec in in_specs],
        scratch_shapes=list(scratch),
        compiler_params=pltpu.CompilerParams(vmem_limit_bytes=36 * 1024 * 1024),
        cost_estimate=pl.CostEstimate(flops=0, bytes_accessed=int(cost * 3.7e6), transcendentals=0),
        **extra,
    )(*operands)


def write_slabs(place, values, slabs):
    rows = values.shape[0] // len(slabs)
    for by, slab in enumerate(slabs):
        first = (place ^ by) * rows
        slab[:rows] = to_fixed(values[pl.ds(pl.multiple_of(first, 16), rows), :])


def own_kernel(groups, place, array, second, scale, *rest):
    slabs, values = rest[:groups], rest[groups]
    second[...] = array[:, second.shape[1] :]
    squares = column_squares(array[...])
    inverse = inverse_norm(squares)
    scale[...] = inverse
    product = transposed_product(array[...], array[...])
    columns = as_columns(inverse, LANES)
    columns = jnp.concatenate([columns] * (product.shape[1] // LANES), axis=1)
    values[...] = product * columns * inverse
    write_slabs(place[0], values, slabs)
    code = coded(squares * inverse)
    for slab in slabs:
        slab[-CODE_ROWS:] = code


def scaled_product(left, right, left_scale):
    right_scale = inverse_norm(column_squares(right))
    product = transposed_product(left, right)
    columns = as_columns(left_scale, LANES)
    columns = jnp.concatenate([columns] * (product.shape[1] // LANES), axis=1)
    return product * columns * right_scale


def first_kernel(groups, place, left, right, left_scale, corner, *rest):
    slabs, values = rest[:groups], rest[groups]
    half = right.shape[1]
    product = scaled_product(left[...], right[...], left_scale[...])
    values[:half] = mirrored_lower(product[:half])
    values[half:] = product[half:]
    corner[...] = product[half:]
    write_slabs(place[0], values, slabs)


def second_kernel(groups, place, left, right, left_scale, corner, *rest):
    slabs, values = rest[:groups], rest[groups]
    half = right.shape[1]
    values[:half] = corner[...].T
    values[half:] = mirrored_lower(scaled_product(left[...], right[...], left_scale[...]))
    write_slabs(place[0], values, slabs)


def shares_kernel(groups, starts, *rest):
    terms, (rows, columns) = rest[:groups], rest[groups:]
    norms = [decoded(term[...]) for term in terms]
    sumsq = functools.reduce(jnp.add, [norm * norm for norm in norms])
    inverse = inverse_norm(sumsq)
    rows[...] = jnp.zeros(rows.shape, jnp.float32)
    for by, norm in enumerate(norms):
        rows[by : by + 1, :] = norm * inverse
    rows[groups : groups + 1, : starts.shape[1]] = starts[...].astype(jnp.float32)
    rows[groups + 1 : groups + 2, :] = sumsq * lax.rsqrt(sumsq) * inverse
    fill = jnp.zeros((LANES - rows.shape[0], rows.shape[1]), jnp.float32)
    columns[...] = jnp.concatenate([rows[...], fill], axis=0).T


def per_device(genotypes, annotations, window_start, window_end):
    stripe = genotypes.shape[1]
    half = stripe // 2
    groups = lax.axis_size("ind")
    count_all = float(genotypes.shape[0] * groups)
    sub_rows = stripe // groups
    place = lax.axis_index("ind").astype(jnp.int32)
    place = jnp.stack([place, lax.axis_index("snp").astype(jnp.int32) * stripe])
    scalar = pl.BlockSpec(memory_space=pltpu.SMEM)

    def shape(*dims, dtype=jnp.float32):
        return jax.ShapeDtypeStruct(dims, dtype)

    def slab_shapes(rows, columns):
        return (shape(rows, columns, dtype=jnp.int16),) * groups

    above_first = shifted(genotypes[:, :half], "snp", -1)
    second, scale, *own_slabs = kernel_call(
        functools.partial(own_kernel, groups),
        (
            shape(genotypes.shape[0], half, dtype=genotypes.dtype),
            shape(1, stripe),
            *slab_shapes(sub_rows + CODE_ROWS, stripe),
        ),
        (place, genotypes),
        [scalar, None],
        scratch=[pltpu.VMEM((stripe, stripe), jnp.float32)],
        cost=COST_O,
    )
    own_terms = exchanged(own_slabs, "ind")
    above_second = shifted(second, "snp", -1)

    above_first = after(above_first, own_terms[1])
    corner, *first_slabs = kernel_call(
        functools.partial(first_kernel, groups),
        (shape(half, half), *slab_shapes(sub_rows, half)),
        (place, genotypes, above_first, scale),
        [scalar, None, None, None],
        scratch=[pltpu.VMEM((stripe, half), jnp.float32)],
        cost=COST_F,
    )
    first_terms = exchanged(first_slabs, "ind")
    annot_above = shifted(after(annotations, own_terms[1]), "snp", -1)

    above_second = after(above_second, first_terms[1])
    second_slabs = kernel_call(
        functools.partial(second_kernel, groups),
        slab_shapes(sub_rows, half),
        (place, genotypes, above_second, scale, corner),
        [
            scalar,
            pl.BlockSpec((genotypes.shape[0], half), lambda i: (0, 1)),
            None,
            pl.BlockSpec((1, half), lambda i: (0, 1)),
            None,
        ],
        grid=(1,),
        scratch=[pltpu.VMEM((stripe, half), jnp.float32)],
        cost=COST_S,
    )
    second_terms = exchanged(second_slabs, "ind")

    code = pl.BlockSpec((CODE_ROWS, stripe), lambda i: (sub_rows // CODE_ROWS, 0))
    info_rows = -(-(groups + 2) // 8) * 8
    shares, share_columns = kernel_call(
        functools.partial(shares_kernel, groups),
        (shape(info_rows, stripe), shape(stripe, LANES)),
        (window_start[None], *(after(term, corner) for term in own_terms)),
        [None] + [code] * groups,
        grid=(1,),
        cost=COST_H,
    )
    above = shifted(shares, "snp", -1)

    def rows_of(array):
        return lax.dynamic_slice_in_dim(array, place[0] * sub_rows, sub_rows, 0)

    ids = jnp.arange(stripe, dtype=jnp.int32)[None, :]
    row_ids = place[0] * sub_rows + jnp.arange(sub_rows, dtype=jnp.int32)[:, None]
    lower = row_ids >= ids
    own_ids = place[1] + ids
    here = rows_of(share_columns)
    next_here = rows_of(above.T)

    def column(array, by):
        return array[:, by : by + 1]

    def row(array, by):
        return array[by : by + 1, :]

    own_corr = sum(
        term[:sub_rows].astype(jnp.float32) * column(here, by) * row(shares, by)
        for by, term in enumerate(own_terms)
    )
    own_corr = own_corr * (1.0 / UNIT) * column(here, groups + 1)
    inside = (own_ids >= window_start[:, None]) & (own_ids < window_end[:, None])
    own_weights = jnp.where(inside, adjusted(own_corr, count_all), 0.0).astype(jnp.bfloat16)
    score = jnp.dot(own_weights, annotations, preferred_element_type=jnp.float32)

    cross_corr = 0.0
    for by in range(groups):
        term = jnp.concatenate([first_terms[by], second_terms[by]], axis=1).astype(jnp.float32)
        below = column(here, by) * row(above, by)
        cross_corr += term * jnp.where(lower, below, column(next_here, by) * row(shares, by))
    cross_weights = adjusted(cross_corr * (1.0 / UNIT), count_all).astype(jnp.bfloat16)
    start_above = above[groups, :sub_rows].astype(jnp.int32)
    inside = (own_ids >= start_above[:, None]) & (ids >= row_ids)
    mirrored = jnp.where(inside, cross_weights, 0)
    mirrored = jnp.dot(mirrored, annotations, preferred_element_type=jnp.float32)
    mirrored = shifted(mirrored.astype(jnp.bfloat16), "snp", 1)

    inside = (own_ids + stripe < window_end[:, None]) & lower
    above_weights = jnp.where(inside, cross_weights, 0)
    score += jnp.dot(above_weights, annot_above, preferred_element_type=jnp.float32)
    return score + mirrored.astype(jnp.float32)


def solution(mesh):
    in_specs = (P("ind", "snp"), P("snp", None), P(("snp", "ind")), P(("snp", "ind")))
    out_specs = P(("snp", "ind"), None)
    return jax.shard_map(
        per_device, mesh=mesh, in_specs=in_specs, out_specs=out_specs, check_vma=False
    )
```

time: 131 us -> 52.8 us (0.40)
  waiting for transfers between devices: 81.4 us -> 14.7 us
  starting transfers between devices: 7.49 us -> 24.4 us
  between operations: 13.5 us -> 0.22 us
  blocking collectives: 12.1 us -> 0 us
  Pallas kernels: 0 us -> 7.19 us
  other arithmetic: 5.55 us -> 0.77 us
  matrix products: 5.98 us -> 2.71 us
  local copies, waits for them, and re-layouts: 4.26 us -> 2.46 us
    reduce_scatter x2 -> x0, waiting for transfers between devices: 54.1 us -> none  [the longest x1 30.2 us: per_device(): lax.psum_scatter(transposed_product(genotypes, wide_geno), 'ind', scatter...]
    ppermute x3 -> x5, waiting for transfers between devices: 27.2 us -> 5.86 us  [shifted(): return lax.ppermute(array, axis, pairs)]
    ppermute x0 -> x9, starting transfers between devices: none -> 14 us  [exchanged(): lax.ppermute(slabs[by], axis, [(i, i ^ by) for i in range(devices)])]
    psum x1 -> x0, blocking collectives: 12.1 us -> none  [per_device(): col_sumsq = lax.psum(column_squares(wide_geno), 'ind')]
    ppermute x0 -> x9, waiting for transfers between devices: none -> 8.81 us  [exchanged(): lax.ppermute(slabs[by], axis, [(i, i ^ by) for i in range(devices)])]
    pallas_call x0 -> x4, Pallas kernels: none -> 7.19 us  [kernel_call(): pl.pallas_call(kernel, out_shape=out_shape, in_specs=[spec or whole for s...]
    unnamed x11 -> x8, local copies, waits for them, and re-layouts: 3.86 us -> 0.02 us
    dot_general x3, matrix products: 5.98 us -> 2.71 us  [the longest x1 1.45 us: per_device(): jnp.dot(own_weights, annotations, preferred_element_type=jnp.float32)]
  transfers between devices with their start and end apart: 5 -> 14, of which waited for: 4 -> 5; matrix products, arithmetic and copies ran while one was open for 5% -> 5% of each run, Pallas kernels for 0% -> 14%
where the time goes in v4:
time: 52.8 us; the launch traced here: 52.4 us
  starting transfers between devices  24.4 us (46%)
  waiting for transfers between devices  14.7 us (28%)
  Pallas kernels  7.19 us (14%)
  matrix products  2.71 us (5%)
  local copies, waits for them, and re-layouts  2.46 us (5%)
  other arithmetic  0.77 us (1%)
    ppermute x9, starting transfers between devices, exchanged(): lax.ppermute(slabs[by], axis, [(i, i ^ by) for i in range(devices)])  14 us
    ppermute x5, starting transfers between devices, shifted(): return lax.ppermute(array, axis, pairs)  10.4 us
    ppermute x9, waiting for transfers between devices, exchanged(): lax.ppermute(slabs[by], axis, [(i, i ^ by) for i in range(devices)])  8.81 us
    pallas_call x4, Pallas kernels, kernel_call(): pl.pallas_call(kernel, out_shape=out_shape, in_specs=[spec or whole for s...  7.19 us
    ppermute x5, waiting for transfers between devices, shifted(): return lax.ppermute(array, axis, pairs)  5.86 us
    slice x1, local copies, waits for them, and re-layouts, per_device(): above_first = shifted(genotypes[:, :half], 'snp', -1)  2.41 us
    dot_general x1, matrix products, per_device(): jnp.dot(own_weights, annotations, preferred_element_type=jnp.float32)  1.45 us
  transfers between devices with their start and end apart: 14, of which 5 were waited for; matrix products, arithmetic and copies ran while one was open for 5% of the time, Pallas kernels for 14%

profile of v4, /device:TPU:4, one launch (start us, length us, event | category | flops | bytes accessed | tf_op | source)
XLA Modules:
  0.0 52.4 jit_solution(6642229354712163421)
XLA Ops:
  0.0 2.4 %slice.78 = bf16[2048,256]{1,0:T(8,128)(2,1)} slice(bf16[2048,512]{1,0:T(8,128)(2,1)} %left.3), slice={[0:2048], [0:256]} | slice | bytes 2097152 | tf_op jit(solution)/shard_map/slice | solution.py:178
  2.4 2.8 %collective-permute-start = (bf16[2048,256]{1,0:T(8,128)(2,1)}, bf16[2048,256]{1,0:T(8,128)(2,1)}, u32[]{:S(2)}, u32[]{:S(2)}) collective-permute-start(bf16[2048,256]{1,0:T(8,128)(2,1)} %slice.78), channel_id=1, source_target_pairs={{4,0},{8,4},{12,8},{16,12},{20,16},{24,20},{28,24},{5,1},{9,5},{13... | collective-permute-start | bytes 3145736 | tf_op jit(solution)/shard_map/ppermute | solution.py:19
  5.3 3.0 %shard_map.46 = (bf16[2048,256]{1,0:T(8,128)(2,1)}, f32[1,512]{1,0:T(1,128)S(1)}, s16[144,512]{1,0:T(8,128)(2,1)S(1)}, s16[144,512]{1,0:T(8,128)(2,1)}, s16[144,...) custom-call(s32[2]{0:T(128)S(1)} %pad_add_fusion.place, bf16[2048,512]{1,0:T(8,128)(2,1)S(1)} %copy-done), custom_call_target="tpu_custom_call" | custom-call | bytes 9250000 | tf_op jit(solution)/shard_map/pallas_call | solution.py:88
  8.3 1.6 %collective-permute-start.1 = (s16[144,512]{1,0:T(8,128)(2,1)}, s16[144,512]{1,0:T(8,128)(2,1)S(1)}, u32[]{:S(2)}, u32[]{:S(2)}) collective-permute-start(s16[144,512]{1,0:T(8,128)(2,1)} %get-tuple-element.30), channel_id=1, source_target_pairs={{0,1},{1,0},{2,3},{3,2},{4,5},{5,4},{6,7},{7,6},{8,9},{9,8},{10,11... | collective-permute-start | bytes 442376 | tf_op jit(solution)/shard_map/ppermute | solution.py:29
  9.9 2.6 %collective-permute-start.2 = (s16[144,512]{1,0:T(8,128)(2,1)}, s16[144,512]{1,0:T(8,128)(2,1)}, u32[]{:S(2)}, u32[]{:S(2)}) collective-permute-start(s16[144,512]{1,0:T(8,128)(2,1)} %get-tuple-element.36), channel_id=1, source_target_pairs={{0,2},{1,3},{2,0},{3,1},{4,6},{5,7},{6,4},{7,5},{8,10},{9,11},{10,... | collective-permute-start | bytes 442376 | tf_op jit(solution)/shard_map/ppermute | solution.py:29
  12.7 1.9 %collective-permute-start.4 = (bf16[2048,256]{1,0:T(8,128)(2,1)}, bf16[2048,256]{1,0:T(8,128)(2,1)S(1)}, u32[]{:S(2)}, u32[]{:S(2)}) collective-permute-start(bf16[2048,256]{1,0:T(8,128)(2,1)} %get-tuple-element.43), channel_id=1, source_target_pairs={{4,0},{8,4},{12,8},{16,12},{20,16},{24,20},{28,24},{5,1},{9,5},{13... | collective-permute-start | bytes 3145736 | tf_op jit(solution)/shard_map/ppermute | solution.py:19
  14.6 1.1 %collective-permute-done.1.rest_1_ = s16[144,512]{1,0:T(8,128)(2,1)S(1)} collective-permute-done((s16[144,512]{1,0:T(8,128)(2,1)}, s16[144,512]{1,0:T(8,128)(2,1)S(1)}, u32[]{:S(2)}, u32[]{:S(2)}) %collective-permute-start.1) | collective-permute-done | bytes 147488 | tf_op jit(solution)/shard_map/ppermute | solution.py:29
  15.7 2.1 %collective-permute-done.right = bf16[2048,256]{1,0:T(8,128)(2,1)} collective-permute-done((bf16[2048,256]{1,0:T(8,128)(2,1)}, bf16[2048,256]{1,0:T(8,128)(2,1)}, u32[]{:S(2)}, u32[]{:S(2)}) %collective-permute-start) | collective-permute-done | bytes 1048608 | tf_op jit(solution)/shard_map/ppermute | solution.py:19
  17.8 2.1 %shard_map.47 = (f32[256,256]{1,0:T(8,128)S(1)}, s16[128,256]{1,0:T(8,128)(2,1)S(1)}, s16[128,256]{1,0:T(8,128)(2,1)S(1)}, s16[128,256]{1,0:T(8,128)(2,1)S(1)}, s16[128,256]{1,0:T(8,128)(2,1)S(1)}) custom-call(s32[2]{0:T(128)S(1)} %pad_add_fusion.place, bf16[2048,512]{1,0:T(8,128)(2,1)S(1)} %copy-done, bf16[2048,256]{1,0:T(8,128)(2,1)} %collective-permute-done.right, ...), custom_call_target="tpu_custom_call" | custom-call | bytes 9250000 | tf_op jit(solution)/shard_map/pallas_call | solution.py:88
  19.9 4.3 %collective-permute-done.2.rest_2_ = s16[144,512]{1,0:T(8,128)(2,1)} collective-permute-done((s16[144,512]{1,0:T(8,128)(2,1)}, s16[144,512]{1,0:T(8,128)(2,1)}, u32[]{:S(2)}, u32[]{:S(2)}) %collective-permute-start.2) | collective-permute-done | bytes 147488 | tf_op jit(solution)/shard_map/ppermute | solution.py:29
  25.1 1.9 %collective-permute-start.6 = (f32[8,512]{1,0:T(8,128)S(1)}, f32[8,512]{1,0:T(8,128)S(1)}, u32[]{:S(2)}, u32[]{:S(2)}) collective-permute-start(f32[8,512]{1,0:T(8,128)S(1)} %get-tuple-element.41), channel_id=1, source_target_pairs={{4,0},{8,4},{12,8},{16,12},{20,16},{24,20},{28,24},{5,1},{9,5},{13... | collective-permute-start | bytes 49160 | tf_op jit(solution)/shard_map/ppermute | solution.py:19
  27.1 2.6 %collective-permute-start.5 = (s16[128,256]{1,0:T(8,128)(2,1)S(1)}, s16[128,256]{1,0:T(8,128)(2,1)S(1)}, u32[]{:S(2)}, u32[]{:S(2)}) collective-permute-start(s16[128,256]{1,0:T(8,128)(2,1)S(1)} %get-tuple-element.44), channel_id=1, source_target_pairs={{0,1},{1,0},{2,3},{3,2},{4,5},{5,4},{6,7},{7,6},{8,9},{9,8},{10,11... | collective-permute-start | bytes 196616 | tf_op jit(solution)/shard_map/ppermute | solution.py:29
  29.7 1.1 %collective-permute-start.8 = (s16[128,256]{1,0:T(8,128)(2,1)S(1)}, s16[128,256]{1,0:T(8,128)(2,1)S(1)}, u32[]{:S(2)}, u32[]{:S(2)}) collective-permute-start(s16[128,256]{1,0:T(8,128)(2,1)S(1)} %get-tuple-element.48), channel_id=1, source_target_pairs={{0,2},{1,3},{2,0},{3,1},{4,6},{5,7},{6,4},{7,5},{8,10},{9,11},{10,... | collective-permute-start | bytes 196616 | tf_op jit(solution)/shard_map/ppermute | solution.py:29
  30.8 1.4 %collective-permute-start.10 = (s16[128,256]{1,0:T(8,128)(2,1)S(1)}, s16[128,256]{1,0:T(8,128)(2,1)S(1)}, u32[]{:S(2)}, u32[]{:S(2)}) collective-permute-start(s16[128,256]{1,0:T(8,128)(2,1)S(1)} %get-tuple-element.50), channel_id=1, source_target_pairs={{0,3},{1,2},{2,1},{3,0},{4,7},{5,6},{6,5},{7,4},{8,11},{9,10},{10,... | collective-permute-start | bytes 196616 | tf_op jit(solution)/shard_map/ppermute | solution.py:29
  32.5 1.2 %shard_map.49 = (s16[128,256]{1,0:T(8,128)(2,1)S(1)}, s16[128,256]{1,0:T(8,128)(2,1)S(1)}, s16[128,256]{1,0:T(8,128)(2,1)S(1)}, s16[128,256]{1,0:T(8,128)(2,1)S(1)}) custom-call(s32[2]{0:T(128)S(1)} %pad_add_fusion.place, bf16[2048,512]{1,0:T(8,128)(2,1)S(1)} %copy-done, bf16[2048,256]{1,0:T(8,128)(2,1)S(1)} %collective-permute-done.4.right, ...), custom_call_target="tpu_custom_call" | custom-call | bytes 7400000 | tf_op jit(solution)/shard_map/pallas_call | solution.py:88
  33.7 2.0 %collective-permute-start.7 = (s16[128,256]{1,0:T(8,128)(2,1)S(1)}, s16[128,256]{1,0:T(8,128)(2,1)S(1)}, u32[]{:S(2)}, u32[]{:S(2)}) collective-permute-start(s16[128,256]{1,0:T(8,128)(2,1)S(1)} %get-tuple-element.47), channel_id=1, source_target_pairs={{0,1},{1,0},{2,3},{3,2},{4,5},{5,4},{6,7},{7,6},{8,9},{9,8},{10,11... | collective-permute-start | bytes 196616 | tf_op jit(solution)/shard_map/ppermute | solution.py:29
  35.7 1.1 %collective-permute-start.9 = (s16[128,256]{1,0:T(8,128)(2,1)S(1)}, s16[128,256]{1,0:T(8,128)(2,1)S(1)}, u32[]{:S(2)}, u32[]{:S(2)}) collective-permute-start(s16[128,256]{1,0:T(8,128)(2,1)S(1)} %get-tuple-element.49), channel_id=1, source_target_pairs={{0,2},{1,3},{2,0},{3,1},{4,6},{5,7},{6,4},{7,5},{8,10},{9,11},{10,... | collective-permute-start | bytes 196616 | tf_op jit(solution)/shard_map/ppermute | solution.py:29
  36.8 1.4 %collective-permute-start.11 = (s16[128,256]{1,0:T(8,128)(2,1)S(1)}, s16[128,256]{1,0:T(8,128)(2,1)S(1)}, u32[]{:S(2)}, u32[]{:S(2)}) collective-permute-start(s16[128,256]{1,0:T(8,128)(2,1)S(1)} %get-tuple-element.51), channel_id=1, source_target_pairs={{0,3},{1,2},{2,1},{3,0},{4,7},{5,6},{6,5},{7,4},{8,11},{9,10},{10,... | collective-permute-start | bytes 196616 | tf_op jit(solution)/shard_map/ppermute | solution.py:29
  38.2 1.9 %collective-permute-start.12 = (bf16[512,512]{1,0:T(8,128)(2,1)S(1)}, bf16[512,512]{1,0:T(8,128)(2,1)S(1)}, u32[]{:S(2)}, u32[]{:S(2)}) collective-permute-start(bf16[512,512]{1,0:T(8,128)(2,1)S(1)} %copy-done.3), channel_id=1, source_target_pairs={{4,0},{8,4},{12,8},{16,12},{20,16},{24,20},{28,24},{5,1},{9,5},{13... | collective-permute-start | bytes 1572872 | tf_op jit(solution)/shard_map/ppermute | solution.py:19
  40.1 3.4 %collective-permute-done.9 = s16[128,256]{1,0:T(8,128)(2,1)S(1)} collective-permute-done((s16[128,256]{1,0:T(8,128)(2,1)S(1)}, s16[128,256]{1,0:T(8,128)(2,1)S(1)}, u32[]{:S(2)}, u32[]{:S(2)}) %collective-permute-start.9) | collective-permute-done | bytes 65568 | tf_op jit(solution)/shard_map/ppermute | solution.py:29
  44.3 1.9 %collective-permute-start.13 = (bf16[128,512]{1,0:T(8,128)(2,1)S(1)}, bf16[128,512]{1,0:T(8,128)(2,1)S(1)}, u32[]{:S(2)}, u32[]{:S(2)}) collective-permute-start(bf16[128,512]{1,0:T(8,128)(2,1)S(1)} %convolution_convert_fusion), channel_id=1, source_target_pairs={{0,4},{4,8},{8,12},{12,16},{16,20},{20,24},{24,28},{1,5},{5,9},{9,... | collective-permute-start | bytes 393224 | tf_op jit(solution)/shard_map/ppermute | solution.py:19
  46.2 1.5 %fusion.13 = f32[128,512]{1,0:T(8,128)S(1)} fusion(bf16[512,512]{1,0:T(8,128)(2,1)S(1)} %copy-done.3, s16[144,512]{1,0:T(8,128)(2,1)} %collective-permute-done.3.rest_3_, s16[144,512]{1,0:T(8,128)(2,1)} %collective-permute-done.2.rest_2_, s16[144,512]{1,0:T(8,128)(2,1)S(1)} %collective-permute-done.1.rest_1_, f32[128]{0:T(128)S(1)} %get-tuple-element.57, ...), kind=kOutput, calls=%fused_computation.17 | convolution fusion | flops 68747264 | bytes 1324544 | tf_op jit(solution)/shard_map/dot_general | solution.py:259
  47.7 3.8 %collective-permute-done.13 = bf16[128,512]{1,0:T(8,128)(2,1)S(1)} collective-permute-done((bf16[128,512]{1,0:T(8,128)(2,1)S(1)}, bf16[128,512]{1,0:T(8,128)(2,1)S(1)}, u32[]{:S(2)}, u32[]{:S(2)}) %collective-permute-start.13) | collective-permute-done | bytes 131104 | tf_op jit(solution)/shard_map/ppermute | solution.py:19
  51.4 1.0 %fusion = f32[128,512]{1,0:T(8,128)} fusion(f32[128,512]{1,0:T(8,128)S(1)} %fusion.13, bf16[512,512]{1,0:T(8,128)(2,1)S(1)} %collective-permute-done.12, bf16[128,512]{1,0:T(8,128)(2,1)S(1)} %collective-permute-done.13, bf16[128,512]{1,0:T(8,128)(2,1)S(1)} %subtract_convert_fusion, s32[128]{0:T(128)S(1)} %iota_add_fusion.1, s32[512]{0:T(512)S(1)} %broadcast_add_fusion, ...), kind=kOutput, calls=%fused_computation.1 | convolution fusion | flops 67567616 | bytes 1313792 | tf_op jit(solution)/shard_map/dot_general | solution.py:275
  (31 shorter events, 2.3 us)
Async XLA Ops:
  0.0 5.3 %copy-start = (bf16[2048,512]{1,0:T(8,128)(2,1)S(1)}, bf16[2048,512]{1,0:T(8,128)(2,1)}, u32[]{:S(2)}) copy-start(bf16[2048,512]{1,0:T(8,128)(2,1)} %left.3) | copy-start | bytes 6291460
  2.4 15.4 %collective-permute-start = (bf16[2048,256]{1,0:T(8,128)(2,1)}, bf16[2048,256]{1,0:T(8,128)(2,1)}, u32[]{:S(2)}, u32[]{:S(2)}) collective-permute-start(bf16[2048,256]{1,0:T(8,128)(2,1)} %slice.78), channel_id=1, source_target_pairs={{4,0},{8,4},{12,8},{16,12},{20,16},{24,20},{28,24},{5,1},{9,5},{13... | collective-permute-start | bytes 3145736 | tf_op jit(solution)/shard_map/ppermute | solution.py:19
  8.3 15.9 %copy-start.1 = (s32[128]{0:T(128)S(1)}, s32[128]{0:T(128)}, u32[]{:S(2)}) copy-start(s32[128]{0:T(128)} %param.6) | copy-start | bytes 1540
  8.3 7.4 %collective-permute-start.1 = (s16[144,512]{1,0:T(8,128)(2,1)}, s16[144,512]{1,0:T(8,128)(2,1)S(1)}, u32[]{:S(2)}, u32[]{:S(2)}) collective-permute-start(s16[144,512]{1,0:T(8,128)(2,1)} %get-tuple-element.30), channel_id=1, source_target_pairs={{0,1},{1,0},{2,3},{3,2},{4,5},{5,4},{6,7},{7,6},{8,9},{9,8},{10,11... | collective-permute-start | bytes 442376 | tf_op jit(solution)/shard_map/ppermute | solution.py:29
  9.9 14.3 %collective-permute-start.2 = (s16[144,512]{1,0:T(8,128)(2,1)}, s16[144,512]{1,0:T(8,128)(2,1)}, u32[]{:S(2)}, u32[]{:S(2)}) collective-permute-start(s16[144,512]{1,0:T(8,128)(2,1)} %get-tuple-element.36), channel_id=1, source_target_pairs={{0,2},{1,3},{2,0},{3,1},{4,6},{5,7},{6,4},{7,5},{8,10},{9,11},{10,... | collective-permute-start | bytes 442376 | tf_op jit(solution)/shard_map/ppermute | solution.py:29
  12.5 11.7 %collective-permute-start.3 = (s16[144,512]{1,0:T(8,128)(2,1)}, s16[144,512]{1,0:T(8,128)(2,1)}, u32[]{:S(2)}, u32[]{:S(2)}) collective-permute-start(s16[144,512]{1,0:T(8,128)(2,1)} %get-tuple-element.38), channel_id=1, source_target_pairs={{0,3},{1,2},{2,1},{3,0},{4,7},{5,6},{6,5},{7,4},{8,11},{9,10},{10,... | collective-permute-start | bytes 442376 | tf_op jit(solution)/shard_map/ppermute | solution.py:29
  12.7 19.8 %collective-permute-start.4 = (bf16[2048,256]{1,0:T(8,128)(2,1)}, bf16[2048,256]{1,0:T(8,128)(2,1)S(1)}, u32[]{:S(2)}, u32[]{:S(2)}) collective-permute-start(bf16[2048,256]{1,0:T(8,128)(2,1)} %get-tuple-element.43), channel_id=1, source_target_pairs={{4,0},{8,4},{12,8},{16,12},{20,16},{24,20},{28,24},{5,1},{9,5},{13... | collective-permute-start | bytes 3145736 | tf_op jit(solution)/shard_map/ppermute | solution.py:19
  24.1 14.0 %copy-start.3 = (bf16[512,512]{1,0:T(8,128)(2,1)S(1)}, bf16[512,512]{1,0:T(8,128)(2,1)}, u32[]{:S(2)}) copy-start(bf16[512,512]{1,0:T(8,128)(2,1)} %param.5) | copy-start | bytes 1572868
  25.1 7.3 %collective-permute-start.6 = (f32[8,512]{1,0:T(8,128)S(1)}, f32[8,512]{1,0:T(8,128)S(1)}, u32[]{:S(2)}, u32[]{:S(2)}) collective-permute-start(f32[8,512]{1,0:T(8,128)S(1)} %get-tuple-element.41), channel_id=1, source_target_pairs={{4,0},{8,4},{12,8},{16,12},{20,16},{24,20},{28,24},{5,1},{9,5},{13... | collective-permute-start | bytes 49160 | tf_op jit(solution)/shard_map/ppermute | solution.py:19
  27.1 5.5 %collective-permute-start.5 = (s16[128,256]{1,0:T(8,128)(2,1)S(1)}, s16[128,256]{1,0:T(8,128)(2,1)S(1)}, u32[]{:S(2)}, u32[]{:S(2)}) collective-permute-start(s16[128,256]{1,0:T(8,128)(2,1)S(1)} %get-tuple-element.44), channel_id=1, source_target_pairs={{0,1},{1,0},{2,3},{3,2},{4,5},{5,4},{6,7},{7,6},{8,9},{9,8},{10,11... | collective-permute-start | bytes 196616 | tf_op jit(solution)/shard_map/ppermute | solution.py:29
  29.7 8.5 %collective-permute-start.8 = (s16[128,256]{1,0:T(8,128)(2,1)S(1)}, s16[128,256]{1,0:T(8,128)(2,1)S(1)}, u32[]{:S(2)}, u32[]{:S(2)}) collective-permute-start(s16[128,256]{1,0:T(8,128)(2,1)S(1)} %get-tuple-element.48), channel_id=1, source_target_pairs={{0,2},{1,3},{2,0},{3,1},{4,6},{5,7},{6,4},{7,5},{8,10},{9,11},{10,... | collective-permute-start | bytes 196616 | tf_op jit(solution)/shard_map/ppermute | solution.py:29
  30.8 9.3 %collective-permute-start.10 = (s16[128,256]{1,0:T(8,128)(2,1)S(1)}, s16[128,256]{1,0:T(8,128)(2,1)S(1)}, u32[]{:S(2)}, u32[]{:S(2)}) collective-permute-start(s16[128,256]{1,0:T(8,128)(2,1)S(1)} %get-tuple-element.50), channel_id=1, source_target_pairs={{0,3},{1,2},{2,1},{3,0},{4,7},{5,6},{6,5},{7,4},{8,11},{9,10},{10,... | collective-permute-start | bytes 196616 | tf_op jit(solution)/shard_map/ppermute | solution.py:29
  32.5 13.7 %copy-start.2 = (s32[128]{0:T(128)S(1)}, s32[128]{0:T(128)}, u32[]{:S(2)}) copy-start(s32[128]{0:T(128)} %param.7) | copy-start | bytes 1540
  33.7 6.4 %collective-permute-start.7 = (s16[128,256]{1,0:T(8,128)(2,1)S(1)}, s16[128,256]{1,0:T(8,128)(2,1)S(1)}, u32[]{:S(2)}, u32[]{:S(2)}) collective-permute-start(s16[128,256]{1,0:T(8,128)(2,1)S(1)} %get-tuple-element.47), channel_id=1, source_target_pairs={{0,1},{1,0},{2,3},{3,2},{4,5},{5,4},{6,7},{7,6},{8,9},{9,8},{10,11... | collective-permute-start | bytes 196616 | tf_op jit(solution)/shard_map/ppermute | solution.py:29
  35.7 7.9 %collective-permute-start.9 = (s16[128,256]{1,0:T(8,128)(2,1)S(1)}, s16[128,256]{1,0:T(8,128)(2,1)S(1)}, u32[]{:S(2)}, u32[]{:S(2)}) collective-permute-start(s16[128,256]{1,0:T(8,128)(2,1)S(1)} %get-tuple-element.49), channel_id=1, source_target_pairs={{0,2},{1,3},{2,0},{3,1},{4,6},{5,7},{6,4},{7,5},{8,10},{9,11},{10,... | collective-permute-start | bytes 196616 | tf_op jit(solution)/shard_map/ppermute | solution.py:29
  36.8 6.8 %collective-permute-start.11 = (s16[128,256]{1,0:T(8,128)(2,1)S(1)}, s16[128,256]{1,0:T(8,128)(2,1)S(1)}, u32[]{:S(2)}, u32[]{:S(2)}) collective-permute-start(s16[128,256]{1,0:T(8,128)(2,1)S(1)} %get-tuple-element.51), channel_id=1, source_target_pairs={{0,3},{1,2},{2,1},{3,0},{4,7},{5,6},{6,5},{7,4},{8,11},{9,10},{10,... | collective-permute-start | bytes 196616 | tf_op jit(solution)/shard_map/ppermute | solution.py:29
  38.2 9.5 %collective-permute-start.12 = (bf16[512,512]{1,0:T(8,128)(2,1)S(1)}, bf16[512,512]{1,0:T(8,128)(2,1)S(1)}, u32[]{:S(2)}, u32[]{:S(2)}) collective-permute-start(bf16[512,512]{1,0:T(8,128)(2,1)S(1)} %copy-done.3), channel_id=1, source_target_pairs={{4,0},{8,4},{12,8},{16,12},{20,16},{24,20},{28,24},{5,1},{9,5},{13... | collective-permute-start | bytes 1572872 | tf_op jit(solution)/shard_map/ppermute | solution.py:19
  44.3 7.2 %collective-permute-start.13 = (bf16[128,512]{1,0:T(8,128)(2,1)S(1)}, bf16[128,512]{1,0:T(8,128)(2,1)S(1)}, u32[]{:S(2)}, u32[]{:S(2)}) collective-permute-start(bf16[128,512]{1,0:T(8,128)(2,1)S(1)} %convolution_convert_fusion), channel_id=1, source_target_pairs={{0,4},{4,8},{8,12},{12,16},{16,20},{20,24},{24,28},{1,5},{5,9},{9,... | collective-permute-start | bytes 393224 | tf_op jit(solution)/shard_map/ppermute | solution.py:19

commit v5 on v4

--- a/solution.py
+++ b/solution.py
@@ -25,10 +25,11 @@
 
 def exchanged(slabs, axis):
     devices = lax.axis_size(axis)
-    return [slabs[0]] + [
-        lax.ppermute(slabs[by], axis, [(i, i ^ by) for i in range(devices)])
-        for by in range(1, devices)
-    ]
+    terms = [slabs[0]] * devices
+    for by in range(1, devices):
+        pairs = [(i, (i + by) % devices) for i in range(devices)]
+        terms[by] = lax.ppermute(slabs[by], axis, pairs)
+    return terms
 
 
 def column_squares(block):
@@ -99,7 +100,7 @@
 def write_slabs(place, values, slabs):
     rows = values.shape[0] // len(slabs)
     for by, slab in enumerate(slabs):
-        first = (place ^ by) * rows
+        first = lax.rem(place + by, len(slabs)) * rows
         slab[:rows] = to_fixed(values[pl.ds(pl.multiple_of(first, 16), rows), :])
 
 
@@ -189,9 +190,8 @@
         cost=COST_O,
     )
     own_terms = exchanged(own_slabs, "ind")
-    above_second = shifted(second, "snp", -1)
-
-    above_first = after(above_first, own_terms[1])
+    above_second = shifted(after(second, scale), "snp", -1)
+
     corner, *first_slabs = kernel_call(
         functools.partial(first_kernel, groups),
         (shape(half, half), *slab_shapes(sub_rows, half)),
@@ -200,8 +200,20 @@
         scratch=[pltpu.VMEM((stripe, half), jnp.float32)],
         cost=COST_F,
     )
-    first_terms = exchanged(first_slabs, "ind")
+    first_terms = exchanged([after(slab, own_terms[2]) for slab in first_slabs], "ind")
     annot_above = shifted(after(annotations, own_terms[1]), "snp", -1)
+
+    code = pl.BlockSpec((CODE_ROWS, stripe), lambda i: (sub_rows // CODE_ROWS, 0))
+    info_rows = -(-(groups + 2) // 8) * 8
+    shares, share_columns = kernel_call(
+        functools.partial(shares_kernel, groups),
+        (shape(info_rows, stripe), shape(stripe, LANES)),
+        (window_start[None], *(after(term, corner) for term in own_terms)),
+        [None] + [code] * groups,
+        grid=(1,),
+        cost=COST_H,
+    )
+    above = shifted(shares, "snp", -1)
 
     above_second = after(above_second, first_terms[1])
     second_slabs = kernel_call(
@@ -221,18 +233,6 @@
     )
     second_terms = exchanged(second_slabs, "ind")
 
-    code = pl.BlockSpec((CODE_ROWS, stripe), lambda i: (sub_rows // CODE_ROWS, 0))
-    info_rows = -(-(groups + 2) // 8) * 8
-    shares, share_columns = kernel_call(
-        functools.partial(shares_kernel, groups),
-        (shape(info_rows, stripe), shape(stripe, LANES)),
-        (window_start[None], *(after(term, corner) for term in own_terms)),
-        [None] + [code] * groups,
-        grid=(1,),
-        cost=COST_H,
-    )
-    above = shifted(shares, "snp", -1)
-
     def rows_of(array):
         return lax.dynamic_slice_in_dim(array, place[0] * sub_rows, sub_rows, 0)
 

time: 52.8 us -> 51.5 us (0.975)
  waiting for transfers between devices: 14.7 us -> 10.2 us
  starting transfers between devices: 24.4 us -> 27.4 us
    ppermute x9, waiting for transfers between devices: 8.81 us -> 5.85 us  [exchanged(): terms[by] = lax.ppermute(slabs[by], axis, pairs)]
    ppermute x9, starting transfers between devices: 14 us -> 16 us  [exchanged(): terms[by] = lax.ppermute(slabs[by], axis, pairs)]
    ppermute x5, waiting for transfers between devices: 5.86 us -> 4.33 us  [shifted(): return lax.ppermute(array, axis, pairs)]
    ppermute x5, starting transfers between devices: 10.4 us -> 11.4 us  [shifted(): return lax.ppermute(array, axis, pairs)]
  transfers between devices with their start and end apart: 14 -> 14, of which waited for: 5 -> 8; matrix products, arithmetic and copies ran while one was open for 5% -> 5% of each run, Pallas kernels for 14% -> 15%
where the time goes in v5:
time: 51.5 us; the launch traced here: 51.2 us
  starting transfers between devices  27.4 us (53%)
  waiting for transfers between devices  10.2 us (20%)
  Pallas kernels  7.45 us (14%)
  matrix products  2.71 us (5%)
  local copies, waits for them, and re-layouts  2.46 us (5%)
  other arithmetic  0.77 us (1%)
    ppermute x9, starting transfers between devices, exchanged(): terms[by] = lax.ppermute(slabs[by], axis, pairs)  16 us
    ppermute x5, starting transfers between devices, shifted(): return lax.ppermute(array, axis, pairs)  11.4 us
    pallas_call x4, Pallas kernels, kernel_call(): pl.pallas_call(kernel, out_shape=out_shape, in_specs=[spec or whole for s...  7.45 us
    ppermute x9, waiting for transfers between devices, exchanged(): terms[by] = lax.ppermute(slabs[by], axis, pairs)  5.85 us
    ppermute x5, waiting for transfers between devices, shifted(): return lax.ppermute(array, axis, pairs)  4.33 us
    slice x1, local copies, waits for them, and re-layouts, per_device(): above_first = shifted(genotypes[:, :half], 'snp', -1)  2.41 us
    dot_general x1, matrix products, per_device(): jnp.dot(own_weights, annotations, preferred_element_type=jnp.float32)  1.45 us
  transfers between devices with their start and end apart: 14, of which 8 were waited for; matrix products, arithmetic and copies ran while one was open for 5% of the time, Pallas kernels for 15%

profile of v5, /device:TPU:4, one launch (start us, length us, event | category | flops | bytes accessed | tf_op | source)
XLA Modules:
  0.0 51.2 jit_solution(7728698503376726297)
XLA Ops:
  0.0 2.4 %slice.78 = bf16[2048,256]{1,0:T(8,128)(2,1)} slice(bf16[2048,512]{1,0:T(8,128)(2,1)} %left.3), slice={[0:2048], [0:256]} | slice | bytes 2097152 | tf_op jit(solution)/shard_map/slice | solution.py:179
  2.4 2.8 %collective-permute-start = (bf16[2048,256]{1,0:T(8,128)(2,1)}, bf16[2048,256]{1,0:T(8,128)(2,1)}, u32[]{:S(2)}, u32[]{:S(2)}) collective-permute-start(bf16[2048,256]{1,0:T(8,128)(2,1)} %slice.78), channel_id=1, source_target_pairs={{4,0},{8,4},{12,8},{16,12},{20,16},{24,20},{28,24},{5,1},{9,5},{13... | collective-permute-start | bytes 3145736 | tf_op jit(solution)/shard_map/ppermute | solution.py:19
  5.3 3.1 %shard_map.46 = (bf16[2048,256]{1,0:T(8,128)(2,1)}, f32[1,512]{1,0:T(1,128)S(1)}, s16[144,512]{1,0:T(8,128)(2,1)S(1)}, s16[144,512]{1,0:T(8,128)(2,1)}, s16[144,...) custom-call(s32[2]{0:T(128)S(1)} %pad_add_fusion.place, bf16[2048,512]{1,0:T(8,128)(2,1)S(1)} %copy-done), custom_call_target="tpu_custom_call" | custom-call | bytes 9250000 | tf_op jit(solution)/shard_map/pallas_call | solution.py:89
  8.4 1.6 %collective-permute-start.1 = (s16[144,512]{1,0:T(8,128)(2,1)}, s16[144,512]{1,0:T(8,128)(2,1)S(1)}, u32[]{:S(2)}, u32[]{:S(2)}) collective-permute-start(s16[144,512]{1,0:T(8,128)(2,1)} %get-tuple-element.37), channel_id=1, source_target_pairs={{0,1},{1,2},{2,3},{3,0},{4,5},{5,6},{6,7},{7,4},{8,9},{9,10},{10,1... | collective-permute-start | bytes 442376 | tf_op jit(solution)/shard_map/ppermute | solution.py:31
  10.0 2.6 %collective-permute-start.2 = (s16[144,512]{1,0:T(8,128)(2,1)}, s16[144,512]{1,0:T(8,128)(2,1)}, u32[]{:S(2)}, u32[]{:S(2)}) collective-permute-start(s16[144,512]{1,0:T(8,128)(2,1)} %get-tuple-element.39), channel_id=1, source_target_pairs={{0,2},{1,3},{2,0},{3,1},{4,6},{5,7},{6,4},{7,5},{8,10},{9,11},{10,... | collective-permute-start | bytes 442376 | tf_op jit(solution)/shard_map/ppermute | solution.py:31
  12.6 1.3 %collective-permute-start.3 = (s16[144,512]{1,0:T(8,128)(2,1)}, s16[144,512]{1,0:T(8,128)(2,1)}, u32[]{:S(2)}, u32[]{:S(2)}) collective-permute-start(s16[144,512]{1,0:T(8,128)(2,1)} %get-tuple-element.41), channel_id=1, source_target_pairs={{0,3},{1,0},{2,1},{3,2},{4,7},{5,4},{6,5},{7,6},{8,11},{9,8},{10,9... | collective-permute-start | bytes 442376 | tf_op jit(solution)/shard_map/ppermute | solution.py:31
  13.9 1.9 %collective-permute-start.4 = (bf16[2048,256]{1,0:T(8,128)(2,1)}, bf16[2048,256]{1,0:T(8,128)(2,1)S(1)}, u32[]{:S(2)}, u32[]{:S(2)}) collective-permute-start(bf16[2048,256]{1,0:T(8,128)(2,1)} %get-tuple-element.48), channel_id=1, source_target_pairs={{4,0},{8,4},{12,8},{16,12},{20,16},{24,20},{28,24},{5,1},{9,5},{13... | collective-permute-start | bytes 3145736 | tf_op jit(solution)/shard_map/ppermute | solution.py:19
  15.9 1.4 %collective-permute-done.1.rest_1_ = s16[144,512]{1,0:T(8,128)(2,1)S(1)} collective-permute-done((s16[144,512]{1,0:T(8,128)(2,1)}, s16[144,512]{1,0:T(8,128)(2,1)S(1)}, u32[]{:S(2)}, u32[]{:S(2)}) %collective-permute-start.1) | collective-permute-done | bytes 147488 | tf_op jit(solution)/shard_map/ppermute | solution.py:31
  17.8 2.1 %shard_map.47 = (f32[256,256]{1,0:T(8,128)S(1)}, s16[128,256]{1,0:T(8,128)(2,1)S(1)}, s16[128,256]{1,0:T(8,128)(2,1)S(1)}, s16[128,256]{1,0:T(8,128)(2,1)S(1)}, s16[128,256]{1,0:T(8,128)(2,1)S(1)}) custom-call(s32[2]{0:T(128)S(1)} %pad_add_fusion.place, bf16[2048,512]{1,0:T(8,128)(2,1)S(1)} %copy-done, bf16[2048,256]{1,0:T(8,128)(2,1)} %collective-permute-done.right, ...), custom_call_target="tpu_custom_call" | custom-call | bytes 9250000 | tf_op jit(solution)/shard_map/pallas_call | solution.py:89
  20.0 2.4 %collective-permute-done.2.rest_2_ = s16[144,512]{1,0:T(8,128)(2,1)} collective-permute-done((s16[144,512]{1,0:T(8,128)(2,1)}, s16[144,512]{1,0:T(8,128)(2,1)}, u32[]{:S(2)}, u32[]{:S(2)}) %collective-permute-start.2) | collective-permute-done | bytes 147488 | tf_op jit(solution)/shard_map/ppermute | solution.py:31
  23.4 2.9 %collective-permute-start.6 = (f32[8,512]{1,0:T(8,128)S(1)}, f32[8,512]{1,0:T(8,128)S(1)}, u32[]{:S(2)}, u32[]{:S(2)}) collective-permute-start(f32[8,512]{1,0:T(8,128)S(1)} %get-tuple-element.44), channel_id=1, source_target_pairs={{4,0},{8,4},{12,8},{16,12},{20,16},{24,20},{28,24},{5,1},{9,5},{13... | collective-permute-start | bytes 49160 | tf_op jit(solution)/shard_map/ppermute | solution.py:19
  26.3 3.8 %collective-permute-start.5 = (s16[128,256]{1,0:T(8,128)(2,1)S(1)}, s16[128,256]{1,0:T(8,128)(2,1)S(1)}, u32[]{:S(2)}, u32[]{:S(2)}) collective-permute-start(s16[128,256]{1,0:T(8,128)(2,1)S(1)} %get-tuple-element.50), channel_id=1, source_target_pairs={{0,1},{1,2},{2,3},{3,0},{4,5},{5,6},{6,7},{7,4},{8,9},{9,10},{10,1... | collective-permute-start | bytes 196616 | tf_op jit(solution)/shard_map/ppermute | solution.py:31
  30.1 1.3 %collective-permute-start.8 = (s16[128,256]{1,0:T(8,128)(2,1)S(1)}, s16[128,256]{1,0:T(8,128)(2,1)S(1)}, u32[]{:S(2)}, u32[]{:S(2)}) collective-permute-start(s16[128,256]{1,0:T(8,128)(2,1)S(1)} %get-tuple-element.55), channel_id=1, source_target_pairs={{0,2},{1,3},{2,0},{3,1},{4,6},{5,7},{6,4},{7,5},{8,10},{9,11},{10,... | collective-permute-start | bytes 196616 | tf_op jit(solution)/shard_map/ppermute | solution.py:31
  31.4 1.1 %collective-permute-start.10 = (s16[128,256]{1,0:T(8,128)(2,1)S(1)}, s16[128,256]{1,0:T(8,128)(2,1)S(1)}, u32[]{:S(2)}, u32[]{:S(2)}) collective-permute-start(s16[128,256]{1,0:T(8,128)(2,1)S(1)} %get-tuple-element.58), channel_id=1, source_target_pairs={{0,3},{1,0},{2,1},{3,2},{4,7},{5,4},{6,5},{7,6},{8,11},{9,8},{10,9... | collective-permute-start | bytes 196616 | tf_op jit(solution)/shard_map/ppermute | solution.py:31
  33.1 1.2 %shard_map.49 = (s16[128,256]{1,0:T(8,128)(2,1)S(1)}, s16[128,256]{1,0:T(8,128)(2,1)S(1)}, s16[128,256]{1,0:T(8,128)(2,1)S(1)}, s16[128,256]{1,0:T(8,128)(2,1)S(1)}) custom-call(s32[2]{0:T(128)S(1)} %pad_add_fusion.place, bf16[2048,512]{1,0:T(8,128)(2,1)S(1)} %copy-done, bf16[2048,256]{1,0:T(8,128)(2,1)S(1)} %collective-permute-done.4.right, ...), custom_call_target="tpu_custom_call" | custom-call | bytes 7400000 | tf_op jit(solution)/shard_map/pallas_call | solution.py:89
  34.3 1.8 %collective-permute-start.7 = (s16[128,256]{1,0:T(8,128)(2,1)S(1)}, s16[128,256]{1,0:T(8,128)(2,1)S(1)}, u32[]{:S(2)}, u32[]{:S(2)}) collective-permute-start(s16[128,256]{1,0:T(8,128)(2,1)S(1)} %get-tuple-element.53), channel_id=1, source_target_pairs={{0,1},{1,2},{2,3},{3,0},{4,5},{5,6},{6,7},{7,4},{8,9},{9,10},{10,1... | collective-permute-start | bytes 196616 | tf_op jit(solution)/shard_map/ppermute | solution.py:31
  36.1 1.3 %collective-permute-start.9 = (s16[128,256]{1,0:T(8,128)(2,1)S(1)}, s16[128,256]{1,0:T(8,128)(2,1)S(1)}, u32[]{:S(2)}, u32[]{:S(2)}) collective-permute-start(s16[128,256]{1,0:T(8,128)(2,1)S(1)} %get-tuple-element.56), channel_id=1, source_target_pairs={{0,2},{1,3},{2,0},{3,1},{4,6},{5,7},{6,4},{7,5},{8,10},{9,11},{10,... | collective-permute-start | bytes 196616 | tf_op jit(solution)/shard_map/ppermute | solution.py:31
  37.4 1.2 %collective-permute-start.11 = (s16[128,256]{1,0:T(8,128)(2,1)S(1)}, s16[128,256]{1,0:T(8,128)(2,1)S(1)}, u32[]{:S(2)}, u32[]{:S(2)}) collective-permute-start(s16[128,256]{1,0:T(8,128)(2,1)S(1)} %get-tuple-element.59), channel_id=1, source_target_pairs={{0,3},{1,0},{2,1},{3,2},{4,7},{5,4},{6,5},{7,6},{8,11},{9,8},{10,9... | collective-permute-start | bytes 196616 | tf_op jit(solution)/shard_map/ppermute | solution.py:31
  38.6 1.9 %collective-permute-start.12 = (bf16[512,512]{1,0:T(8,128)(2,1)S(1)}, bf16[512,512]{1,0:T(8,128)(2,1)S(1)}, u32[]{:S(2)}, u32[]{:S(2)}) collective-permute-start(bf16[512,512]{1,0:T(8,128)(2,1)S(1)} %copy-done.3), channel_id=1, source_target_pairs={{4,0},{8,4},{12,8},{16,12},{20,16},{24,20},{28,24},{5,1},{9,5},{13... | collective-permute-start | bytes 1572872 | tf_op jit(solution)/shard_map/ppermute | solution.py:19
  41.0 1.4 %collective-permute-done.9 = s16[128,256]{1,0:T(8,128)(2,1)S(1)} collective-permute-done((s16[128,256]{1,0:T(8,128)(2,1)S(1)}, s16[128,256]{1,0:T(8,128)(2,1)S(1)}, u32[]{:S(2)}, u32[]{:S(2)}) %collective-permute-start.9) | collective-permute-done | bytes 65568 | tf_op jit(solution)/shard_map/ppermute | solution.py:31
  43.0 1.9 %collective-permute-start.13 = (bf16[128,512]{1,0:T(8,128)(2,1)S(1)}, bf16[128,512]{1,0:T(8,128)(2,1)S(1)}, u32[]{:S(2)}, u32[]{:S(2)}) collective-permute-start(bf16[128,512]{1,0:T(8,128)(2,1)S(1)} %convolution_convert_fusion), channel_id=1, source_target_pairs={{0,4},{4,8},{8,12},{12,16},{16,20},{20,24},{24,28},{1,5},{5,9},{9,... | collective-permute-start | bytes 393224 | tf_op jit(solution)/shard_map/ppermute | solution.py:19
  45.0 1.5 %fusion.13 = f32[128,512]{1,0:T(8,128)S(1)} fusion(bf16[512,512]{1,0:T(8,128)(2,1)S(1)} %copy-done.3, s16[144,512]{1,0:T(8,128)(2,1)} %collective-permute-done.3.rest_3_, s16[144,512]{1,0:T(8,128)(2,1)} %collective-permute-done.2.rest_2_, s16[144,512]{1,0:T(8,128)(2,1)S(1)} %collective-permute-done.1.rest_1_, f32[128]{0:T(128)S(1)} %get-tuple-element.65, ...), kind=kOutput, calls=%fused_computation.17 | convolution fusion | flops 68747264 | bytes 1324544 | tf_op jit(solution)/shard_map/dot_general | solution.py:259
  47.2 3.0 %collective-permute-done.13 = bf16[128,512]{1,0:T(8,128)(2,1)S(1)} collective-permute-done((bf16[128,512]{1,0:T(8,128)(2,1)S(1)}, bf16[128,512]{1,0:T(8,128)(2,1)S(1)}, u32[]{:S(2)}, u32[]{:S(2)}) %collective-permute-start.13) | collective-permute-done | bytes 131104 | tf_op jit(solution)/shard_map/ppermute | solution.py:19
  50.2 1.0 %fusion = f32[128,512]{1,0:T(8,128)} fusion(f32[128,512]{1,0:T(8,128)S(1)} %fusion.13, bf16[512,512]{1,0:T(8,128)(2,1)S(1)} %collective-permute-done.12, bf16[128,512]{1,0:T(8,128)(2,1)S(1)} %collective-permute-done.13, bf16[128,512]{1,0:T(8,128)(2,1)S(1)} %subtract_convert_fusion, s32[128]{0:T(128)S(1)} %iota_add_fusion.1, s32[512]{0:T(512)S(1)} %broadcast_add_fusion, ...), kind=kOutput, calls=%fused_computation.1 | convolution fusion | flops 67567616 | bytes 1313792 | tf_op jit(solution)/shard_map/dot_general | solution.py:275
  (31 shorter events, 4.0 us)
Async XLA Ops:
  0.0 5.3 %copy-start = (bf16[2048,512]{1,0:T(8,128)(2,1)S(1)}, bf16[2048,512]{1,0:T(8,128)(2,1)}, u32[]{:S(2)}) copy-start(bf16[2048,512]{1,0:T(8,128)(2,1)} %left.3) | copy-start | bytes 6291460
  2.4 15.4 %collective-permute-start = (bf16[2048,256]{1,0:T(8,128)(2,1)}, bf16[2048,256]{1,0:T(8,128)(2,1)}, u32[]{:S(2)}, u32[]{:S(2)}) collective-permute-start(bf16[2048,256]{1,0:T(8,128)(2,1)} %slice.78), channel_id=1, source_target_pairs={{4,0},{8,4},{12,8},{16,12},{20,16},{24,20},{28,24},{5,1},{9,5},{13... | collective-permute-start | bytes 3145736 | tf_op jit(solution)/shard_map/ppermute | solution.py:19
  8.4 14.0 %copy-start.1 = (s32[128]{0:T(128)S(1)}, s32[128]{0:T(128)}, u32[]{:S(2)}) copy-start(s32[128]{0:T(128)} %param.6) | copy-start | bytes 1540
  8.4 8.9 %collective-permute-start.1 = (s16[144,512]{1,0:T(8,128)(2,1)}, s16[144,512]{1,0:T(8,128)(2,1)S(1)}, u32[]{:S(2)}, u32[]{:S(2)}) collective-permute-start(s16[144,512]{1,0:T(8,128)(2,1)} %get-tuple-element.37), channel_id=1, source_target_pairs={{0,1},{1,2},{2,3},{3,0},{4,5},{5,6},{6,7},{7,4},{8,9},{9,10},{10,1... | collective-permute-start | bytes 442376 | tf_op jit(solution)/shard_map/ppermute | solution.py:31
  10.0 12.4 %collective-permute-start.2 = (s16[144,512]{1,0:T(8,128)(2,1)}, s16[144,512]{1,0:T(8,128)(2,1)}, u32[]{:S(2)}, u32[]{:S(2)}) collective-permute-start(s16[144,512]{1,0:T(8,128)(2,1)} %get-tuple-element.39), channel_id=1, source_target_pairs={{0,2},{1,3},{2,0},{3,1},{4,6},{5,7},{6,4},{7,5},{8,10},{9,11},{10,... | collective-permute-start | bytes 442376 | tf_op jit(solution)/shard_map/ppermute | solution.py:31
  12.6 9.8 %collective-permute-start.3 = (s16[144,512]{1,0:T(8,128)(2,1)}, s16[144,512]{1,0:T(8,128)(2,1)}, u32[]{:S(2)}, u32[]{:S(2)}) collective-permute-start(s16[144,512]{1,0:T(8,128)(2,1)} %get-tuple-element.41), channel_id=1, source_target_pairs={{0,3},{1,0},{2,1},{3,2},{4,7},{5,4},{6,5},{7,6},{8,11},{9,8},{10,9... | collective-permute-start | bytes 442376 | tf_op jit(solution)/shard_map/ppermute | solution.py:31
  13.9 18.9 %collective-permute-start.4 = (bf16[2048,256]{1,0:T(8,128)(2,1)}, bf16[2048,256]{1,0:T(8,128)(2,1)S(1)}, u32[]{:S(2)}, u32[]{:S(2)}) collective-permute-start(bf16[2048,256]{1,0:T(8,128)(2,1)} %get-tuple-element.48), channel_id=1, source_target_pairs={{4,0},{8,4},{12,8},{16,12},{20,16},{24,20},{28,24},{5,1},{9,5},{13... | collective-permute-start | bytes 3145736 | tf_op jit(solution)/shard_map/ppermute | solution.py:19
  22.4 16.2 %copy-start.3 = (bf16[512,512]{1,0:T(8,128)(2,1)S(1)}, bf16[512,512]{1,0:T(8,128)(2,1)}, u32[]{:S(2)}) copy-start(bf16[512,512]{1,0:T(8,128)(2,1)} %param.5) | copy-start | bytes 1572868
  23.4 9.4 %collective-permute-start.6 = (f32[8,512]{1,0:T(8,128)S(1)}, f32[8,512]{1,0:T(8,128)S(1)}, u32[]{:S(2)}, u32[]{:S(2)}) collective-permute-start(f32[8,512]{1,0:T(8,128)S(1)} %get-tuple-element.44), channel_id=1, source_target_pairs={{4,0},{8,4},{12,8},{16,12},{20,16},{24,20},{28,24},{5,1},{9,5},{13... | collective-permute-start | bytes 49160 | tf_op jit(solution)/shard_map/ppermute | solution.py:19
  26.3 6.8 %collective-permute-start.5 = (s16[128,256]{1,0:T(8,128)(2,1)S(1)}, s16[128,256]{1,0:T(8,128)(2,1)S(1)}, u32[]{:S(2)}, u32[]{:S(2)}) collective-permute-start(s16[128,256]{1,0:T(8,128)(2,1)S(1)} %get-tuple-element.50), channel_id=1, source_target_pairs={{0,1},{1,2},{2,3},{3,0},{4,5},{5,6},{6,7},{7,4},{8,9},{9,10},{10,1... | collective-permute-start | bytes 196616 | tf_op jit(solution)/shard_map/ppermute | solution.py:31
  30.1 8.6 %collective-permute-start.8 = (s16[128,256]{1,0:T(8,128)(2,1)S(1)}, s16[128,256]{1,0:T(8,128)(2,1)S(1)}, u32[]{:S(2)}, u32[]{:S(2)}) collective-permute-start(s16[128,256]{1,0:T(8,128)(2,1)S(1)} %get-tuple-element.55), channel_id=1, source_target_pairs={{0,2},{1,3},{2,0},{3,1},{4,6},{5,7},{6,4},{7,5},{8,10},{9,11},{10,... | collective-permute-start | bytes 196616 | tf_op jit(solution)/shard_map/ppermute | solution.py:31
  31.4 9.2 %collective-permute-start.10 = (s16[128,256]{1,0:T(8,128)(2,1)S(1)}, s16[128,256]{1,0:T(8,128)(2,1)S(1)}, u32[]{:S(2)}, u32[]{:S(2)}) collective-permute-start(s16[128,256]{1,0:T(8,128)(2,1)S(1)} %get-tuple-element.58), channel_id=1, source_target_pairs={{0,3},{1,0},{2,1},{3,2},{4,7},{5,4},{6,5},{7,6},{8,11},{9,8},{10,9... | collective-permute-start | bytes 196616 | tf_op jit(solution)/shard_map/ppermute | solution.py:31
  32.8 12.1 %copy-start.2 = (s32[128]{0:T(128)S(1)}, s32[128]{0:T(128)}, u32[]{:S(2)}) copy-start(s32[128]{0:T(128)} %param.7) | copy-start | bytes 1540
  34.3 6.7 %collective-permute-start.7 = (s16[128,256]{1,0:T(8,128)(2,1)S(1)}, s16[128,256]{1,0:T(8,128)(2,1)S(1)}, u32[]{:S(2)}, u32[]{:S(2)}) collective-permute-start(s16[128,256]{1,0:T(8,128)(2,1)S(1)} %get-tuple-element.53), channel_id=1, source_target_pairs={{0,1},{1,2},{2,3},{3,0},{4,5},{5,6},{6,7},{7,4},{8,9},{9,10},{10,1... | collective-permute-start | bytes 196616 | tf_op jit(solution)/shard_map/ppermute | solution.py:31
  36.1 6.2 %collective-permute-start.9 = (s16[128,256]{1,0:T(8,128)(2,1)S(1)}, s16[128,256]{1,0:T(8,128)(2,1)S(1)}, u32[]{:S(2)}, u32[]{:S(2)}) collective-permute-start(s16[128,256]{1,0:T(8,128)(2,1)S(1)} %get-tuple-element.56), channel_id=1, source_target_pairs={{0,2},{1,3},{2,0},{3,1},{4,6},{5,7},{6,4},{7,5},{8,10},{9,11},{10,... | collective-permute-start | bytes 196616 | tf_op jit(solution)/shard_map/ppermute | solution.py:31
  37.4 5.0 %collective-permute-start.11 = (s16[128,256]{1,0:T(8,128)(2,1)S(1)}, s16[128,256]{1,0:T(8,128)(2,1)S(1)}, u32[]{:S(2)}, u32[]{:S(2)}) collective-permute-start(s16[128,256]{1,0:T(8,128)(2,1)S(1)} %get-tuple-element.59), channel_id=1, source_target_pairs={{0,3},{1,0},{2,1},{3,2},{4,7},{5,4},{6,5},{7,6},{8,11},{9,8},{10,9... | collective-permute-start | bytes 196616 | tf_op jit(solution)/shard_map/ppermute | solution.py:31
  38.6 8.6 %collective-permute-start.12 = (bf16[512,512]{1,0:T(8,128)(2,1)S(1)}, bf16[512,512]{1,0:T(8,128)(2,1)S(1)}, u32[]{:S(2)}, u32[]{:S(2)}) collective-permute-start(bf16[512,512]{1,0:T(8,128)(2,1)S(1)} %copy-done.3), channel_id=1, source_target_pairs={{4,0},{8,4},{12,8},{16,12},{20,16},{24,20},{28,24},{5,1},{9,5},{13... | collective-permute-start | bytes 1572872 | tf_op jit(solution)/shard_map/ppermute | solution.py:19
  43.0 7.2 %collective-permute-start.13 = (bf16[128,512]{1,0:T(8,128)(2,1)S(1)}, bf16[128,512]{1,0:T(8,128)(2,1)S(1)}, u32[]{:S(2)}, u32[]{:S(2)}) collective-permute-start(bf16[128,512]{1,0:T(8,128)(2,1)S(1)} %convolution_convert_fusion), channel_id=1, source_target_pairs={{0,4},{4,8},{8,12},{12,16},{16,20},{20,24},{24,28},{1,5},{5,9},{9,... | collective-permute-start | bytes 393224 | tf_op jit(solution)/shard_map/ppermute | solution.py:19

commit v6 on v5

--- a/solution.py
+++ b/solution.py
@@ -10,7 +10,7 @@
 UNIT = 32000.0
 COST_T, COST_O, COST_F, COST_S, COST_H = 2.0, 2.5, 2.5, 2.0, 1.0
 LANES = 128
-CODE_ROWS = 16
+CODE_ROWS = 8
 
 
 def shifted(array, axis, by):

time: 51.5 us -> 50.9 us (0.988)
  waiting for transfers between devices: 10.2 us -> 9.31 us
    ppermute x9, waiting for transfers between devices: 5.85 us -> 4.79 us  [exchanged(): terms[by] = lax.ppermute(slabs[by], axis, pairs)]
where the time goes in v6:
time: 50.9 us; the launch traced here: 50.6 us
  starting transfers between devices  27.8 us (55%)
  waiting for transfers between devices  9.31 us (18%)
  Pallas kernels  7.42 us (15%)
  matrix products  2.71 us (5%)
  local copies, waits for them, and re-layouts  2.46 us (5%)
  other arithmetic  0.77 us (2%)
    ppermute x9, starting transfers between devices, exchanged(): terms[by] = lax.ppermute(slabs[by], axis, pairs)  16.1 us
    ppermute x5, starting transfers between devices, shifted(): return lax.ppermute(array, axis, pairs)  11.7 us
    pallas_call x4, Pallas kernels, kernel_call(): pl.pallas_call(kernel, out_shape=out_shape, in_specs=[spec or whole for s...  7.42 us
    ppermute x9, waiting for transfers between devices, exchanged(): terms[by] = lax.ppermute(slabs[by], axis, pairs)  4.79 us
    ppermute x5, waiting for transfers between devices, shifted(): return lax.ppermute(array, axis, pairs)  4.51 us
    slice x1, local copies, waits for them, and re-layouts, per_device(): above_first = shifted(genotypes[:, :half], 'snp', -1)  2.41 us
    dot_general x1, matrix products, per_device(): jnp.dot(own_weights, annotations, preferred_element_type=jnp.float32)  1.46 us
  transfers between devices with their start and end apart: 14, of which 8 were waited for; matrix products, arithmetic and copies ran while one was open for 5% of the time, Pallas kernels for 15%

profile of v6, /device:TPU:4, one launch (start us, length us, event | category | flops | bytes accessed | tf_op | source)
XLA Modules:
  0.0 50.6 jit_solution(14836548048021902106)
XLA Ops:
  0.0 2.4 %slice.78 = bf16[2048,256]{1,0:T(8,128)(2,1)} slice(bf16[2048,512]{1,0:T(8,128)(2,1)} %left.3), slice={[0:2048], [0:256]} | slice | bytes 2097152 | tf_op jit(solution)/shard_map/slice | solution.py:179
  2.4 2.8 %collective-permute-start = (bf16[2048,256]{1,0:T(8,128)(2,1)}, bf16[2048,256]{1,0:T(8,128)(2,1)}, u32[]{:S(2)}, u32[]{:S(2)}) collective-permute-start(bf16[2048,256]{1,0:T(8,128)(2,1)} %slice.78), channel_id=1, source_target_pairs={{4,0},{8,4},{12,8},{16,12},{20,16},{24,20},{28,24},{5,1},{9,5},{13... | collective-permute-start | bytes 3145736 | tf_op jit(solution)/shard_map/ppermute | solution.py:19
  5.3 3.1 %shard_map.46 = (bf16[2048,256]{1,0:T(8,128)(2,1)}, f32[1,512]{1,0:T(1,128)S(1)}, s16[136,512]{1,0:T(8,128)(2,1)S(1)}, s16[136,512]{1,0:T(8,128)(2,1)}, s16[136,...) custom-call(s32[2]{0:T(128)S(1)} %pad_add_fusion.place, bf16[2048,512]{1,0:T(8,128)(2,1)S(1)} %copy-done), custom_call_target="tpu_custom_call" | custom-call | bytes 9250000 | tf_op jit(solution)/shard_map/pallas_call | solution.py:89
  8.4 1.6 %collective-permute-start.1 = (s16[136,512]{1,0:T(8,128)(2,1)}, s16[136,512]{1,0:T(8,128)(2,1)S(1)}, u32[]{:S(2)}, u32[]{:S(2)}) collective-permute-start(s16[136,512]{1,0:T(8,128)(2,1)} %get-tuple-element.37), channel_id=1, source_target_pairs={{0,1},{1,2},{2,3},{3,0},{4,5},{5,6},{6,7},{7,4},{8,9},{9,10},{10,1... | collective-permute-start | bytes 417800 | tf_op jit(solution)/shard_map/ppermute | solution.py:31
  10.0 2.6 %collective-permute-start.2 = (s16[136,512]{1,0:T(8,128)(2,1)}, s16[136,512]{1,0:T(8,128)(2,1)}, u32[]{:S(2)}, u32[]{:S(2)}) collective-permute-start(s16[136,512]{1,0:T(8,128)(2,1)} %get-tuple-element.39), channel_id=1, source_target_pairs={{0,2},{1,3},{2,0},{3,1},{4,6},{5,7},{6,4},{7,5},{8,10},{9,11},{10,... | collective-permute-start | bytes 417800 | tf_op jit(solution)/shard_map/ppermute | solution.py:31
  12.6 1.3 %collective-permute-start.3 = (s16[136,512]{1,0:T(8,128)(2,1)}, s16[136,512]{1,0:T(8,128)(2,1)}, u32[]{:S(2)}, u32[]{:S(2)}) collective-permute-start(s16[136,512]{1,0:T(8,128)(2,1)} %get-tuple-element.41), channel_id=1, source_target_pairs={{0,3},{1,0},{2,1},{3,2},{4,7},{5,4},{6,5},{7,6},{8,11},{9,8},{10,9... | collective-permute-start | bytes 417800 | tf_op jit(solution)/shard_map/ppermute | solution.py:31
  13.9 1.9 %collective-permute-start.4 = (bf16[2048,256]{1,0:T(8,128)(2,1)}, bf16[2048,256]{1,0:T(8,128)(2,1)S(1)}, u32[]{:S(2)}, u32[]{:S(2)}) collective-permute-start(bf16[2048,256]{1,0:T(8,128)(2,1)} %get-tuple-element.48), channel_id=1, source_target_pairs={{4,0},{8,4},{12,8},{16,12},{20,16},{24,20},{28,24},{5,1},{9,5},{13... | collective-permute-start | bytes 3145736 | tf_op jit(solution)/shard_map/ppermute | solution.py:19
  15.9 1.2 %collective-permute-done.1.rest_1_ = s16[136,512]{1,0:T(8,128)(2,1)S(1)} collective-permute-done((s16[136,512]{1,0:T(8,128)(2,1)}, s16[136,512]{1,0:T(8,128)(2,1)S(1)}, u32[]{:S(2)}, u32[]{:S(2)}) %collective-permute-start.1) | collective-permute-done | bytes 139296 | tf_op jit(solution)/shard_map/ppermute | solution.py:31
  17.8 2.1 %shard_map.47 = (f32[256,256]{1,0:T(8,128)S(1)}, s16[128,256]{1,0:T(8,128)(2,1)S(1)}, s16[128,256]{1,0:T(8,128)(2,1)S(1)}, s16[128,256]{1,0:T(8,128)(2,1)S(1)}, s16[128,256]{1,0:T(8,128)(2,1)S(1)}) custom-call(s32[2]{0:T(128)S(1)} %pad_add_fusion.place, bf16[2048,512]{1,0:T(8,128)(2,1)S(1)} %copy-done, bf16[2048,256]{1,0:T(8,128)(2,1)} %collective-permute-done.right, ...), custom_call_target="tpu_custom_call" | custom-call | bytes 9250000 | tf_op jit(solution)/shard_map/pallas_call | solution.py:89
  20.0 1.9 %collective-permute-done.2.rest_2_ = s16[136,512]{1,0:T(8,128)(2,1)} collective-permute-done((s16[136,512]{1,0:T(8,128)(2,1)}, s16[136,512]{1,0:T(8,128)(2,1)}, u32[]{:S(2)}, u32[]{:S(2)}) %collective-permute-start.2) | collective-permute-done | bytes 139296 | tf_op jit(solution)/shard_map/ppermute | solution.py:31
  22.8 3.1 %collective-permute-start.6 = (f32[8,512]{1,0:T(8,128)S(1)}, f32[8,512]{1,0:T(8,128)S(1)}, u32[]{:S(2)}, u32[]{:S(2)}) collective-permute-start(f32[8,512]{1,0:T(8,128)S(1)} %get-tuple-element.44), channel_id=1, source_target_pairs={{4,0},{8,4},{12,8},{16,12},{20,16},{24,20},{28,24},{5,1},{9,5},{13... | collective-permute-start | bytes 49160 | tf_op jit(solution)/shard_map/ppermute | solution.py:19
  26.0 3.4 %collective-permute-start.5 = (s16[128,256]{1,0:T(8,128)(2,1)S(1)}, s16[128,256]{1,0:T(8,128)(2,1)S(1)}, u32[]{:S(2)}, u32[]{:S(2)}) collective-permute-start(s16[128,256]{1,0:T(8,128)(2,1)S(1)} %get-tuple-element.50), channel_id=1, source_target_pairs={{0,1},{1,2},{2,3},{3,0},{4,5},{5,6},{6,7},{7,4},{8,9},{9,10},{10,1... | collective-permute-start | bytes 196616 | tf_op jit(solution)/shard_map/ppermute | solution.py:31
  29.3 1.3 %collective-permute-start.8 = (s16[128,256]{1,0:T(8,128)(2,1)S(1)}, s16[128,256]{1,0:T(8,128)(2,1)S(1)}, u32[]{:S(2)}, u32[]{:S(2)}) collective-permute-start(s16[128,256]{1,0:T(8,128)(2,1)S(1)} %get-tuple-element.55), channel_id=1, source_target_pairs={{0,2},{1,3},{2,0},{3,1},{4,6},{5,7},{6,4},{7,5},{8,10},{9,11},{10,... | collective-permute-start | bytes 196616 | tf_op jit(solution)/shard_map/ppermute | solution.py:31
  30.6 1.2 %collective-permute-start.10 = (s16[128,256]{1,0:T(8,128)(2,1)S(1)}, s16[128,256]{1,0:T(8,128)(2,1)S(1)}, u32[]{:S(2)}, u32[]{:S(2)}) collective-permute-start(s16[128,256]{1,0:T(8,128)(2,1)S(1)} %get-tuple-element.58), channel_id=1, source_target_pairs={{0,3},{1,0},{2,1},{3,2},{4,7},{5,4},{6,5},{7,6},{8,11},{9,8},{10,9... | collective-permute-start | bytes 196616 | tf_op jit(solution)/shard_map/ppermute | solution.py:31
  32.3 1.2 %shard_map.49 = (s16[128,256]{1,0:T(8,128)(2,1)S(1)}, s16[128,256]{1,0:T(8,128)(2,1)S(1)}, s16[128,256]{1,0:T(8,128)(2,1)S(1)}, s16[128,256]{1,0:T(8,128)(2,1)S(1)}) custom-call(s32[2]{0:T(128)S(1)} %pad_add_fusion.place, bf16[2048,512]{1,0:T(8,128)(2,1)S(1)} %copy-done, bf16[2048,256]{1,0:T(8,128)(2,1)S(1)} %collective-permute-done.4.right, ...), custom_call_target="tpu_custom_call" | custom-call | bytes 7400000 | tf_op jit(solution)/shard_map/pallas_call | solution.py:89
  33.6 1.8 %collective-permute-start.7 = (s16[128,256]{1,0:T(8,128)(2,1)S(1)}, s16[128,256]{1,0:T(8,128)(2,1)S(1)}, u32[]{:S(2)}, u32[]{:S(2)}) collective-permute-start(s16[128,256]{1,0:T(8,128)(2,1)S(1)} %get-tuple-element.53), channel_id=1, source_target_pairs={{0,1},{1,2},{2,3},{3,0},{4,5},{5,6},{6,7},{7,4},{8,9},{9,10},{10,1... | collective-permute-start | bytes 196616 | tf_op jit(solution)/shard_map/ppermute | solution.py:31
  35.4 1.1 %collective-permute-start.9 = (s16[128,256]{1,0:T(8,128)(2,1)S(1)}, s16[128,256]{1,0:T(8,128)(2,1)S(1)}, u32[]{:S(2)}, u32[]{:S(2)}) collective-permute-start(s16[128,256]{1,0:T(8,128)(2,1)S(1)} %get-tuple-element.56), channel_id=1, source_target_pairs={{0,2},{1,3},{2,0},{3,1},{4,6},{5,7},{6,4},{7,5},{8,10},{9,11},{10,... | collective-permute-start | bytes 196616 | tf_op jit(solution)/shard_map/ppermute | solution.py:31
  36.5 1.8 %collective-permute-start.11 = (s16[128,256]{1,0:T(8,128)(2,1)S(1)}, s16[128,256]{1,0:T(8,128)(2,1)S(1)}, u32[]{:S(2)}, u32[]{:S(2)}) collective-permute-start(s16[128,256]{1,0:T(8,128)(2,1)S(1)} %get-tuple-element.59), channel_id=1, source_target_pairs={{0,3},{1,0},{2,1},{3,2},{4,7},{5,4},{6,5},{7,6},{8,11},{9,8},{10,9... | collective-permute-start | bytes 196616 | tf_op jit(solution)/shard_map/ppermute | solution.py:31
  38.4 1.9 %collective-permute-start.12 = (bf16[512,512]{1,0:T(8,128)(2,1)S(1)}, bf16[512,512]{1,0:T(8,128)(2,1)S(1)}, u32[]{:S(2)}, u32[]{:S(2)}) collective-permute-start(bf16[512,512]{1,0:T(8,128)(2,1)S(1)} %copy-done.3), channel_id=1, source_target_pairs={{4,0},{8,4},{12,8},{16,12},{20,16},{24,20},{28,24},{5,1},{9,5},{13... | collective-permute-start | bytes 1572872 | tf_op jit(solution)/shard_map/ppermute | solution.py:19
  40.5 1.3 %collective-permute-done.9 = s16[128,256]{1,0:T(8,128)(2,1)S(1)} collective-permute-done((s16[128,256]{1,0:T(8,128)(2,1)S(1)}, s16[128,256]{1,0:T(8,128)(2,1)S(1)}, u32[]{:S(2)}, u32[]{:S(2)}) %collective-permute-start.9) | collective-permute-done | bytes 65568 | tf_op jit(solution)/shard_map/ppermute | solution.py:31
  42.5 1.9 %collective-permute-start.13 = (bf16[128,512]{1,0:T(8,128)(2,1)S(1)}, bf16[128,512]{1,0:T(8,128)(2,1)S(1)}, u32[]{:S(2)}, u32[]{:S(2)}) collective-permute-start(bf16[128,512]{1,0:T(8,128)(2,1)S(1)} %convolution_convert_fusion), channel_id=1, source_target_pairs={{0,4},{4,8},{8,12},{12,16},{16,20},{20,24},{24,28},{1,5},{5,9},{9,... | collective-permute-start | bytes 393224 | tf_op jit(solution)/shard_map/ppermute | solution.py:19
  44.4 1.5 %fusion.13 = f32[128,512]{1,0:T(8,128)S(1)} fusion(bf16[512,512]{1,0:T(8,128)(2,1)S(1)} %copy-done.3, s16[136,512]{1,0:T(8,128)(2,1)} %collective-permute-done.3.rest_3_, s16[136,512]{1,0:T(8,128)(2,1)} %collective-permute-done.2.rest_2_, s16[136,512]{1,0:T(8,128)(2,1)S(1)} %collective-permute-done.1.rest_1_, f32[128]{0:T(128)S(1)} %get-tuple-element.65, ...), kind=kOutput, calls=%fused_computation.17 | convolution fusion | flops 68747264 | bytes 1324544 | tf_op jit(solution)/shard_map/dot_general | solution.py:259
  45.9 1.3 %collective-permute-done.12 = bf16[512,512]{1,0:T(8,128)(2,1)S(1)} collective-permute-done((bf16[512,512]{1,0:T(8,128)(2,1)S(1)}, bf16[512,512]{1,0:T(8,128)(2,1)S(1)}, u32[]{:S(2)}, u32[]{:S(2)}) %collective-permute-start.12) | collective-permute-done | bytes 524320 | tf_op jit(solution)/shard_map/ppermute | solution.py:19
  47.2 2.4 %collective-permute-done.13 = bf16[128,512]{1,0:T(8,128)(2,1)S(1)} collective-permute-done((bf16[128,512]{1,0:T(8,128)(2,1)S(1)}, bf16[128,512]{1,0:T(8,128)(2,1)S(1)}, u32[]{:S(2)}, u32[]{:S(2)}) %collective-permute-start.13) | collective-permute-done | bytes 131104 | tf_op jit(solution)/shard_map/ppermute | solution.py:19
  (31 shorter events, 4.1 us)
Async XLA Ops:
  0.0 5.3 %copy-start = (bf16[2048,512]{1,0:T(8,128)(2,1)S(1)}, bf16[2048,512]{1,0:T(8,128)(2,1)}, u32[]{:S(2)}) copy-start(bf16[2048,512]{1,0:T(8,128)(2,1)} %left.3) | copy-start | bytes 6291460
  2.4 15.4 %collective-permute-start = (bf16[2048,256]{1,0:T(8,128)(2,1)}, bf16[2048,256]{1,0:T(8,128)(2,1)}, u32[]{:S(2)}, u32[]{:S(2)}) collective-permute-start(bf16[2048,256]{1,0:T(8,128)(2,1)} %slice.78), channel_id=1, source_target_pairs={{4,0},{8,4},{12,8},{16,12},{20,16},{24,20},{28,24},{5,1},{9,5},{13... | collective-permute-start | bytes 3145736 | tf_op jit(solution)/shard_map/ppermute | solution.py:19
  8.4 13.5 %copy-start.1 = (s32[128]{0:T(128)S(1)}, s32[128]{0:T(128)}, u32[]{:S(2)}) copy-start(s32[128]{0:T(128)} %param.6) | copy-start | bytes 1540
  8.4 8.7 %collective-permute-start.1 = (s16[136,512]{1,0:T(8,128)(2,1)}, s16[136,512]{1,0:T(8,128)(2,1)S(1)}, u32[]{:S(2)}, u32[]{:S(2)}) collective-permute-start(s16[136,512]{1,0:T(8,128)(2,1)} %get-tuple-element.37), channel_id=1, source_target_pairs={{0,1},{1,2},{2,3},{3,0},{4,5},{5,6},{6,7},{7,4},{8,9},{9,10},{10,1... | collective-permute-start | bytes 417800 | tf_op jit(solution)/shard_map/ppermute | solution.py:31
  10.0 11.9 %collective-permute-start.2 = (s16[136,512]{1,0:T(8,128)(2,1)}, s16[136,512]{1,0:T(8,128)(2,1)}, u32[]{:S(2)}, u32[]{:S(2)}) collective-permute-start(s16[136,512]{1,0:T(8,128)(2,1)} %get-tuple-element.39), channel_id=1, source_target_pairs={{0,2},{1,3},{2,0},{3,1},{4,6},{5,7},{6,4},{7,5},{8,10},{9,11},{10,... | collective-permute-start | bytes 417800 | tf_op jit(solution)/shard_map/ppermute | solution.py:31
  12.6 9.3 %collective-permute-start.3 = (s16[136,512]{1,0:T(8,128)(2,1)}, s16[136,512]{1,0:T(8,128)(2,1)}, u32[]{:S(2)}, u32[]{:S(2)}) collective-permute-start(s16[136,512]{1,0:T(8,128)(2,1)} %get-tuple-element.41), channel_id=1, source_target_pairs={{0,3},{1,0},{2,1},{3,2},{4,7},{5,4},{6,5},{7,6},{8,11},{9,8},{10,9... | collective-permute-start | bytes 417800 | tf_op jit(solution)/shard_map/ppermute | solution.py:31
  13.9 18.3 %collective-permute-start.4 = (bf16[2048,256]{1,0:T(8,128)(2,1)}, bf16[2048,256]{1,0:T(8,128)(2,1)S(1)}, u32[]{:S(2)}, u32[]{:S(2)}) collective-permute-start(bf16[2048,256]{1,0:T(8,128)(2,1)} %get-tuple-element.48), channel_id=1, source_target_pairs={{4,0},{8,4},{12,8},{16,12},{20,16},{24,20},{28,24},{5,1},{9,5},{13... | collective-permute-start | bytes 3145736 | tf_op jit(solution)/shard_map/ppermute | solution.py:19
  21.9 16.5 %copy-start.3 = (bf16[512,512]{1,0:T(8,128)(2,1)S(1)}, bf16[512,512]{1,0:T(8,128)(2,1)}, u32[]{:S(2)}) copy-start(bf16[512,512]{1,0:T(8,128)(2,1)} %param.5) | copy-start | bytes 1572868
  22.8 9.3 %collective-permute-start.6 = (f32[8,512]{1,0:T(8,128)S(1)}, f32[8,512]{1,0:T(8,128)S(1)}, u32[]{:S(2)}, u32[]{:S(2)}) collective-permute-start(f32[8,512]{1,0:T(8,128)S(1)} %get-tuple-element.44), channel_id=1, source_target_pairs={{4,0},{8,4},{12,8},{16,12},{20,16},{24,20},{28,24},{5,1},{9,5},{13... | collective-permute-start | bytes 49160 | tf_op jit(solution)/shard_map/ppermute | solution.py:19
  26.0 6.4 %collective-permute-start.5 = (s16[128,256]{1,0:T(8,128)(2,1)S(1)}, s16[128,256]{1,0:T(8,128)(2,1)S(1)}, u32[]{:S(2)}, u32[]{:S(2)}) collective-permute-start(s16[128,256]{1,0:T(8,128)(2,1)S(1)} %get-tuple-element.50), channel_id=1, source_target_pairs={{0,1},{1,2},{2,3},{3,0},{4,5},{5,6},{6,7},{7,4},{8,9},{9,10},{10,1... | collective-permute-start | bytes 196616 | tf_op jit(solution)/shard_map/ppermute | solution.py:31
  29.3 9.0 %collective-permute-start.8 = (s16[128,256]{1,0:T(8,128)(2,1)S(1)}, s16[128,256]{1,0:T(8,128)(2,1)S(1)}, u32[]{:S(2)}, u32[]{:S(2)}) collective-permute-start(s16[128,256]{1,0:T(8,128)(2,1)S(1)} %get-tuple-element.55), channel_id=1, source_target_pairs={{0,2},{1,3},{2,0},{3,1},{4,6},{5,7},{6,4},{7,5},{8,10},{9,11},{10,... | collective-permute-start | bytes 196616 | tf_op jit(solution)/shard_map/ppermute | solution.py:31
  30.6 9.7 %collective-permute-start.10 = (s16[128,256]{1,0:T(8,128)(2,1)S(1)}, s16[128,256]{1,0:T(8,128)(2,1)S(1)}, u32[]{:S(2)}, u32[]{:S(2)}) collective-permute-start(s16[128,256]{1,0:T(8,128)(2,1)S(1)} %get-tuple-element.58), channel_id=1, source_target_pairs={{0,3},{1,0},{2,1},{3,2},{4,7},{5,4},{6,5},{7,6},{8,11},{9,8},{10,9... | collective-permute-start | bytes 196616 | tf_op jit(solution)/shard_map/ppermute | solution.py:31
  32.2 12.3 %copy-start.2 = (s32[128]{0:T(128)S(1)}, s32[128]{0:T(128)}, u32[]{:S(2)}) copy-start(s32[128]{0:T(128)} %param.7) | copy-start | bytes 1540
  33.6 6.9 %collective-permute-start.7 = (s16[128,256]{1,0:T(8,128)(2,1)S(1)}, s16[128,256]{1,0:T(8,128)(2,1)S(1)}, u32[]{:S(2)}, u32[]{:S(2)}) collective-permute-start(s16[128,256]{1,0:T(8,128)(2,1)S(1)} %get-tuple-element.53), channel_id=1, source_target_pairs={{0,1},{1,2},{2,3},{3,0},{4,5},{5,6},{6,7},{7,4},{8,9},{9,10},{10,1... | collective-permute-start | bytes 196616 | tf_op jit(solution)/shard_map/ppermute | solution.py:31
  35.4 6.4 %collective-permute-start.9 = (s16[128,256]{1,0:T(8,128)(2,1)S(1)}, s16[128,256]{1,0:T(8,128)(2,1)S(1)}, u32[]{:S(2)}, u32[]{:S(2)}) collective-permute-start(s16[128,256]{1,0:T(8,128)(2,1)S(1)} %get-tuple-element.56), channel_id=1, source_target_pairs={{0,2},{1,3},{2,0},{3,1},{4,6},{5,7},{6,4},{7,5},{8,10},{9,11},{10,... | collective-permute-start | bytes 196616 | tf_op jit(solution)/shard_map/ppermute | solution.py:31
  36.5 5.3 %collective-permute-start.11 = (s16[128,256]{1,0:T(8,128)(2,1)S(1)}, s16[128,256]{1,0:T(8,128)(2,1)S(1)}, u32[]{:S(2)}, u32[]{:S(2)}) collective-permute-start(s16[128,256]{1,0:T(8,128)(2,1)S(1)} %get-tuple-element.59), channel_id=1, source_target_pairs={{0,3},{1,0},{2,1},{3,2},{4,7},{5,4},{6,5},{7,6},{8,11},{9,8},{10,9... | collective-permute-start | bytes 196616 | tf_op jit(solution)/shard_map/ppermute | solution.py:31
  38.4 8.9 %collective-permute-start.12 = (bf16[512,512]{1,0:T(8,128)(2,1)S(1)}, bf16[512,512]{1,0:T(8,128)(2,1)S(1)}, u32[]{:S(2)}, u32[]{:S(2)}) collective-permute-start(bf16[512,512]{1,0:T(8,128)(2,1)S(1)} %copy-done.3), channel_id=1, source_target_pairs={{4,0},{8,4},{12,8},{16,12},{20,16},{24,20},{28,24},{5,1},{9,5},{13... | collective-permute-start | bytes 1572872 | tf_op jit(solution)/shard_map/ppermute | solution.py:19
  42.5 7.2 %collective-permute-start.13 = (bf16[128,512]{1,0:T(8,128)(2,1)S(1)}, bf16[128,512]{1,0:T(8,128)(2,1)S(1)}, u32[]{:S(2)}, u32[]{:S(2)}) collective-permute-start(bf16[128,512]{1,0:T(8,128)(2,1)S(1)} %convolution_convert_fusion), channel_id=1, source_target_pairs={{0,4},{4,8},{8,12},{12,16},{16,20},{20,24},{24,28},{1,5},{5,9},{9,... | collective-permute-start | bytes 393224 | tf_op jit(solution)/shard_map/ppermute | solution.py:19

commit v7 on v6

--- a/solution.py
+++ b/solution.py
@@ -8,7 +8,6 @@
 from jax.sharding import PartitionSpec as P
 
 UNIT = 32000.0
-COST_T, COST_O, COST_F, COST_S, COST_H = 2.0, 2.5, 2.5, 2.0, 1.0
 LANES = 128
 CODE_ROWS = 8
 
@@ -82,7 +81,7 @@
     return squared - (1.0 - squared) / (count_all - 2.0)
 
 
-def kernel_call(kernel, out_shape, operands, in_specs=None, grid=None, scratch=(), cost=0.0):
+def kernel_call(kernel, out_shape, operands, in_specs=None, grid=None, scratch=()):
     in_specs = in_specs or [None] * len(operands)
     whole = pl.BlockSpec(memory_space=pltpu.VMEM)
     extra = {} if grid is None else {"grid": grid}
@@ -92,7 +91,6 @@
         in_specs=[spec or whole for spec in in_specs],
         scratch_shapes=list(scratch),
         compiler_params=pltpu.CompilerParams(vmem_limit_bytes=36 * 1024 * 1024),
-        cost_estimate=pl.CostEstimate(flops=0, bytes_accessed=int(cost * 3.7e6), transcendentals=0),
         **extra,
     )(*operands)
 
@@ -187,7 +185,6 @@
         (place, genotypes),
         [scalar, None],
         scratch=[pltpu.VMEM((stripe, stripe), jnp.float32)],
-        cost=COST_O,
     )
     own_terms = exchanged(own_slabs, "ind")
     above_second = shifted(after(second, scale), "snp", -1)
@@ -198,10 +195,9 @@
         (place, genotypes, above_first, scale),
         [scalar, None, None, None],
         scratch=[pltpu.VMEM((stripe, half), jnp.float32)],
-        cost=COST_F,
     )
     first_terms = exchanged([after(slab, own_terms[2]) for slab in first_slabs], "ind")
-    annot_above = shifted(after(annotations, own_terms[1]), "snp", -1)
+    annot_above = shifted(after(annotations, scale), "snp", -1)
 
     code = pl.BlockSpec((CODE_ROWS, stripe), lambda i: (sub_rows // CODE_ROWS, 0))
     info_rows = -(-(groups + 2) // 8) * 8
@@ -211,11 +207,10 @@
         (window_start[None], *(after(term, corner) for term in own_terms)),
         [None] + [code] * groups,
         grid=(1,),
-        cost=COST_H,
     )
     above = shifted(shares, "snp", -1)
 
-    above_second = after(above_second, first_terms[1])
+    above_second = after(above_second, shares, first_terms[1])
     second_slabs = kernel_call(
         functools.partial(second_kernel, groups),
         slab_shapes(sub_rows, half),
@@ -229,7 +224,6 @@
         ],
         grid=(1,),
         scratch=[pltpu.VMEM((stripe, half), jnp.float32)],
-        cost=COST_S,
     )
     second_terms = exchanged(second_slabs, "ind")
 

time: 50.9 us -> 50.9 us (level)
  starting transfers between devices: 27.8 us -> 26.8 us
  waiting for transfers between devices: 9.31 us -> 10.2 us
    ppermute x5, waiting for transfers between devices: 4.51 us -> 5.73 us  [shifted(): return lax.ppermute(array, axis, pairs)]
    ppermute x9, starting transfers between devices: 16.1 us -> 15.2 us  [exchanged(): terms[by] = lax.ppermute(slabs[by], axis, pairs)]
  transfers between devices with their start and end apart: 14 -> 14, of which waited for: 8 -> 7; matrix products, arithmetic and copies ran while one was open for 5% -> 5% of each run, Pallas kernels for 15% -> 15%
where the time goes in v7:
time: 50.9 us; the launch traced here: 50.6 us
  starting transfers between devices  26.8 us (53%)
  waiting for transfers between devices  10.2 us (20%)
  Pallas kernels  7.42 us (15%)
  matrix products  2.71 us (5%)
  local copies, waits for them, and re-layouts  2.46 us (5%)
  other arithmetic  0.77 us (2%)
    ppermute x9, starting transfers between devices, exchanged(): terms[by] = lax.ppermute(slabs[by], axis, pairs)  15.2 us
    ppermute x5, starting transfers between devices, shifted(): return lax.ppermute(array, axis, pairs)  11.7 us
    pallas_call x4, Pallas kernels, kernel_call(): pl.pallas_call(kernel, out_shape=out_shape, in_specs=[spec or whole for s...  7.42 us
    ppermute x5, waiting for transfers between devices, shifted(): return lax.ppermute(array, axis, pairs)  5.73 us
    ppermute x9, waiting for transfers between devices, exchanged(): terms[by] = lax.ppermute(slabs[by], axis, pairs)  4.43 us
    slice x1, local copies, waits for them, and re-layouts, per_device(): above_first = shifted(genotypes[:, :half], 'snp', -1)  2.41 us
    dot_general x1, matrix products, per_device(): jnp.dot(own_weights, annotations, preferred_element_type=jnp.float32)  1.46 us
  transfers between devices with their start and end apart: 14, of which 7 were waited for; matrix products, arithmetic and copies ran while one was open for 5% of the time, Pallas kernels for 15%

profile of v7, /device:TPU:4, one launch (start us, length us, event | category | flops | bytes accessed | tf_op | source)
XLA Modules:
  0.0 50.6 jit_solution(4440400740011076431)
XLA Ops:
  0.0 2.4 %slice.78 = bf16[2048,256]{1,0:T(8,128)(2,1)} slice(bf16[2048,512]{1,0:T(8,128)(2,1)} %left.3), slice={[0:2048], [0:256]} | slice | bytes 2097152 | tf_op jit(solution)/shard_map/slice | solution.py:177
  2.4 2.8 %collective-permute-start = (bf16[2048,256]{1,0:T(8,128)(2,1)}, bf16[2048,256]{1,0:T(8,128)(2,1)}, u32[]{:S(2)}, u32[]{:S(2)}) collective-permute-start(bf16[2048,256]{1,0:T(8,128)(2,1)} %slice.78), channel_id=1, source_target_pairs={{4,0},{8,4},{12,8},{16,12},{20,16},{24,20},{28,24},{5,1},{9,5},{13... | collective-permute-start | bytes 3145736 | tf_op jit(solution)/shard_map/ppermute | solution.py:18
  5.3 3.1 %shard_map.46 = (bf16[2048,256]{1,0:T(8,128)(2,1)}, f32[1,512]{1,0:T(1,128)S(1)}, s16[136,512]{1,0:T(8,128)(2,1)S(1)}, s16[136,512]{1,0:T(8,128)(2,1)}, s16[136,...) custom-call(s32[2]{0:T(128)S(1)} %pad_add_fusion.place, bf16[2048,512]{1,0:T(8,128)(2,1)S(1)} %copy-done), custom_call_target="tpu_custom_call" | custom-call | tf_op jit(solution)/shard_map/pallas_call | solution.py:88
  8.4 1.6 %collective-permute-start.1 = (s16[136,512]{1,0:T(8,128)(2,1)}, s16[136,512]{1,0:T(8,128)(2,1)S(1)}, u32[]{:S(2)}, u32[]{:S(2)}) collective-permute-start(s16[136,512]{1,0:T(8,128)(2,1)} %get-tuple-element.37), channel_id=1, source_target_pairs={{0,1},{1,2},{2,3},{3,0},{4,5},{5,6},{6,7},{7,4},{8,9},{9,10},{10,1... | collective-permute-start | bytes 417800 | tf_op jit(solution)/shard_map/ppermute | solution.py:30
  10.0 2.6 %collective-permute-start.2 = (s16[136,512]{1,0:T(8,128)(2,1)}, s16[136,512]{1,0:T(8,128)(2,1)}, u32[]{:S(2)}, u32[]{:S(2)}) collective-permute-start(s16[136,512]{1,0:T(8,128)(2,1)} %get-tuple-element.39), channel_id=1, source_target_pairs={{0,2},{1,3},{2,0},{3,1},{4,6},{5,7},{6,4},{7,5},{8,10},{9,11},{10,... | collective-permute-start | bytes 417800 | tf_op jit(solution)/shard_map/ppermute | solution.py:30
  12.6 1.3 %collective-permute-start.3 = (s16[136,512]{1,0:T(8,128)(2,1)}, s16[136,512]{1,0:T(8,128)(2,1)}, u32[]{:S(2)}, u32[]{:S(2)}) collective-permute-start(s16[136,512]{1,0:T(8,128)(2,1)} %get-tuple-element.41), channel_id=1, source_target_pairs={{0,3},{1,0},{2,1},{3,2},{4,7},{5,4},{6,5},{7,6},{8,11},{9,8},{10,9... | collective-permute-start | bytes 417800 | tf_op jit(solution)/shard_map/ppermute | solution.py:30
  13.9 1.9 %collective-permute-start.4 = (bf16[2048,256]{1,0:T(8,128)(2,1)}, bf16[2048,256]{1,0:T(8,128)(2,1)S(1)}, u32[]{:S(2)}, u32[]{:S(2)}) collective-permute-start(bf16[2048,256]{1,0:T(8,128)(2,1)} %get-tuple-element.48), channel_id=1, source_target_pairs={{4,0},{8,4},{12,8},{16,12},{20,16},{24,20},{28,24},{5,1},{9,5},{13... | collective-permute-start | bytes 3145736 | tf_op jit(solution)/shard_map/ppermute | solution.py:18
  15.9 1.9 %collective-permute-done.right = bf16[2048,256]{1,0:T(8,128)(2,1)} collective-permute-done((bf16[2048,256]{1,0:T(8,128)(2,1)}, bf16[2048,256]{1,0:T(8,128)(2,1)}, u32[]{:S(2)}, u32[]{:S(2)}) %collective-permute-start) | collective-permute-done | bytes 1048608 | tf_op jit(solution)/shard_map/ppermute | solution.py:18
  17.8 2.1 %shard_map.47 = (f32[256,256]{1,0:T(8,128)S(1)}, s16[128,256]{1,0:T(8,128)(2,1)S(1)}, s16[128,256]{1,0:T(8,128)(2,1)S(1)}, s16[128,256]{1,0:T(8,128)(2,1)S(1)}, s16[128,256]{1,0:T(8,128)(2,1)S(1)}) custom-call(s32[2]{0:T(128)S(1)} %pad_add_fusion.place, bf16[2048,512]{1,0:T(8,128)(2,1)S(1)} %copy-done, bf16[2048,256]{1,0:T(8,128)(2,1)} %collective-permute-done.right, ...), custom_call_target="tpu_custom_call" | custom-call | tf_op jit(solution)/shard_map/pallas_call | solution.py:88
  20.0 1.9 %collective-permute-done.2.rest_2_ = s16[136,512]{1,0:T(8,128)(2,1)} collective-permute-done((s16[136,512]{1,0:T(8,128)(2,1)}, s16[136,512]{1,0:T(8,128)(2,1)}, u32[]{:S(2)}, u32[]{:S(2)}) %collective-permute-start.2) | collective-permute-done | bytes 139296 | tf_op jit(solution)/shard_map/ppermute | solution.py:30
  22.8 3.1 %collective-permute-start.6 = (f32[8,512]{1,0:T(8,128)S(1)}, f32[8,512]{1,0:T(8,128)S(1)}, u32[]{:S(2)}, u32[]{:S(2)}) collective-permute-start(f32[8,512]{1,0:T(8,128)S(1)} %get-tuple-element.44), channel_id=1, source_target_pairs={{4,0},{8,4},{12,8},{16,12},{20,16},{24,20},{28,24},{5,1},{9,5},{13... | collective-permute-start | bytes 49160 | tf_op jit(solution)/shard_map/ppermute | solution.py:18
  26.0 3.3 %collective-permute-start.5 = (s16[128,256]{1,0:T(8,128)(2,1)S(1)}, s16[128,256]{1,0:T(8,128)(2,1)S(1)}, u32[]{:S(2)}, u32[]{:S(2)}) collective-permute-start(s16[128,256]{1,0:T(8,128)(2,1)S(1)} %get-tuple-element.50), channel_id=1, source_target_pairs={{0,1},{1,2},{2,3},{3,0},{4,5},{5,6},{6,7},{7,4},{8,9},{9,10},{10,1... | collective-permute-start | bytes 196616 | tf_op jit(solution)/shard_map/ppermute | solution.py:30
  29.3 1.3 %collective-permute-start.8 = (s16[128,256]{1,0:T(8,128)(2,1)S(1)}, s16[128,256]{1,0:T(8,128)(2,1)S(1)}, u32[]{:S(2)}, u32[]{:S(2)}) collective-permute-start(s16[128,256]{1,0:T(8,128)(2,1)S(1)} %get-tuple-element.55), channel_id=1, source_target_pairs={{0,2},{1,3},{2,0},{3,1},{4,6},{5,7},{6,4},{7,5},{8,10},{9,11},{10,... | collective-permute-start | bytes 196616 | tf_op jit(solution)/shard_map/ppermute | solution.py:30
  30.6 1.1 %collective-permute-start.10 = (s16[128,256]{1,0:T(8,128)(2,1)S(1)}, s16[128,256]{1,0:T(8,128)(2,1)S(1)}, u32[]{:S(2)}, u32[]{:S(2)}) collective-permute-start(s16[128,256]{1,0:T(8,128)(2,1)S(1)} %get-tuple-element.58), channel_id=1, source_target_pairs={{0,3},{1,0},{2,1},{3,2},{4,7},{5,4},{6,5},{7,6},{8,11},{9,8},{10,9... | collective-permute-start | bytes 196616 | tf_op jit(solution)/shard_map/ppermute | solution.py:30
  33.0 1.2 %shard_map.49 = (s16[128,256]{1,0:T(8,128)(2,1)S(1)}, s16[128,256]{1,0:T(8,128)(2,1)S(1)}, s16[128,256]{1,0:T(8,128)(2,1)S(1)}, s16[128,256]{1,0:T(8,128)(2,1)S(1)}) custom-call(s32[2]{0:T(128)S(1)} %pad_add_fusion.place, bf16[2048,512]{1,0:T(8,128)(2,1)S(1)} %copy-done, bf16[2048,256]{1,0:T(8,128)(2,1)S(1)} %collective-permute-done.4.right, ...), custom_call_target="tpu_custom_call" | custom-call | tf_op jit(solution)/shard_map/pallas_call | solution.py:88
  34.2 1.4 %collective-permute-start.7 = (s16[128,256]{1,0:T(8,128)(2,1)S(1)}, s16[128,256]{1,0:T(8,128)(2,1)S(1)}, u32[]{:S(2)}, u32[]{:S(2)}) collective-permute-start(s16[128,256]{1,0:T(8,128)(2,1)S(1)} %get-tuple-element.53), channel_id=1, source_target_pairs={{0,1},{1,2},{2,3},{3,0},{4,5},{5,6},{6,7},{7,4},{8,9},{9,10},{10,1... | collective-permute-start | bytes 196616 | tf_op jit(solution)/shard_map/ppermute | solution.py:30
  35.6 1.2 %collective-permute-start.9 = (s16[128,256]{1,0:T(8,128)(2,1)S(1)}, s16[128,256]{1,0:T(8,128)(2,1)S(1)}, u32[]{:S(2)}, u32[]{:S(2)}) collective-permute-start(s16[128,256]{1,0:T(8,128)(2,1)S(1)} %get-tuple-element.56), channel_id=1, source_target_pairs={{0,2},{1,3},{2,0},{3,1},{4,6},{5,7},{6,4},{7,5},{8,10},{9,11},{10,... | collective-permute-start | bytes 196616 | tf_op jit(solution)/shard_map/ppermute | solution.py:30
  36.7 1.3 %collective-permute-start.11 = (s16[128,256]{1,0:T(8,128)(2,1)S(1)}, s16[128,256]{1,0:T(8,128)(2,1)S(1)}, u32[]{:S(2)}, u32[]{:S(2)}) collective-permute-start(s16[128,256]{1,0:T(8,128)(2,1)S(1)} %get-tuple-element.59), channel_id=1, source_target_pairs={{0,3},{1,0},{2,1},{3,2},{4,7},{5,4},{6,5},{7,6},{8,11},{9,8},{10,9... | collective-permute-start | bytes 196616 | tf_op jit(solution)/shard_map/ppermute | solution.py:30
  38.1 1.9 %collective-permute-start.12 = (bf16[512,512]{1,0:T(8,128)(2,1)S(1)}, bf16[512,512]{1,0:T(8,128)(2,1)S(1)}, u32[]{:S(2)}, u32[]{:S(2)}) collective-permute-start(bf16[512,512]{1,0:T(8,128)(2,1)S(1)} %copy-done.3), channel_id=1, source_target_pairs={{4,0},{8,4},{12,8},{16,12},{20,16},{24,20},{28,24},{5,1},{9,5},{13... | collective-permute-start | bytes 1572872 | tf_op jit(solution)/shard_map/ppermute | solution.py:18
  40.3 1.4 %collective-permute-done.9 = s16[128,256]{1,0:T(8,128)(2,1)S(1)} collective-permute-done((s16[128,256]{1,0:T(8,128)(2,1)S(1)}, s16[128,256]{1,0:T(8,128)(2,1)S(1)}, u32[]{:S(2)}, u32[]{:S(2)}) %collective-permute-start.9) | collective-permute-done | bytes 65568 | tf_op jit(solution)/shard_map/ppermute | solution.py:30
  42.4 1.9 %collective-permute-start.13 = (bf16[128,512]{1,0:T(8,128)(2,1)S(1)}, bf16[128,512]{1,0:T(8,128)(2,1)S(1)}, u32[]{:S(2)}, u32[]{:S(2)}) collective-permute-start(bf16[128,512]{1,0:T(8,128)(2,1)S(1)} %convolution_convert_fusion), channel_id=1, source_target_pairs={{0,4},{4,8},{8,12},{12,16},{16,20},{20,24},{24,28},{1,5},{5,9},{9,... | collective-permute-start | bytes 393224 | tf_op jit(solution)/shard_map/ppermute | solution.py:18
  44.3 1.5 %fusion.13 = f32[128,512]{1,0:T(8,128)S(1)} fusion(bf16[512,512]{1,0:T(8,128)(2,1)S(1)} %copy-done.3, s16[136,512]{1,0:T(8,128)(2,1)} %collective-permute-done.3.rest_3_, s16[136,512]{1,0:T(8,128)(2,1)} %collective-permute-done.2.rest_2_, s16[136,512]{1,0:T(8,128)(2,1)S(1)} %collective-permute-done.1.rest_1_, f32[128]{0:T(128)S(1)} %get-tuple-element.65, ...), kind=kOutput, calls=%fused_computation.17 | convolution fusion | flops 68747264 | bytes 1324544 | tf_op jit(solution)/shard_map/dot_general | solution.py:253
  46.7 2.9 %collective-permute-done.13 = bf16[128,512]{1,0:T(8,128)(2,1)S(1)} collective-permute-done((bf16[128,512]{1,0:T(8,128)(2,1)S(1)}, bf16[128,512]{1,0:T(8,128)(2,1)S(1)}, u32[]{:S(2)}, u32[]{:S(2)}) %collective-permute-start.13) | collective-permute-done | bytes 131104 | tf_op jit(solution)/shard_map/ppermute | solution.py:18
  49.6 1.0 %fusion = f32[128,512]{1,0:T(8,128)} fusion(f32[128,512]{1,0:T(8,128)S(1)} %fusion.13, bf16[512,512]{1,0:T(8,128)(2,1)S(1)} %collective-permute-done.12, bf16[128,512]{1,0:T(8,128)(2,1)S(1)} %collective-permute-done.13, bf16[128,512]{1,0:T(8,128)(2,1)S(1)} %subtract_convert_fusion, s32[128]{0:T(128)S(1)} %iota_add_fusion.1, s32[512]{0:T(512)S(1)} %broadcast_add_fusion, ...), kind=kOutput, calls=%fused_computation.1 | convolution fusion | flops 67567616 | bytes 1313792 | tf_op jit(solution)/shard_map/dot_general | solution.py:269
  (31 shorter events, 4.1 us)
Async XLA Ops:
  0.0 5.3 %copy-start = (bf16[2048,512]{1,0:T(8,128)(2,1)S(1)}, bf16[2048,512]{1,0:T(8,128)(2,1)}, u32[]{:S(2)}) copy-start(bf16[2048,512]{1,0:T(8,128)(2,1)} %left.3) | copy-start | bytes 6291460
  2.4 15.4 %collective-permute-start = (bf16[2048,256]{1,0:T(8,128)(2,1)}, bf16[2048,256]{1,0:T(8,128)(2,1)}, u32[]{:S(2)}, u32[]{:S(2)}) collective-permute-start(bf16[2048,256]{1,0:T(8,128)(2,1)} %slice.78), channel_id=1, source_target_pairs={{4,0},{8,4},{12,8},{16,12},{20,16},{24,20},{28,24},{5,1},{9,5},{13... | collective-permute-start | bytes 3145736 | tf_op jit(solution)/shard_map/ppermute | solution.py:18
  8.4 13.5 %copy-start.1 = (s32[128]{0:T(128)S(1)}, s32[128]{0:T(128)}, u32[]{:S(2)}) copy-start(s32[128]{0:T(128)} %param.6) | copy-start | bytes 1540
  8.4 11.6 %collective-permute-start.1 = (s16[136,512]{1,0:T(8,128)(2,1)}, s16[136,512]{1,0:T(8,128)(2,1)S(1)}, u32[]{:S(2)}, u32[]{:S(2)}) collective-permute-start(s16[136,512]{1,0:T(8,128)(2,1)} %get-tuple-element.37), channel_id=1, source_target_pairs={{0,1},{1,2},{2,3},{3,0},{4,5},{5,6},{6,7},{7,4},{8,9},{9,10},{10,1... | collective-permute-start | bytes 417800 | tf_op jit(solution)/shard_map/ppermute | solution.py:30
  10.0 11.9 %collective-permute-start.2 = (s16[136,512]{1,0:T(8,128)(2,1)}, s16[136,512]{1,0:T(8,128)(2,1)}, u32[]{:S(2)}, u32[]{:S(2)}) collective-permute-start(s16[136,512]{1,0:T(8,128)(2,1)} %get-tuple-element.39), channel_id=1, source_target_pairs={{0,2},{1,3},{2,0},{3,1},{4,6},{5,7},{6,4},{7,5},{8,10},{9,11},{10,... | collective-permute-start | bytes 417800 | tf_op jit(solution)/shard_map/ppermute | solution.py:30
  12.6 9.3 %collective-permute-start.3 = (s16[136,512]{1,0:T(8,128)(2,1)}, s16[136,512]{1,0:T(8,128)(2,1)}, u32[]{:S(2)}, u32[]{:S(2)}) collective-permute-start(s16[136,512]{1,0:T(8,128)(2,1)} %get-tuple-element.41), channel_id=1, source_target_pairs={{0,3},{1,0},{2,1},{3,2},{4,7},{5,4},{6,5},{7,6},{8,11},{9,8},{10,9... | collective-permute-start | bytes 417800 | tf_op jit(solution)/shard_map/ppermute | solution.py:30
  13.9 18.2 %collective-permute-start.4 = (bf16[2048,256]{1,0:T(8,128)(2,1)}, bf16[2048,256]{1,0:T(8,128)(2,1)S(1)}, u32[]{:S(2)}, u32[]{:S(2)}) collective-permute-start(bf16[2048,256]{1,0:T(8,128)(2,1)} %get-tuple-element.48), channel_id=1, source_target_pairs={{4,0},{8,4},{12,8},{16,12},{20,16},{24,20},{28,24},{5,1},{9,5},{13... | collective-permute-start | bytes 3145736 | tf_op jit(solution)/shard_map/ppermute | solution.py:18
  21.9 16.2 %copy-start.3 = (bf16[512,512]{1,0:T(8,128)(2,1)S(1)}, bf16[512,512]{1,0:T(8,128)(2,1)}, u32[]{:S(2)}) copy-start(bf16[512,512]{1,0:T(8,128)(2,1)} %param.5) | copy-start | bytes 1572868
  22.8 9.2 %collective-permute-start.6 = (f32[8,512]{1,0:T(8,128)S(1)}, f32[8,512]{1,0:T(8,128)S(1)}, u32[]{:S(2)}, u32[]{:S(2)}) collective-permute-start(f32[8,512]{1,0:T(8,128)S(1)} %get-tuple-element.44), channel_id=1, source_target_pairs={{4,0},{8,4},{12,8},{16,12},{20,16},{24,20},{28,24},{5,1},{9,5},{13... | collective-permute-start | bytes 49160 | tf_op jit(solution)/shard_map/ppermute | solution.py:18
  26.0 7.0 %collective-permute-start.5 = (s16[128,256]{1,0:T(8,128)(2,1)S(1)}, s16[128,256]{1,0:T(8,128)(2,1)S(1)}, u32[]{:S(2)}, u32[]{:S(2)}) collective-permute-start(s16[128,256]{1,0:T(8,128)(2,1)S(1)} %get-tuple-element.50), channel_id=1, source_target_pairs={{0,1},{1,2},{2,3},{3,0},{4,5},{5,6},{6,7},{7,4},{8,9},{9,10},{10,1... | collective-permute-start | bytes 196616 | tf_op jit(solution)/shard_map/ppermute | solution.py:30
  29.3 8.7 %collective-permute-start.8 = (s16[128,256]{1,0:T(8,128)(2,1)S(1)}, s16[128,256]{1,0:T(8,128)(2,1)S(1)}, u32[]{:S(2)}, u32[]{:S(2)}) collective-permute-start(s16[128,256]{1,0:T(8,128)(2,1)S(1)} %get-tuple-element.55), channel_id=1, source_target_pairs={{0,2},{1,3},{2,0},{3,1},{4,6},{5,7},{6,4},{7,5},{8,10},{9,11},{10,... | collective-permute-start | bytes 196616 | tf_op jit(solution)/shard_map/ppermute | solution.py:30
  30.6 9.4 %collective-permute-start.10 = (s16[128,256]{1,0:T(8,128)(2,1)S(1)}, s16[128,256]{1,0:T(8,128)(2,1)S(1)}, u32[]{:S(2)}, u32[]{:S(2)}) collective-permute-start(s16[128,256]{1,0:T(8,128)(2,1)S(1)} %get-tuple-element.58), channel_id=1, source_target_pairs={{0,3},{1,0},{2,1},{3,2},{4,7},{5,4},{6,5},{7,6},{8,11},{9,8},{10,9... | collective-permute-start | bytes 196616 | tf_op jit(solution)/shard_map/ppermute | solution.py:30
  32.1 12.2 %copy-start.2 = (s32[128]{0:T(128)S(1)}, s32[128]{0:T(128)}, u32[]{:S(2)}) copy-start(s32[128]{0:T(128)} %param.7) | copy-start | bytes 1540
  34.2 6.1 %collective-permute-start.7 = (s16[128,256]{1,0:T(8,128)(2,1)S(1)}, s16[128,256]{1,0:T(8,128)(2,1)S(1)}, u32[]{:S(2)}, u32[]{:S(2)}) collective-permute-start(s16[128,256]{1,0:T(8,128)(2,1)S(1)} %get-tuple-element.53), channel_id=1, source_target_pairs={{0,1},{1,2},{2,3},{3,0},{4,5},{5,6},{6,7},{7,4},{8,9},{9,10},{10,1... | collective-permute-start | bytes 196616 | tf_op jit(solution)/shard_map/ppermute | solution.py:30
  35.6 6.1 %collective-permute-start.9 = (s16[128,256]{1,0:T(8,128)(2,1)S(1)}, s16[128,256]{1,0:T(8,128)(2,1)S(1)}, u32[]{:S(2)}, u32[]{:S(2)}) collective-permute-start(s16[128,256]{1,0:T(8,128)(2,1)S(1)} %get-tuple-element.56), channel_id=1, source_target_pairs={{0,2},{1,3},{2,0},{3,1},{4,6},{5,7},{6,4},{7,5},{8,10},{9,11},{10,... | collective-permute-start | bytes 196616 | tf_op jit(solution)/shard_map/ppermute | solution.py:30
  36.7 5.0 %collective-permute-start.11 = (s16[128,256]{1,0:T(8,128)(2,1)S(1)}, s16[128,256]{1,0:T(8,128)(2,1)S(1)}, u32[]{:S(2)}, u32[]{:S(2)}) collective-permute-start(s16[128,256]{1,0:T(8,128)(2,1)S(1)} %get-tuple-element.59), channel_id=1, source_target_pairs={{0,3},{1,0},{2,1},{3,2},{4,7},{5,4},{6,5},{7,6},{8,11},{9,8},{10,9... | collective-permute-start | bytes 196616 | tf_op jit(solution)/shard_map/ppermute | solution.py:30
  38.1 8.6 %collective-permute-start.12 = (bf16[512,512]{1,0:T(8,128)(2,1)S(1)}, bf16[512,512]{1,0:T(8,128)(2,1)S(1)}, u32[]{:S(2)}, u32[]{:S(2)}) collective-permute-start(bf16[512,512]{1,0:T(8,128)(2,1)S(1)} %copy-done.3), channel_id=1, source_target_pairs={{4,0},{8,4},{12,8},{16,12},{20,16},{24,20},{28,24},{5,1},{9,5},{13... | collective-permute-start | bytes 1572872 | tf_op jit(solution)/shard_map/ppermute | solution.py:18
  42.4 7.2 %collective-permute-start.13 = (bf16[128,512]{1,0:T(8,128)(2,1)S(1)}, bf16[128,512]{1,0:T(8,128)(2,1)S(1)}, u32[]{:S(2)}, u32[]{:S(2)}) collective-permute-start(bf16[128,512]{1,0:T(8,128)(2,1)S(1)} %convolution_convert_fusion), channel_id=1, source_target_pairs={{0,4},{4,8},{8,12},{12,16},{16,20},{20,24},{24,28},{1,5},{5,9},{9,... | collective-permute-start | bytes 393224 | tf_op jit(solution)/shard_map/ppermute | solution.py:18

commit v8 on v7

--- a/solution.py
+++ b/solution.py
@@ -25,7 +25,7 @@
 def exchanged(slabs, axis):
     devices = lax.axis_size(axis)
     terms = [slabs[0]] * devices
-    for by in range(1, devices):
+    for by in reversed(range(1, devices)):
         pairs = [(i, (i + by) % devices) for i in range(devices)]
         terms[by] = lax.ppermute(slabs[by], axis, pairs)
     return terms
@@ -140,7 +140,8 @@
     slabs, values = rest[:groups], rest[groups]
     half = right.shape[1]
     values[:half] = corner[...].T
-    values[half:] = mirrored_lower(scaled_product(left[...], right[...], left_scale[...]))
+    product = scaled_product(left[:, half:], right[...], left_scale[:, half:])
+    values[half:] = mirrored_lower(product)
     write_slabs(place[0], values, slabs)
 
 
@@ -215,14 +216,7 @@
         functools.partial(second_kernel, groups),
         slab_shapes(sub_rows, half),
         (place, genotypes, above_second, scale, corner),
-        [
-            scalar,
-            pl.BlockSpec((genotypes.shape[0], half), lambda i: (0, 1)),
-            None,
-            pl.BlockSpec((1, half), lambda i: (0, 1)),
-            None,
-        ],
-        grid=(1,),
+        [scalar, None, None, None, None],
         scratch=[pltpu.VMEM((stripe, half), jnp.float32)],
     )
     second_terms = exchanged(second_slabs, "ind")

time: 50.9 us -> 50.8 us (level)
  no operation moved by 1% of the time
where the time goes in v8:
time: 50.8 us; the launch traced here: 50.6 us
  starting transfers between devices  26.8 us (53%)
  waiting for transfers between devices  10.2 us (20%)
  Pallas kernels  7.41 us (15%)
  matrix products  2.71 us (5%)
  local copies, waits for them, and re-layouts  2.46 us (5%)
  other arithmetic  0.77 us (2%)
    ppermute x9, starting transfers between devices, exchanged(): terms[by] = lax.ppermute(slabs[by], axis, pairs)  15.2 us
    ppermute x5, starting transfers between devices, shifted(): return lax.ppermute(array, axis, pairs)  11.7 us
    pallas_call x4, Pallas kernels, kernel_call(): pl.pallas_call(kernel, out_shape=out_shape, in_specs=[spec or whole for s...  7.41 us
    ppermute x5, waiting for transfers between devices, shifted(): return lax.ppermute(array, axis, pairs)  5.73 us
    ppermute x9, waiting for transfers between devices, exchanged(): terms[by] = lax.ppermute(slabs[by], axis, pairs)  4.43 us
    slice x1, local copies, waits for them, and re-layouts, per_device(): above_first = shifted(genotypes[:, :half], 'snp', -1)  2.41 us
    dot_general x1, matrix products, per_device(): jnp.dot(own_weights, annotations, preferred_element_type=jnp.float32)  1.46 us
  transfers between devices with their start and end apart: 14, of which 7 were waited for; matrix products, arithmetic and copies ran while one was open for 5% of the time, Pallas kernels for 15%

profile of v8, /device:TPU:4, one launch (start us, length us, event | category | flops | bytes accessed | tf_op | source)
XLA Modules:
  0.0 50.6 jit_solution(2878530894323056148)
XLA Ops:
  0.0 2.4 %slice.78 = bf16[2048,256]{1,0:T(8,128)(2,1)} slice(bf16[2048,512]{1,0:T(8,128)(2,1)} %left.3), slice={[0:2048], [0:256]} | slice | bytes 2097152 | tf_op jit(solution)/shard_map/slice | solution.py:178
  2.4 2.8 %collective-permute-start = (bf16[2048,256]{1,0:T(8,128)(2,1)}, bf16[2048,256]{1,0:T(8,128)(2,1)}, u32[]{:S(2)}, u32[]{:S(2)}) collective-permute-start(bf16[2048,256]{1,0:T(8,128)(2,1)} %slice.78), channel_id=1, source_target_pairs={{4,0},{8,4},{12,8},{16,12},{20,16},{24,20},{28,24},{5,1},{9,5},{13... | collective-permute-start | bytes 3145736 | tf_op jit(solution)/shard_map/ppermute | solution.py:18
  5.3 3.1 %shard_map.46 = (bf16[2048,256]{1,0:T(8,128)(2,1)}, f32[1,512]{1,0:T(1,128)S(1)}, s16[136,512]{1,0:T(8,128)(2,1)S(1)}, s16[136,512]{1,0:T(8,128)(2,1)}, s16[136,...) custom-call(s32[2]{0:T(128)S(1)} %pad_add_fusion.place, bf16[2048,512]{1,0:T(8,128)(2,1)S(1)} %copy-done), custom_call_target="tpu_custom_call" | custom-call | tf_op jit(solution)/shard_map/pallas_call | solution.py:88
  8.4 1.6 %collective-permute-start.1 = (s16[136,512]{1,0:T(8,128)(2,1)}, s16[136,512]{1,0:T(8,128)(2,1)S(1)}, u32[]{:S(2)}, u32[]{:S(2)}) collective-permute-start(s16[136,512]{1,0:T(8,128)(2,1)} %get-tuple-element.37), channel_id=1, source_target_pairs={{0,1},{1,2},{2,3},{3,0},{4,5},{5,6},{6,7},{7,4},{8,9},{9,10},{10,1... | collective-permute-start | bytes 417800 | tf_op jit(solution)/shard_map/ppermute | solution.py:30
  10.0 2.6 %collective-permute-start.2 = (s16[136,512]{1,0:T(8,128)(2,1)}, s16[136,512]{1,0:T(8,128)(2,1)}, u32[]{:S(2)}, u32[]{:S(2)}) collective-permute-start(s16[136,512]{1,0:T(8,128)(2,1)} %get-tuple-element.39), channel_id=1, source_target_pairs={{0,2},{1,3},{2,0},{3,1},{4,6},{5,7},{6,4},{7,5},{8,10},{9,11},{10,... | collective-permute-start | bytes 417800 | tf_op jit(solution)/shard_map/ppermute | solution.py:30
  12.6 1.3 %collective-permute-start.3 = (s16[136,512]{1,0:T(8,128)(2,1)}, s16[136,512]{1,0:T(8,128)(2,1)}, u32[]{:S(2)}, u32[]{:S(2)}) collective-permute-start(s16[136,512]{1,0:T(8,128)(2,1)} %get-tuple-element.41), channel_id=1, source_target_pairs={{0,3},{1,0},{2,1},{3,2},{4,7},{5,4},{6,5},{7,6},{8,11},{9,8},{10,9... | collective-permute-start | bytes 417800 | tf_op jit(solution)/shard_map/ppermute | solution.py:30
  13.9 1.9 %collective-permute-start.4 = (bf16[2048,256]{1,0:T(8,128)(2,1)}, bf16[2048,256]{1,0:T(8,128)(2,1)S(1)}, u32[]{:S(2)}, u32[]{:S(2)}) collective-permute-start(bf16[2048,256]{1,0:T(8,128)(2,1)} %get-tuple-element.48), channel_id=1, source_target_pairs={{4,0},{8,4},{12,8},{16,12},{20,16},{24,20},{28,24},{5,1},{9,5},{13... | collective-permute-start | bytes 3145736 | tf_op jit(solution)/shard_map/ppermute | solution.py:18
  15.9 1.9 %collective-permute-done.right = bf16[2048,256]{1,0:T(8,128)(2,1)} collective-permute-done((bf16[2048,256]{1,0:T(8,128)(2,1)}, bf16[2048,256]{1,0:T(8,128)(2,1)}, u32[]{:S(2)}, u32[]{:S(2)}) %collective-permute-start) | collective-permute-done | bytes 1048608 | tf_op jit(solution)/shard_map/ppermute | solution.py:18
  17.8 2.1 %shard_map.47 = (f32[256,256]{1,0:T(8,128)S(1)}, s16[128,256]{1,0:T(8,128)(2,1)S(1)}, s16[128,256]{1,0:T(8,128)(2,1)S(1)}, s16[128,256]{1,0:T(8,128)(2,1)S(1)}, s16[128,256]{1,0:T(8,128)(2,1)S(1)}) custom-call(s32[2]{0:T(128)S(1)} %pad_add_fusion.place, bf16[2048,512]{1,0:T(8,128)(2,1)S(1)} %copy-done, bf16[2048,256]{1,0:T(8,128)(2,1)} %collective-permute-done.right, ...), custom_call_target="tpu_custom_call" | custom-call | tf_op jit(solution)/shard_map/pallas_call | solution.py:88
  20.0 1.9 %collective-permute-done.2.rest_2_ = s16[136,512]{1,0:T(8,128)(2,1)} collective-permute-done((s16[136,512]{1,0:T(8,128)(2,1)}, s16[136,512]{1,0:T(8,128)(2,1)}, u32[]{:S(2)}, u32[]{:S(2)}) %collective-permute-start.2) | collective-permute-done | bytes 139296 | tf_op jit(solution)/shard_map/ppermute | solution.py:30
  22.8 3.1 %collective-permute-start.6 = (f32[8,512]{1,0:T(8,128)S(1)}, f32[8,512]{1,0:T(8,128)S(1)}, u32[]{:S(2)}, u32[]{:S(2)}) collective-permute-start(f32[8,512]{1,0:T(8,128)S(1)} %get-tuple-element.44), channel_id=1, source_target_pairs={{4,0},{8,4},{12,8},{16,12},{20,16},{24,20},{28,24},{5,1},{9,5},{13... | collective-permute-start | bytes 49160 | tf_op jit(solution)/shard_map/ppermute | solution.py:18
  26.0 3.3 %collective-permute-start.5 = (s16[128,256]{1,0:T(8,128)(2,1)S(1)}, s16[128,256]{1,0:T(8,128)(2,1)S(1)}, u32[]{:S(2)}, u32[]{:S(2)}) collective-permute-start(s16[128,256]{1,0:T(8,128)(2,1)S(1)} %get-tuple-element.50), channel_id=1, source_target_pairs={{0,1},{1,2},{2,3},{3,0},{4,5},{5,6},{6,7},{7,4},{8,9},{9,10},{10,1... | collective-permute-start | bytes 196616 | tf_op jit(solution)/shard_map/ppermute | solution.py:30
  29.3 1.3 %collective-permute-start.8 = (s16[128,256]{1,0:T(8,128)(2,1)S(1)}, s16[128,256]{1,0:T(8,128)(2,1)S(1)}, u32[]{:S(2)}, u32[]{:S(2)}) collective-permute-start(s16[128,256]{1,0:T(8,128)(2,1)S(1)} %get-tuple-element.55), channel_id=1, source_target_pairs={{0,2},{1,3},{2,0},{3,1},{4,6},{5,7},{6,4},{7,5},{8,10},{9,11},{10,... | collective-permute-start | bytes 196616 | tf_op jit(solution)/shard_map/ppermute | solution.py:30
  30.6 1.1 %collective-permute-start.10 = (s16[128,256]{1,0:T(8,128)(2,1)S(1)}, s16[128,256]{1,0:T(8,128)(2,1)S(1)}, u32[]{:S(2)}, u32[]{:S(2)}) collective-permute-start(s16[128,256]{1,0:T(8,128)(2,1)S(1)} %get-tuple-element.58), channel_id=1, source_target_pairs={{0,3},{1,0},{2,1},{3,2},{4,7},{5,4},{6,5},{7,6},{8,11},{9,8},{10,9... | collective-permute-start | bytes 196616 | tf_op jit(solution)/shard_map/ppermute | solution.py:30
  33.0 1.2 %shard_map.49 = (s16[128,256]{1,0:T(8,128)(2,1)S(1)}, s16[128,256]{1,0:T(8,128)(2,1)S(1)}, s16[128,256]{1,0:T(8,128)(2,1)S(1)}, s16[128,256]{1,0:T(8,128)(2,1)S(1)}) custom-call(s32[2]{0:T(128)S(1)} %pad_add_fusion.place, bf16[2048,512]{1,0:T(8,128)(2,1)S(1)} %copy-done, bf16[2048,256]{1,0:T(8,128)(2,1)S(1)} %collective-permute-done.4.right, ...), custom_call_target="tpu_custom_call" | custom-call | tf_op jit(solution)/shard_map/pallas_call | solution.py:88
  34.2 1.4 %collective-permute-start.7 = (s16[128,256]{1,0:T(8,128)(2,1)S(1)}, s16[128,256]{1,0:T(8,128)(2,1)S(1)}, u32[]{:S(2)}, u32[]{:S(2)}) collective-permute-start(s16[128,256]{1,0:T(8,128)(2,1)S(1)} %get-tuple-element.53), channel_id=1, source_target_pairs={{0,1},{1,2},{2,3},{3,0},{4,5},{5,6},{6,7},{7,4},{8,9},{9,10},{10,1... | collective-permute-start | bytes 196616 | tf_op jit(solution)/shard_map/ppermute | solution.py:30
  35.6 1.2 %collective-permute-start.9 = (s16[128,256]{1,0:T(8,128)(2,1)S(1)}, s16[128,256]{1,0:T(8,128)(2,1)S(1)}, u32[]{:S(2)}, u32[]{:S(2)}) collective-permute-start(s16[128,256]{1,0:T(8,128)(2,1)S(1)} %get-tuple-element.56), channel_id=1, source_target_pairs={{0,2},{1,3},{2,0},{3,1},{4,6},{5,7},{6,4},{7,5},{8,10},{9,11},{10,... | collective-permute-start | bytes 196616 | tf_op jit(solution)/shard_map/ppermute | solution.py:30
  36.7 1.3 %collective-permute-start.11 = (s16[128,256]{1,0:T(8,128)(2,1)S(1)}, s16[128,256]{1,0:T(8,128)(2,1)S(1)}, u32[]{:S(2)}, u32[]{:S(2)}) collective-permute-start(s16[128,256]{1,0:T(8,128)(2,1)S(1)} %get-tuple-element.59), channel_id=1, source_target_pairs={{0,3},{1,0},{2,1},{3,2},{4,7},{5,4},{6,5},{7,6},{8,11},{9,8},{10,9... | collective-permute-start | bytes 196616 | tf_op jit(solution)/shard_map/ppermute | solution.py:30
  38.1 1.9 %collective-permute-start.12 = (bf16[512,512]{1,0:T(8,128)(2,1)S(1)}, bf16[512,512]{1,0:T(8,128)(2,1)S(1)}, u32[]{:S(2)}, u32[]{:S(2)}) collective-permute-start(bf16[512,512]{1,0:T(8,128)(2,1)S(1)} %copy-done.3), channel_id=1, source_target_pairs={{4,0},{8,4},{12,8},{16,12},{20,16},{24,20},{28,24},{5,1},{9,5},{13... | collective-permute-start | bytes 1572872 | tf_op jit(solution)/shard_map/ppermute | solution.py:18
  40.3 1.4 %collective-permute-done.9 = s16[128,256]{1,0:T(8,128)(2,1)S(1)} collective-permute-done((s16[128,256]{1,0:T(8,128)(2,1)S(1)}, s16[128,256]{1,0:T(8,128)(2,1)S(1)}, u32[]{:S(2)}, u32[]{:S(2)}) %collective-permute-start.9) | collective-permute-done | bytes 65568 | tf_op jit(solution)/shard_map/ppermute | solution.py:30
  42.4 1.9 %collective-permute-start.13 = (bf16[128,512]{1,0:T(8,128)(2,1)S(1)}, bf16[128,512]{1,0:T(8,128)(2,1)S(1)}, u32[]{:S(2)}, u32[]{:S(2)}) collective-permute-start(bf16[128,512]{1,0:T(8,128)(2,1)S(1)} %convolution_convert_fusion), channel_id=1, source_target_pairs={{0,4},{4,8},{8,12},{12,16},{16,20},{20,24},{24,28},{1,5},{5,9},{9,... | collective-permute-start | bytes 393224 | tf_op jit(solution)/shard_map/ppermute | solution.py:18
  44.3 1.5 %fusion.13 = f32[128,512]{1,0:T(8,128)S(1)} fusion(bf16[512,512]{1,0:T(8,128)(2,1)S(1)} %copy-done.3, s16[136,512]{1,0:T(8,128)(2,1)} %collective-permute-done.3.rest_3_, s16[136,512]{1,0:T(8,128)(2,1)} %collective-permute-done.2.rest_2_, s16[136,512]{1,0:T(8,128)(2,1)S(1)} %collective-permute-done.1.rest_1_, f32[128]{0:T(128)S(1)} %get-tuple-element.65, ...), kind=kOutput, calls=%fused_computation.17 | convolution fusion | flops 68747264 | bytes 1324544 | tf_op jit(solution)/shard_map/dot_general | solution.py:247
  46.7 2.9 %collective-permute-done.13 = bf16[128,512]{1,0:T(8,128)(2,1)S(1)} collective-permute-done((bf16[128,512]{1,0:T(8,128)(2,1)S(1)}, bf16[128,512]{1,0:T(8,128)(2,1)S(1)}, u32[]{:S(2)}, u32[]{:S(2)}) %collective-permute-start.13) | collective-permute-done | bytes 131104 | tf_op jit(solution)/shard_map/ppermute | solution.py:18
  49.6 1.0 %fusion = f32[128,512]{1,0:T(8,128)} fusion(f32[128,512]{1,0:T(8,128)S(1)} %fusion.13, bf16[512,512]{1,0:T(8,128)(2,1)S(1)} %collective-permute-done.12, bf16[128,512]{1,0:T(8,128)(2,1)S(1)} %collective-permute-done.13, bf16[128,512]{1,0:T(8,128)(2,1)S(1)} %subtract_convert_fusion, s32[128]{0:T(128)S(1)} %iota_add_fusion.1, s32[512]{0:T(512)S(1)} %broadcast_add_fusion, ...), kind=kOutput, calls=%fused_computation.1 | convolution fusion | flops 67567616 | bytes 1313792 | tf_op jit(solution)/shard_map/dot_general | solution.py:263
  (31 shorter events, 4.1 us)
Async XLA Ops:
  0.0 5.3 %copy-start = (bf16[2048,512]{1,0:T(8,128)(2,1)S(1)}, bf16[2048,512]{1,0:T(8,128)(2,1)}, u32[]{:S(2)}) copy-start(bf16[2048,512]{1,0:T(8,128)(2,1)} %left.3) | copy-start | bytes 6291460
  2.4 15.4 %collective-permute-start = (bf16[2048,256]{1,0:T(8,128)(2,1)}, bf16[2048,256]{1,0:T(8,128)(2,1)}, u32[]{:S(2)}, u32[]{:S(2)}) collective-permute-start(bf16[2048,256]{1,0:T(8,128)(2,1)} %slice.78), channel_id=1, source_target_pairs={{4,0},{8,4},{12,8},{16,12},{20,16},{24,20},{28,24},{5,1},{9,5},{13... | collective-permute-start | bytes 3145736 | tf_op jit(solution)/shard_map/ppermute | solution.py:18
  8.4 13.5 %copy-start.1 = (s32[128]{0:T(128)S(1)}, s32[128]{0:T(128)}, u32[]{:S(2)}) copy-start(s32[128]{0:T(128)} %param.6) | copy-start | bytes 1540
  8.4 11.6 %collective-permute-start.1 = (s16[136,512]{1,0:T(8,128)(2,1)}, s16[136,512]{1,0:T(8,128)(2,1)S(1)}, u32[]{:S(2)}, u32[]{:S(2)}) collective-permute-start(s16[136,512]{1,0:T(8,128)(2,1)} %get-tuple-element.37), channel_id=1, source_target_pairs={{0,1},{1,2},{2,3},{3,0},{4,5},{5,6},{6,7},{7,4},{8,9},{9,10},{10,1... | collective-permute-start | bytes 417800 | tf_op jit(solution)/shard_map/ppermute | solution.py:30
  10.0 11.9 %collective-permute-start.2 = (s16[136,512]{1,0:T(8,128)(2,1)}, s16[136,512]{1,0:T(8,128)(2,1)}, u32[]{:S(2)}, u32[]{:S(2)}) collective-permute-start(s16[136,512]{1,0:T(8,128)(2,1)} %get-tuple-element.39), channel_id=1, source_target_pairs={{0,2},{1,3},{2,0},{3,1},{4,6},{5,7},{6,4},{7,5},{8,10},{9,11},{10,... | collective-permute-start | bytes 417800 | tf_op jit(solution)/shard_map/ppermute | solution.py:30
  12.6 9.3 %collective-permute-start.3 = (s16[136,512]{1,0:T(8,128)(2,1)}, s16[136,512]{1,0:T(8,128)(2,1)}, u32[]{:S(2)}, u32[]{:S(2)}) collective-permute-start(s16[136,512]{1,0:T(8,128)(2,1)} %get-tuple-element.41), channel_id=1, source_target_pairs={{0,3},{1,0},{2,1},{3,2},{4,7},{5,4},{6,5},{7,6},{8,11},{9,8},{10,9... | collective-permute-start | bytes 417800 | tf_op jit(solution)/shard_map/ppermute | solution.py:30
  13.9 18.2 %collective-permute-start.4 = (bf16[2048,256]{1,0:T(8,128)(2,1)}, bf16[2048,256]{1,0:T(8,128)(2,1)S(1)}, u32[]{:S(2)}, u32[]{:S(2)}) collective-permute-start(bf16[2048,256]{1,0:T(8,128)(2,1)} %get-tuple-element.48), channel_id=1, source_target_pairs={{4,0},{8,4},{12,8},{16,12},{20,16},{24,20},{28,24},{5,1},{9,5},{13... | collective-permute-start | bytes 3145736 | tf_op jit(solution)/shard_map/ppermute | solution.py:18
  21.9 16.2 %copy-start.3 = (bf16[512,512]{1,0:T(8,128)(2,1)S(1)}, bf16[512,512]{1,0:T(8,128)(2,1)}, u32[]{:S(2)}) copy-start(bf16[512,512]{1,0:T(8,128)(2,1)} %param.5) | copy-start | bytes 1572868
  22.8 9.2 %collective-permute-start.6 = (f32[8,512]{1,0:T(8,128)S(1)}, f32[8,512]{1,0:T(8,128)S(1)}, u32[]{:S(2)}, u32[]{:S(2)}) collective-permute-start(f32[8,512]{1,0:T(8,128)S(1)} %get-tuple-element.44), channel_id=1, source_target_pairs={{4,0},{8,4},{12,8},{16,12},{20,16},{24,20},{28,24},{5,1},{9,5},{13... | collective-permute-start | bytes 49160 | tf_op jit(solution)/shard_map/ppermute | solution.py:18
  26.0 7.0 %collective-permute-start.5 = (s16[128,256]{1,0:T(8,128)(2,1)S(1)}, s16[128,256]{1,0:T(8,128)(2,1)S(1)}, u32[]{:S(2)}, u32[]{:S(2)}) collective-permute-start(s16[128,256]{1,0:T(8,128)(2,1)S(1)} %get-tuple-element.50), channel_id=1, source_target_pairs={{0,1},{1,2},{2,3},{3,0},{4,5},{5,6},{6,7},{7,4},{8,9},{9,10},{10,1... | collective-permute-start | bytes 196616 | tf_op jit(solution)/shard_map/ppermute | solution.py:30
  29.3 8.7 %collective-permute-start.8 = (s16[128,256]{1,0:T(8,128)(2,1)S(1)}, s16[128,256]{1,0:T(8,128)(2,1)S(1)}, u32[]{:S(2)}, u32[]{:S(2)}) collective-permute-start(s16[128,256]{1,0:T(8,128)(2,1)S(1)} %get-tuple-element.55), channel_id=1, source_target_pairs={{0,2},{1,3},{2,0},{3,1},{4,6},{5,7},{6,4},{7,5},{8,10},{9,11},{10,... | collective-permute-start | bytes 196616 | tf_op jit(solution)/shard_map/ppermute | solution.py:30
  30.6 9.4 %collective-permute-start.10 = (s16[128,256]{1,0:T(8,128)(2,1)S(1)}, s16[128,256]{1,0:T(8,128)(2,1)S(1)}, u32[]{:S(2)}, u32[]{:S(2)}) collective-permute-start(s16[128,256]{1,0:T(8,128)(2,1)S(1)} %get-tuple-element.58), channel_id=1, source_target_pairs={{0,3},{1,0},{2,1},{3,2},{4,7},{5,4},{6,5},{7,6},{8,11},{9,8},{10,9... | collective-permute-start | bytes 196616 | tf_op jit(solution)/shard_map/ppermute | solution.py:30
  32.1 12.2 %copy-start.2 = (s32[128]{0:T(128)S(1)}, s32[128]{0:T(128)}, u32[]{:S(2)}) copy-start(s32[128]{0:T(128)} %param.7) | copy-start | bytes 1540
  34.2 6.1 %collective-permute-start.7 = (s16[128,256]{1,0:T(8,128)(2,1)S(1)}, s16[128,256]{1,0:T(8,128)(2,1)S(1)}, u32[]{:S(2)}, u32[]{:S(2)}) collective-permute-start(s16[128,256]{1,0:T(8,128)(2,1)S(1)} %get-tuple-element.53), channel_id=1, source_target_pairs={{0,1},{1,2},{2,3},{3,0},{4,5},{5,6},{6,7},{7,4},{8,9},{9,10},{10,1... | collective-permute-start | bytes 196616 | tf_op jit(solution)/shard_map/ppermute | solution.py:30
  35.6 6.1 %collective-permute-start.9 = (s16[128,256]{1,0:T(8,128)(2,1)S(1)}, s16[128,256]{1,0:T(8,128)(2,1)S(1)}, u32[]{:S(2)}, u32[]{:S(2)}) collective-permute-start(s16[128,256]{1,0:T(8,128)(2,1)S(1)} %get-tuple-element.56), channel_id=1, source_target_pairs={{0,2},{1,3},{2,0},{3,1},{4,6},{5,7},{6,4},{7,5},{8,10},{9,11},{10,... | collective-permute-start | bytes 196616 | tf_op jit(solution)/shard_map/ppermute | solution.py:30
  36.7 5.0 %collective-permute-start.11 = (s16[128,256]{1,0:T(8,128)(2,1)S(1)}, s16[128,256]{1,0:T(8,128)(2,1)S(1)}, u32[]{:S(2)}, u32[]{:S(2)}) collective-permute-start(s16[128,256]{1,0:T(8,128)(2,1)S(1)} %get-tuple-element.59), channel_id=1, source_target_pairs={{0,3},{1,0},{2,1},{3,2},{4,7},{5,4},{6,5},{7,6},{8,11},{9,8},{10,9... | collective-permute-start | bytes 196616 | tf_op jit(solution)/shard_map/ppermute | solution.py:30
  38.1 8.6 %collective-permute-start.12 = (bf16[512,512]{1,0:T(8,128)(2,1)S(1)}, bf16[512,512]{1,0:T(8,128)(2,1)S(1)}, u32[]{:S(2)}, u32[]{:S(2)}) collective-permute-start(bf16[512,512]{1,0:T(8,128)(2,1)S(1)} %copy-done.3), channel_id=1, source_target_pairs={{4,0},{8,4},{12,8},{16,12},{20,16},{24,20},{28,24},{5,1},{9,5},{13... | collective-permute-start | bytes 1572872 | tf_op jit(solution)/shard_map/ppermute | solution.py:18
  42.4 7.2 %collective-permute-start.13 = (bf16[128,512]{1,0:T(8,128)(2,1)S(1)}, bf16[128,512]{1,0:T(8,128)(2,1)S(1)}, u32[]{:S(2)}, u32[]{:S(2)}) collective-permute-start(bf16[128,512]{1,0:T(8,128)(2,1)S(1)} %convolution_convert_fusion), channel_id=1, source_target_pairs={{0,4},{4,8},{8,12},{12,16},{16,20},{20,24},{24,28},{1,5},{5,9},{9,... | collective-permute-start | bytes 393224 | tf_op jit(solution)/shard_map/ppermute | solution.py:18

commit v9 on v7

--- a/solution.py
+++ b/solution.py
@@ -25,7 +25,7 @@
 def exchanged(slabs, axis):
     devices = lax.axis_size(axis)
     terms = [slabs[0]] * devices
-    for by in range(1, devices):
+    for by in reversed(range(1, devices)):
         pairs = [(i, (i + by) % devices) for i in range(devices)]
         terms[by] = lax.ppermute(slabs[by], axis, pairs)
     return terms

time: 50.9 us -> 50.9 us (level)
  no operation moved by 1% of the time
where the time goes in v9:
time: 50.9 us; the launch traced here: 50.6 us
  starting transfers between devices  26.8 us (53%)
  waiting for transfers between devices  10.2 us (20%)
  Pallas kernels  7.42 us (15%)
  matrix products  2.71 us (5%)
  local copies, waits for them, and re-layouts  2.46 us (5%)
  other arithmetic  0.77 us (2%)
    ppermute x9, starting transfers between devices, exchanged(): terms[by] = lax.ppermute(slabs[by], axis, pairs)  15.2 us
    ppermute x5, starting transfers between devices, shifted(): return lax.ppermute(array, axis, pairs)  11.7 us
    pallas_call x4, Pallas kernels, kernel_call(): pl.pallas_call(kernel, out_shape=out_shape, in_specs=[spec or whole for s...  7.42 us
    ppermute x5, waiting for transfers between devices, shifted(): return lax.ppermute(array, axis, pairs)  5.73 us
    ppermute x9, waiting for transfers between devices, exchanged(): terms[by] = lax.ppermute(slabs[by], axis, pairs)  4.43 us
    slice x1, local copies, waits for them, and re-layouts, per_device(): above_first = shifted(genotypes[:, :half], 'snp', -1)  2.41 us
    dot_general x1, matrix products, per_device(): jnp.dot(own_weights, annotations, preferred_element_type=jnp.float32)  1.46 us
  transfers between devices with their start and end apart: 14, of which 7 were waited for; matrix products, arithmetic and copies ran while one was open for 5% of the time, Pallas kernels for 15%

profile of v9, /device:TPU:4, one launch (start us, length us, event | category | flops | bytes accessed | tf_op | source)
XLA Modules:
  0.0 50.6 jit_solution(4440400740011076431)
XLA Ops:
  0.0 2.4 %slice.78 = bf16[2048,256]{1,0:T(8,128)(2,1)} slice(bf16[2048,512]{1,0:T(8,128)(2,1)} %left.3), slice={[0:2048], [0:256]} | slice | bytes 2097152 | tf_op jit(solution)/shard_map/slice | solution.py:177
  2.4 2.8 %collective-permute-start = (bf16[2048,256]{1,0:T(8,128)(2,1)}, bf16[2048,256]{1,0:T(8,128)(2,1)}, u32[]{:S(2)}, u32[]{:S(2)}) collective-permute-start(bf16[2048,256]{1,0:T(8,128)(2,1)} %slice.78), channel_id=1, source_target_pairs={{4,0},{8,4},{12,8},{16,12},{20,16},{24,20},{28,24},{5,1},{9,5},{13... | collective-permute-start | bytes 3145736 | tf_op jit(solution)/shard_map/ppermute | solution.py:18
  5.3 3.1 %shard_map.46 = (bf16[2048,256]{1,0:T(8,128)(2,1)}, f32[1,512]{1,0:T(1,128)S(1)}, s16[136,512]{1,0:T(8,128)(2,1)S(1)}, s16[136,512]{1,0:T(8,128)(2,1)}, s16[136,...) custom-call(s32[2]{0:T(128)S(1)} %pad_add_fusion.place, bf16[2048,512]{1,0:T(8,128)(2,1)S(1)} %copy-done), custom_call_target="tpu_custom_call" | custom-call | tf_op jit(solution)/shard_map/pallas_call | solution.py:88
  8.4 1.6 %collective-permute-start.1 = (s16[136,512]{1,0:T(8,128)(2,1)}, s16[136,512]{1,0:T(8,128)(2,1)S(1)}, u32[]{:S(2)}, u32[]{:S(2)}) collective-permute-start(s16[136,512]{1,0:T(8,128)(2,1)} %get-tuple-element.37), channel_id=1, source_target_pairs={{0,1},{1,2},{2,3},{3,0},{4,5},{5,6},{6,7},{7,4},{8,9},{9,10},{10,1... | collective-permute-start | bytes 417800 | tf_op jit(solution)/shard_map/ppermute | solution.py:30
  10.0 2.6 %collective-permute-start.2 = (s16[136,512]{1,0:T(8,128)(2,1)}, s16[136,512]{1,0:T(8,128)(2,1)}, u32[]{:S(2)}, u32[]{:S(2)}) collective-permute-start(s16[136,512]{1,0:T(8,128)(2,1)} %get-tuple-element.39), channel_id=1, source_target_pairs={{0,2},{1,3},{2,0},{3,1},{4,6},{5,7},{6,4},{7,5},{8,10},{9,11},{10,... | collective-permute-start | bytes 417800 | tf_op jit(solution)/shard_map/ppermute | solution.py:30
  12.6 1.3 %collective-permute-start.3 = (s16[136,512]{1,0:T(8,128)(2,1)}, s16[136,512]{1,0:T(8,128)(2,1)}, u32[]{:S(2)}, u32[]{:S(2)}) collective-permute-start(s16[136,512]{1,0:T(8,128)(2,1)} %get-tuple-element.41), channel_id=1, source_target_pairs={{0,3},{1,0},{2,1},{3,2},{4,7},{5,4},{6,5},{7,6},{8,11},{9,8},{10,9... | collective-permute-start | bytes 417800 | tf_op jit(solution)/shard_map/ppermute | solution.py:30
  13.9 1.9 %collective-permute-start.4 = (bf16[2048,256]{1,0:T(8,128)(2,1)}, bf16[2048,256]{1,0:T(8,128)(2,1)S(1)}, u32[]{:S(2)}, u32[]{:S(2)}) collective-permute-start(bf16[2048,256]{1,0:T(8,128)(2,1)} %get-tuple-element.48), channel_id=1, source_target_pairs={{4,0},{8,4},{12,8},{16,12},{20,16},{24,20},{28,24},{5,1},{9,5},{13... | collective-permute-start | bytes 3145736 | tf_op jit(solution)/shard_map/ppermute | solution.py:18
  15.9 1.9 %collective-permute-done.right = bf16[2048,256]{1,0:T(8,128)(2,1)} collective-permute-done((bf16[2048,256]{1,0:T(8,128)(2,1)}, bf16[2048,256]{1,0:T(8,128)(2,1)}, u32[]{:S(2)}, u32[]{:S(2)}) %collective-permute-start) | collective-permute-done | bytes 1048608 | tf_op jit(solution)/shard_map/ppermute | solution.py:18
  17.8 2.1 %shard_map.47 = (f32[256,256]{1,0:T(8,128)S(1)}, s16[128,256]{1,0:T(8,128)(2,1)S(1)}, s16[128,256]{1,0:T(8,128)(2,1)S(1)}, s16[128,256]{1,0:T(8,128)(2,1)S(1)}, s16[128,256]{1,0:T(8,128)(2,1)S(1)}) custom-call(s32[2]{0:T(128)S(1)} %pad_add_fusion.place, bf16[2048,512]{1,0:T(8,128)(2,1)S(1)} %copy-done, bf16[2048,256]{1,0:T(8,128)(2,1)} %collective-permute-done.right, ...), custom_call_target="tpu_custom_call" | custom-call | tf_op jit(solution)/shard_map/pallas_call | solution.py:88
  20.0 1.9 %collective-permute-done.2.rest_2_ = s16[136,512]{1,0:T(8,128)(2,1)} collective-permute-done((s16[136,512]{1,0:T(8,128)(2,1)}, s16[136,512]{1,0:T(8,128)(2,1)}, u32[]{:S(2)}, u32[]{:S(2)}) %collective-permute-start.2) | collective-permute-done | bytes 139296 | tf_op jit(solution)/shard_map/ppermute | solution.py:30
  22.8 3.1 %collective-permute-start.6 = (f32[8,512]{1,0:T(8,128)S(1)}, f32[8,512]{1,0:T(8,128)S(1)}, u32[]{:S(2)}, u32[]{:S(2)}) collective-permute-start(f32[8,512]{1,0:T(8,128)S(1)} %get-tuple-element.44), channel_id=1, source_target_pairs={{4,0},{8,4},{12,8},{16,12},{20,16},{24,20},{28,24},{5,1},{9,5},{13... | collective-permute-start | bytes 49160 | tf_op jit(solution)/shard_map/ppermute | solution.py:18
  26.0 3.3 %collective-permute-start.5 = (s16[128,256]{1,0:T(8,128)(2,1)S(1)}, s16[128,256]{1,0:T(8,128)(2,1)S(1)}, u32[]{:S(2)}, u32[]{:S(2)}) collective-permute-start(s16[128,256]{1,0:T(8,128)(2,1)S(1)} %get-tuple-element.50), channel_id=1, source_target_pairs={{0,1},{1,2},{2,3},{3,0},{4,5},{5,6},{6,7},{7,4},{8,9},{9,10},{10,1... | collective-permute-start | bytes 196616 | tf_op jit(solution)/shard_map/ppermute | solution.py:30
  29.3 1.3 %collective-permute-start.8 = (s16[128,256]{1,0:T(8,128)(2,1)S(1)}, s16[128,256]{1,0:T(8,128)(2,1)S(1)}, u32[]{:S(2)}, u32[]{:S(2)}) collective-permute-start(s16[128,256]{1,0:T(8,128)(2,1)S(1)} %get-tuple-element.55), channel_id=1, source_target_pairs={{0,2},{1,3},{2,0},{3,1},{4,6},{5,7},{6,4},{7,5},{8,10},{9,11},{10,... | collective-permute-start | bytes 196616 | tf_op jit(solution)/shard_map/ppermute | solution.py:30
  30.6 1.1 %collective-permute-start.10 = (s16[128,256]{1,0:T(8,128)(2,1)S(1)}, s16[128,256]{1,0:T(8,128)(2,1)S(1)}, u32[]{:S(2)}, u32[]{:S(2)}) collective-permute-start(s16[128,256]{1,0:T(8,128)(2,1)S(1)} %get-tuple-element.58), channel_id=1, source_target_pairs={{0,3},{1,0},{2,1},{3,2},{4,7},{5,4},{6,5},{7,6},{8,11},{9,8},{10,9... | collective-permute-start | bytes 196616 | tf_op jit(solution)/shard_map/ppermute | solution.py:30
  33.0 1.2 %shard_map.49 = (s16[128,256]{1,0:T(8,128)(2,1)S(1)}, s16[128,256]{1,0:T(8,128)(2,1)S(1)}, s16[128,256]{1,0:T(8,128)(2,1)S(1)}, s16[128,256]{1,0:T(8,128)(2,1)S(1)}) custom-call(s32[2]{0:T(128)S(1)} %pad_add_fusion.place, bf16[2048,512]{1,0:T(8,128)(2,1)S(1)} %copy-done, bf16[2048,256]{1,0:T(8,128)(2,1)S(1)} %collective-permute-done.4.right, ...), custom_call_target="tpu_custom_call" | custom-call | tf_op jit(solution)/shard_map/pallas_call | solution.py:88
  34.2 1.4 %collective-permute-start.7 = (s16[128,256]{1,0:T(8,128)(2,1)S(1)}, s16[128,256]{1,0:T(8,128)(2,1)S(1)}, u32[]{:S(2)}, u32[]{:S(2)}) collective-permute-start(s16[128,256]{1,0:T(8,128)(2,1)S(1)} %get-tuple-element.53), channel_id=1, source_target_pairs={{0,1},{1,2},{2,3},{3,0},{4,5},{5,6},{6,7},{7,4},{8,9},{9,10},{10,1... | collective-permute-start | bytes 196616 | tf_op jit(solution)/shard_map/ppermute | solution.py:30
  35.6 1.2 %collective-permute-start.9 = (s16[128,256]{1,0:T(8,128)(2,1)S(1)}, s16[128,256]{1,0:T(8,128)(2,1)S(1)}, u32[]{:S(2)}, u32[]{:S(2)}) collective-permute-start(s16[128,256]{1,0:T(8,128)(2,1)S(1)} %get-tuple-element.56), channel_id=1, source_target_pairs={{0,2},{1,3},{2,0},{3,1},{4,6},{5,7},{6,4},{7,5},{8,10},{9,11},{10,... | collective-permute-start | bytes 196616 | tf_op jit(solution)/shard_map/ppermute | solution.py:30
  36.7 1.3 %collective-permute-start.11 = (s16[128,256]{1,0:T(8,128)(2,1)S(1)}, s16[128,256]{1,0:T(8,128)(2,1)S(1)}, u32[]{:S(2)}, u32[]{:S(2)}) collective-permute-start(s16[128,256]{1,0:T(8,128)(2,1)S(1)} %get-tuple-element.59), channel_id=1, source_target_pairs={{0,3},{1,0},{2,1},{3,2},{4,7},{5,4},{6,5},{7,6},{8,11},{9,8},{10,9... | collective-permute-start | bytes 196616 | tf_op jit(solution)/shard_map/ppermute | solution.py:30
  38.1 1.9 %collective-permute-start.12 = (bf16[512,512]{1,0:T(8,128)(2,1)S(1)}, bf16[512,512]{1,0:T(8,128)(2,1)S(1)}, u32[]{:S(2)}, u32[]{:S(2)}) collective-permute-start(bf16[512,512]{1,0:T(8,128)(2,1)S(1)} %copy-done.3), channel_id=1, source_target_pairs={{4,0},{8,4},{12,8},{16,12},{20,16},{24,20},{28,24},{5,1},{9,5},{13... | collective-permute-start | bytes 1572872 | tf_op jit(solution)/shard_map/ppermute | solution.py:18
  40.3 1.4 %collective-permute-done.9 = s16[128,256]{1,0:T(8,128)(2,1)S(1)} collective-permute-done((s16[128,256]{1,0:T(8,128)(2,1)S(1)}, s16[128,256]{1,0:T(8,128)(2,1)S(1)}, u32[]{:S(2)}, u32[]{:S(2)}) %collective-permute-start.9) | collective-permute-done | bytes 65568 | tf_op jit(solution)/shard_map/ppermute | solution.py:30
  42.4 1.9 %collective-permute-start.13 = (bf16[128,512]{1,0:T(8,128)(2,1)S(1)}, bf16[128,512]{1,0:T(8,128)(2,1)S(1)}, u32[]{:S(2)}, u32[]{:S(2)}) collective-permute-start(bf16[128,512]{1,0:T(8,128)(2,1)S(1)} %convolution_convert_fusion), channel_id=1, source_target_pairs={{0,4},{4,8},{8,12},{12,16},{16,20},{20,24},{24,28},{1,5},{5,9},{9,... | collective-permute-start | bytes 393224 | tf_op jit(solution)/shard_map/ppermute | solution.py:18
  44.3 1.5 %fusion.13 = f32[128,512]{1,0:T(8,128)S(1)} fusion(bf16[512,512]{1,0:T(8,128)(2,1)S(1)} %copy-done.3, s16[136,512]{1,0:T(8,128)(2,1)} %collective-permute-done.3.rest_3_, s16[136,512]{1,0:T(8,128)(2,1)} %collective-permute-done.2.rest_2_, s16[136,512]{1,0:T(8,128)(2,1)S(1)} %collective-permute-done.1.rest_1_, f32[128]{0:T(128)S(1)} %get-tuple-element.65, ...), kind=kOutput, calls=%fused_computation.17 | convolution fusion | flops 68747264 | bytes 1324544 | tf_op jit(solution)/shard_map/dot_general | solution.py:253
  46.7 2.9 %collective-permute-done.13 = bf16[128,512]{1,0:T(8,128)(2,1)S(1)} collective-permute-done((bf16[128,512]{1,0:T(8,128)(2,1)S(1)}, bf16[128,512]{1,0:T(8,128)(2,1)S(1)}, u32[]{:S(2)}, u32[]{:S(2)}) %collective-permute-start.13) | collective-permute-done | bytes 131104 | tf_op jit(solution)/shard_map/ppermute | solution.py:18
  49.6 1.0 %fusion = f32[128,512]{1,0:T(8,128)} fusion(f32[128,512]{1,0:T(8,128)S(1)} %fusion.13, bf16[512,512]{1,0:T(8,128)(2,1)S(1)} %collective-permute-done.12, bf16[128,512]{1,0:T(8,128)(2,1)S(1)} %collective-permute-done.13, bf16[128,512]{1,0:T(8,128)(2,1)S(1)} %subtract_convert_fusion, s32[128]{0:T(128)S(1)} %iota_add_fusion.1, s32[512]{0:T(512)S(1)} %broadcast_add_fusion, ...), kind=kOutput, calls=%fused_computation.1 | convolution fusion | flops 67567616 | bytes 1313792 | tf_op jit(solution)/shard_map/dot_general | solution.py:269
  (31 shorter events, 4.1 us)
Async XLA Ops:
  0.0 5.3 %copy-start = (bf16[2048,512]{1,0:T(8,128)(2,1)S(1)}, bf16[2048,512]{1,0:T(8,128)(2,1)}, u32[]{:S(2)}) copy-start(bf16[2048,512]{1,0:T(8,128)(2,1)} %left.3) | copy-start | bytes 6291460
  2.4 15.4 %collective-permute-start = (bf16[2048,256]{1,0:T(8,128)(2,1)}, bf16[2048,256]{1,0:T(8,128)(2,1)}, u32[]{:S(2)}, u32[]{:S(2)}) collective-permute-start(bf16[2048,256]{1,0:T(8,128)(2,1)} %slice.78), channel_id=1, source_target_pairs={{4,0},{8,4},{12,8},{16,12},{20,16},{24,20},{28,24},{5,1},{9,5},{13... | collective-permute-start | bytes 3145736 | tf_op jit(solution)/shard_map/ppermute | solution.py:18
  8.4 13.5 %copy-start.1 = (s32[128]{0:T(128)S(1)}, s32[128]{0:T(128)}, u32[]{:S(2)}) copy-start(s32[128]{0:T(128)} %param.6) | copy-start | bytes 1540
  8.4 11.6 %collective-permute-start.1 = (s16[136,512]{1,0:T(8,128)(2,1)}, s16[136,512]{1,0:T(8,128)(2,1)S(1)}, u32[]{:S(2)}, u32[]{:S(2)}) collective-permute-start(s16[136,512]{1,0:T(8,128)(2,1)} %get-tuple-element.37), channel_id=1, source_target_pairs={{0,1},{1,2},{2,3},{3,0},{4,5},{5,6},{6,7},{7,4},{8,9},{9,10},{10,1... | collective-permute-start | bytes 417800 | tf_op jit(solution)/shard_map/ppermute | solution.py:30
  10.0 11.9 %collective-permute-start.2 = (s16[136,512]{1,0:T(8,128)(2,1)}, s16[136,512]{1,0:T(8,128)(2,1)}, u32[]{:S(2)}, u32[]{:S(2)}) collective-permute-start(s16[136,512]{1,0:T(8,128)(2,1)} %get-tuple-element.39), channel_id=1, source_target_pairs={{0,2},{1,3},{2,0},{3,1},{4,6},{5,7},{6,4},{7,5},{8,10},{9,11},{10,... | collective-permute-start | bytes 417800 | tf_op jit(solution)/shard_map/ppermute | solution.py:30
  12.6 9.3 %collective-permute-start.3 = (s16[136,512]{1,0:T(8,128)(2,1)}, s16[136,512]{1,0:T(8,128)(2,1)}, u32[]{:S(2)}, u32[]{:S(2)}) collective-permute-start(s16[136,512]{1,0:T(8,128)(2,1)} %get-tuple-element.41), channel_id=1, source_target_pairs={{0,3},{1,0},{2,1},{3,2},{4,7},{5,4},{6,5},{7,6},{8,11},{9,8},{10,9... | collective-permute-start | bytes 417800 | tf_op jit(solution)/shard_map/ppermute | solution.py:30
  13.9 18.2 %collective-permute-start.4 = (bf16[2048,256]{1,0:T(8,128)(2,1)}, bf16[2048,256]{1,0:T(8,128)(2,1)S(1)}, u32[]{:S(2)}, u32[]{:S(2)}) collective-permute-start(bf16[2048,256]{1,0:T(8,128)(2,1)} %get-tuple-element.48), channel_id=1, source_target_pairs={{4,0},{8,4},{12,8},{16,12},{20,16},{24,20},{28,24},{5,1},{9,5},{13... | collective-permute-start | bytes 3145736 | tf_op jit(solution)/shard_map/ppermute | solution.py:18
  21.9 16.2 %copy-start.3 = (bf16[512,512]{1,0:T(8,128)(2,1)S(1)}, bf16[512,512]{1,0:T(8,128)(2,1)}, u32[]{:S(2)}) copy-start(bf16[512,512]{1,0:T(8,128)(2,1)} %param.5) | copy-start | bytes 1572868
  22.8 9.2 %collective-permute-start.6 = (f32[8,512]{1,0:T(8,128)S(1)}, f32[8,512]{1,0:T(8,128)S(1)}, u32[]{:S(2)}, u32[]{:S(2)}) collective-permute-start(f32[8,512]{1,0:T(8,128)S(1)} %get-tuple-element.44), channel_id=1, source_target_pairs={{4,0},{8,4},{12,8},{16,12},{20,16},{24,20},{28,24},{5,1},{9,5},{13... | collective-permute-start | bytes 49160 | tf_op jit(solution)/shard_map/ppermute | solution.py:18
  26.0 7.0 %collective-permute-start.5 = (s16[128,256]{1,0:T(8,128)(2,1)S(1)}, s16[128,256]{1,0:T(8,128)(2,1)S(1)}, u32[]{:S(2)}, u32[]{:S(2)}) collective-permute-start(s16[128,256]{1,0:T(8,128)(2,1)S(1)} %get-tuple-element.50), channel_id=1, source_target_pairs={{0,1},{1,2},{2,3},{3,0},{4,5},{5,6},{6,7},{7,4},{8,9},{9,10},{10,1... | collective-permute-start | bytes 196616 | tf_op jit(solution)/shard_map/ppermute | solution.py:30
  29.3 8.7 %collective-permute-start.8 = (s16[128,256]{1,0:T(8,128)(2,1)S(1)}, s16[128,256]{1,0:T(8,128)(2,1)S(1)}, u32[]{:S(2)}, u32[]{:S(2)}) collective-permute-start(s16[128,256]{1,0:T(8,128)(2,1)S(1)} %get-tuple-element.55), channel_id=1, source_target_pairs={{0,2},{1,3},{2,0},{3,1},{4,6},{5,7},{6,4},{7,5},{8,10},{9,11},{10,... | collective-permute-start | bytes 196616 | tf_op jit(solution)/shard_map/ppermute | solution.py:30
  30.6 9.4 %collective-permute-start.10 = (s16[128,256]{1,0:T(8,128)(2,1)S(1)}, s16[128,256]{1,0:T(8,128)(2,1)S(1)}, u32[]{:S(2)}, u32[]{:S(2)}) collective-permute-start(s16[128,256]{1,0:T(8,128)(2,1)S(1)} %get-tuple-element.58), channel_id=1, source_target_pairs={{0,3},{1,0},{2,1},{3,2},{4,7},{5,4},{6,5},{7,6},{8,11},{9,8},{10,9... | collective-permute-start | bytes 196616 | tf_op jit(solution)/shard_map/ppermute | solution.py:30
  32.1 12.2 %copy-start.2 = (s32[128]{0:T(128)S(1)}, s32[128]{0:T(128)}, u32[]{:S(2)}) copy-start(s32[128]{0:T(128)} %param.7) | copy-start | bytes 1540
  34.2 6.1 %collective-permute-start.7 = (s16[128,256]{1,0:T(8,128)(2,1)S(1)}, s16[128,256]{1,0:T(8,128)(2,1)S(1)}, u32[]{:S(2)}, u32[]{:S(2)}) collective-permute-start(s16[128,256]{1,0:T(8,128)(2,1)S(1)} %get-tuple-element.53), channel_id=1, source_target_pairs={{0,1},{1,2},{2,3},{3,0},{4,5},{5,6},{6,7},{7,4},{8,9},{9,10},{10,1... | collective-permute-start | bytes 196616 | tf_op jit(solution)/shard_map/ppermute | solution.py:30
  35.6 6.1 %collective-permute-start.9 = (s16[128,256]{1,0:T(8,128)(2,1)S(1)}, s16[128,256]{1,0:T(8,128)(2,1)S(1)}, u32[]{:S(2)}, u32[]{:S(2)}) collective-permute-start(s16[128,256]{1,0:T(8,128)(2,1)S(1)} %get-tuple-element.56), channel_id=1, source_target_pairs={{0,2},{1,3},{2,0},{3,1},{4,6},{5,7},{6,4},{7,5},{8,10},{9,11},{10,... | collective-permute-start | bytes 196616 | tf_op jit(solution)/shard_map/ppermute | solution.py:30
  36.7 5.0 %collective-permute-start.11 = (s16[128,256]{1,0:T(8,128)(2,1)S(1)}, s16[128,256]{1,0:T(8,128)(2,1)S(1)}, u32[]{:S(2)}, u32[]{:S(2)}) collective-permute-start(s16[128,256]{1,0:T(8,128)(2,1)S(1)} %get-tuple-element.59), channel_id=1, source_target_pairs={{0,3},{1,0},{2,1},{3,2},{4,7},{5,4},{6,5},{7,6},{8,11},{9,8},{10,9... | collective-permute-start | bytes 196616 | tf_op jit(solution)/shard_map/ppermute | solution.py:30
  38.1 8.6 %collective-permute-start.12 = (bf16[512,512]{1,0:T(8,128)(2,1)S(1)}, bf16[512,512]{1,0:T(8,128)(2,1)S(1)}, u32[]{:S(2)}, u32[]{:S(2)}) collective-permute-start(bf16[512,512]{1,0:T(8,128)(2,1)S(1)} %copy-done.3), channel_id=1, source_target_pairs={{4,0},{8,4},{12,8},{16,12},{20,16},{24,20},{28,24},{5,1},{9,5},{13... | collective-permute-start | bytes 1572872 | tf_op jit(solution)/shard_map/ppermute | solution.py:18
  42.4 7.2 %collective-permute-start.13 = (bf16[128,512]{1,0:T(8,128)(2,1)S(1)}, bf16[128,512]{1,0:T(8,128)(2,1)S(1)}, u32[]{:S(2)}, u32[]{:S(2)}) collective-permute-start(bf16[128,512]{1,0:T(8,128)(2,1)S(1)} %convolution_convert_fusion), channel_id=1, source_target_pairs={{0,4},{4,8},{8,12},{12,16},{16,20},{20,24},{24,28},{1,5},{5,9},{9,... | collective-permute-start | bytes 393224 | tf_op jit(solution)/shard_map/ppermute | solution.py:18
